TPU v7x, 32 devices: a whole 2x2x4 slice. The times are simulated.
32 devices in a mesh: gx: 4 (over y, x), gy: 4 (over z), gz: 2 (over core).
Axes of the slice: x: 2, y: 2, z: 4, core: 2. Of those that a mesh axis runs over, the one named last changes fastest.
Arguments:
- dual_rhs: float32 [4, 4, 4, 3, 16, 256], P('gx', 'gy', 'gz'), may hold values from -15 to 15
- factors: bfloat16 [4, 4, 4, 6, 6, 256, 256], P('gx', 'gy', 'gz'), may hold values from -0.1875 to 0.1875
- block_pattern: int32 [4, 4, 4, 6, 6], P('gx', 'gy', 'gz'), may hold values from 0 to 1, as said below
- face_map: int32 [4, 4, 4, 3, 256], P('gx', 'gy', 'gz'), may hold values from 0 to 255, each once within a row
- rigid_modes: float32 [4, 4, 4, 6, 6, 256], P('gx', 'gy', 'gz'), may hold values from -0.21875 to 0.21875
- coarse_solve: float32 [384, 384], P(('gx', 'gy', 'gz')), may hold values from -1 to 2, as said below
Outputs:
- multipliers: float32 [4, 4, 4, 3, 16, 256], P('gx', 'gy', 'gz')
- residual: float32 [4, 4, 4, 3, 16, 256], P('gx', 'gy', 'gz')
Inputs may be any that keep to these rules, and one draw needn't show every extreme that they name: `block_pattern`: the diagonal blocks are always present. coarse_solve is symmetric.
All inputs are finite; a program needn't handle non-finite values.
Results may differ from a plain program's by a relative error of at most 0.0019.
Values sent between devices are 32-bit elements; how exact they have to be, the bound alone decides.
No kernel may reach another device: no remote copies, remote signals or barrier semaphores. Data moves between devices by JAX's collectives and lax.ppermute only.
A program may use at most 64 MiB of HBM per device.

v0:
```python
import jax
import jax.numpy as jnp
from jax import lax
from jax.sharding import PartitionSpec as P

ITERS = 4


highest_prec = lax.Precision.HIGHEST


def shifted(block, axis, distance):
    devices = range(lax.axis_size(axis))
    route = [(i - distance, i) for i in devices if i - distance in devices]
    return lax.ppermute(block, axis, route)


def forward_perm(values, perm_table):
    return jnp.einsum("xyzdcj,xyzdkj->xyzdck", values, perm_table, precision=highest_prec)


def inverse_perm(values, perm_table):
    return jnp.einsum("xyzdcj,xyzdjk->xyzdck", values, perm_table, precision=highest_prec)


def from_below(outgoing):
    face_x = outgoing[:, :, :, 0]
    recv_x = jnp.concatenate([shifted(face_x, "gx", 1), face_x[:-1]], axis=0)
    face_y = outgoing[:, :, :, 1]
    recv_y = jnp.concatenate([shifted(face_y, "gy", 1), face_y[:, :-1]], axis=1)
    face_z = outgoing[:, :, :, 2]
    recv_z = jnp.concatenate([shifted(face_z[:, :, -1:], "gz", 1), face_z[:, :, :-1]], axis=2)
    return jnp.stack([recv_x, recv_y, recv_z], axis=3)


def from_above(minus):
    face_x = minus[:, :, :, 0]
    recv_x = jnp.concatenate([face_x[1:], shifted(face_x, "gx", -1)], axis=0)
    face_y = minus[:, :, :, 1]
    recv_y = jnp.concatenate([face_y[:, 1:], shifted(face_y, "gy", -1)], axis=1)
    face_z = minus[:, :, :, 2]
    recv_z = jnp.concatenate([face_z[:, :, 1:], shifted(face_z[:, :, :1], "gz", -1)], axis=2)
    return jnp.stack([recv_x, recv_y, recv_z], axis=3)


def squares_total(residual):
    return lax.psum(jnp.sum(residual * residual), ("gx", "gy", "gz"))


def per_device(dual_rhs, factors, block_pattern, face_map, rigid_modes, coarse_solve):
    size_x, size_y, size_z = (dual_rhs.shape[0], dual_rhs.shape[1], dual_rhs.shape[2])
    cases = dual_rhs.shape[4]
    modes = rigid_modes.shape[4]
    face_dofs = face_map.shape[4]
    total_x = lax.axis_size("gx") * size_x
    total_y = lax.axis_size("gy") * size_y
    total_z = lax.axis_size("gz") * size_z
    perm_table = (face_map[:, :, :, :, :, None] == jnp.arange(face_dofs, dtype=jnp.int32)).astype(
        jnp.float32
    )
    ones_grid = jnp.ones((size_x, size_y, size_z), jnp.float32)
    global_x = lax.axis_index("gx") * size_x + jnp.arange(size_x)
    global_y = lax.axis_index("gy") * size_y + jnp.arange(size_y)
    global_z = lax.axis_index("gz") * size_z + jnp.arange(size_z)
    mask_x = (global_x < total_x - 1).astype(jnp.float32)[:, None, None] * ones_grid
    mask_y = (global_y < total_y - 1).astype(jnp.float32)[None, :, None] * ones_grid
    mask_z = (global_z < total_z - 1).astype(jnp.float32)[None, None, :] * ones_grid
    mask = jnp.stack([mask_x, mask_y, mask_z], axis=3)[:, :, :, :, None, None]
    masked_w = factors * block_pattern.astype(jnp.bfloat16)[:, :, :, :, :, None, None]
    flat_w = masked_w.reshape((-1,) + factors.shape[3:])

    def spread_dual(values):
        minus = from_below(forward_perm(values, perm_table))
        return jnp.concatenate([values, -minus], axis=3)

    def jump_dual(interface):
        above = from_above(interface[:, :, :, 3:])
        return (interface[:, :, :, :3] - inverse_perm(above, perm_table)) * mask

    def project(values, curve_part):
        interface = spread_dual(values)
        coarse_rhs = jnp.einsum(
            "xyzfmk,xyzfck->xyzmc", rigid_modes, interface, precision=highest_prec
        )
        coarse_rhs = coarse_rhs.reshape(-1, cases)
        gathered = lax.all_gather(coarse_rhs, ("gx", "gy", "gz"), axis=0, tiled=True)
        coarse_sol = jnp.dot(coarse_solve, gathered, precision=highest_prec)
        coarse_sol = coarse_sol.reshape(size_x, size_y, size_z, modes, cases)
        lifted = jnp.einsum("xyzfmk,xyzmc->xyzfck", rigid_modes, coarse_sol, precision=highest_prec)
        return (values - jump_dual(lifted), curve_part)

    multipliers = jnp.zeros_like(dual_rhs)
    residual, unused_total = project(dual_rhs, jnp.zeros((), jnp.float32))
    rho_now = squares_total(residual)
    rho_old = rho_now
    direction = residual
    for iteration in range(ITERS):
        if iteration == 0:
            direction = residual
        else:
            direction = residual + rho_now / rho_old * direction
        interface = spread_dual(direction).astype(jnp.bfloat16)
        flat_u = interface.reshape((-1,) + interface.shape[3:])
        forward = jnp.einsum("sijab,sjcb->sica", flat_w, flat_u, preferred_element_type=jnp.float32)
        curve_part = jnp.sum(forward * forward)
        curvature = lax.psum(curve_part, ("gx", "gy", "gz"))
        forward_half = forward.astype(jnp.bfloat16)
        backward = jnp.einsum(
            "sijab,sica->sjcb", flat_w, forward_half, preferred_element_type=jnp.float32
        ).reshape(interface.shape)
        image, merged_total = project(jump_dual(backward), curve_part)
        step_len = rho_now / curvature
        multipliers = multipliers + step_len * direction
        residual = residual - step_len * image
        if iteration + 1 < ITERS:
            rho_old = rho_now
            rho_now = squares_total(residual)
    return (multipliers, residual)


def solution(mesh):
    return jax.shard_map(
        per_device,
        mesh=mesh,
        in_specs=(
            P("gx", "gy", "gz", None, None, None),
            P("gx", "gy", "gz", None, None, None, None),
            P("gx", "gy", "gz", None, None),
            P("gx", "gy", "gz", None, None),
            P("gx", "gy", "gz", None, None, None),
            P(("gx", "gy", "gz"), None),
        ),
        out_specs=(P("gx", "gy", "gz", None, None, None), P("gx", "gy", "gz", None, None, None)),
        check_vma=False,
    )
```

profile of v0, /device:TPU:0, one launch (start us, length us, event | category | flops | bytes accessed | tf_op | source)
XLA Modules:
  0.0 754.2 jit_solution(13361237027798630441)
XLA Ops:
  1.4 1.7 fusion.50
  3.1 2.4 collective-permute-start.2
  5.5 4.2 collective-permute-start
  9.7 3.5 collective-permute-start.1
  16.1 41.5 %all-gather = f32[32,12,16]{2,1,0:T(8,128)S(1)} all-gather(f32[1,12,16]{2,1,0:T(8,128)S(1)} %reshape.636), channel_id=1, replica_groups=mesh['gx'=4,'gy'=4,'gz'=2] {'gx','gy','gz'}, dimensions={0}, use_global_device_ids=true | all-gather | bytes 25344 | tf_op jit(solution)/shard_map/all_gather | solution.py:86
  59.3 1.6 collective-permute-start.5
  63.7 3.4 collective-permute-done.3
  68.3 2.2 multiply_reduce_fusion.7
  71.6 2.0 collective-permute-start.8
  74.3 4.4 collective-permute-start.6
  81.8 6.9 multiply_reduce_fusion.3
  88.8 1.7 fusion.41
  94.4 3.5 collective-permute-done.9
  101.2 2.2 collective-permute-start.14
  103.3 4.9 collective-permute-start.12
  108.2 4.0 collective-permute-start.13
  112.3 1.5 collective-permute-done.13
  114.1 39.7 %all-gather.1 = f32[32,12,16]{2,1,0:T(8,128)S(1)} all-gather(f32[1,12,16]{2,1,0:T(8,128)S(1)} %reshape.638), channel_id=1, replica_groups=mesh['gx'=4,'gy'=4,'gz'=2] {'gx','gy','gz'}, dimensions={0}, use_global_device_ids=true | all-gather | bytes 25344 | tf_op jit(solution)/shard_map/all_gather | solution.py:86
  156.1 38.9 %all-reduce = (f32[]{:T(128)}, f32[]{:T(128)}) all-reduce(f32[]{:T(128)} %get-tuple-element.55, f32[]{:T(128)} %get-tuple-element.103), channel_id=1, replica_groups=mesh['gx'=4,'gy'=4,'gz'=2] {'gx','gy','gz'}, use_global_device_ids=true, to_apply=%region_1.0 | all-reduce | flops 2 | bytes 16 | tf_op jit(solution)/shard_map/psum | solution.py:47
  199.0 3.4 collective-permute-done.15
  202.4 1.9 collective-permute-done.16
  204.3 1.5 multiply_reduce_fusion.6
  205.8 43.0 %psum.58 = f32[]{:T(128)} all-reduce(f32[]{:T(128)} %get-tuple-element.105), channel_id=1, replica_groups=mesh['gx'=4,'gy'=4,'gz'=2] {'gx','gy','gz'}, use_global_device_ids=true, to_apply=%region_5.0 | all-reduce | flops 1 | bytes 8 | tf_op jit(solution)/shard_map/psum | solution.py:47
  252.6 4.2 collective-permute-start.18
  256.8 2.1 collective-permute-start.19
  260.3 6.9 multiply_reduce_fusion.2
  267.2 5.4 fusion.44
  276.5 3.4 collective-permute-done.21
  283.3 2.2 collective-permute-start.26
  285.4 4.6 collective-permute-start.24
  290.1 3.8 collective-permute-start.25
  293.9 1.5 collective-permute-done.25
  295.8 39.7 %all-gather.2 = f32[32,12,16]{2,1,0:T(8,128)S(1)} all-gather(f32[1,12,16]{2,1,0:T(8,128)S(1)} %reshape.640), channel_id=1, replica_groups=mesh['gx'=4,'gy'=4,'gz'=2] {'gx','gy','gz'}, dimensions={0}, use_global_device_ids=true | all-gather | bytes 25344 | tf_op jit(solution)/shard_map/all_gather | solution.py:86
  337.8 39.2 %psum.59 = f32[]{:T(128)} all-reduce(f32[]{:T(128)} %get-tuple-element.107), channel_id=1, replica_groups=mesh['gx'=4,'gy'=4,'gz'=2] {'gx','gy','gz'}, use_global_device_ids=true, to_apply=%region_7.0 | all-reduce | flops 1 | bytes 8 | tf_op jit(solution)/shard_map/psum | solution.py:106
  381.0 3.4 collective-permute-done.27
  384.4 1.9 collective-permute-done.28
  386.3 1.5 multiply_reduce_fusion.5
  387.8 43.0 %psum.60 = f32[]{:T(128)} all-reduce(f32[]{:T(128)} %get-tuple-element.109), channel_id=1, replica_groups=mesh['gx'=4,'gy'=4,'gz'=2] {'gx','gy','gz'}, use_global_device_ids=true, to_apply=%region_9.0 | all-reduce | flops 1 | bytes 8 | tf_op jit(solution)/shard_map/psum | solution.py:47
  434.6 4.2 collective-permute-start.30
  438.8 2.1 collective-permute-start.31
  442.3 6.9 multiply_reduce_fusion.1
  449.2 5.4 fusion.47
  458.5 3.4 collective-permute-done.33
  465.3 2.2 collective-permute-start.38
  467.4 4.6 collective-permute-start.36
  472.1 3.8 collective-permute-start.37
  475.9 1.5 collective-permute-done.37
  477.8 39.7 %all-gather.3 = f32[32,12,16]{2,1,0:T(8,128)S(1)} all-gather(f32[1,12,16]{2,1,0:T(8,128)S(1)} %reshape.642), channel_id=1, replica_groups=mesh['gx'=4,'gy'=4,'gz'=2] {'gx','gy','gz'}, dimensions={0}, use_global_device_ids=true | all-gather | bytes 25344 | tf_op jit(solution)/shard_map/all_gather | solution.py:86
  519.8 39.2 %psum.61 = f32[]{:T(128)} all-reduce(f32[]{:T(128)} %get-tuple-element.111), channel_id=1, replica_groups=mesh['gx'=4,'gy'=4,'gz'=2] {'gx','gy','gz'}, use_global_device_ids=true, to_apply=%region_11.0 | all-reduce | flops 1 | bytes 8 | tf_op jit(solution)/shard_map/psum | solution.py:106
  563.0 3.4 collective-permute-done.39
  566.4 1.9 collective-permute-done.40
  569.8 43.0 %psum.62 = f32[]{:T(128)} all-reduce(f32[]{:T(128)} %get-tuple-element.113), channel_id=1, replica_groups=mesh['gx'=4,'gy'=4,'gz'=2] {'gx','gy','gz'}, use_global_device_ids=true, to_apply=%region_13.0 | all-reduce | flops 1 | bytes 8 | tf_op jit(solution)/shard_map/psum | solution.py:47
  616.6 4.2 collective-permute-start.42
  620.7 2.2 collective-permute-start.43
  624.3 6.9 multiply_reduce_fusion
  631.2 5.4 fusion.29
  640.5 3.4 collective-permute-done.45
  647.3 2.2 collective-permute-start.50
  649.4 42.0 %psum.63 = f32[]{:T(128)} all-reduce(f32[]{:T(128)} %get-tuple-element.115), channel_id=1, replica_groups=mesh['gx'=4,'gy'=4,'gz'=2] {'gx','gy','gz'}, use_global_device_ids=true, to_apply=%region_15.0 | all-reduce | flops 1 | bytes 8 | tf_op jit(solution)/shard_map/psum | solution.py:106
  692.8 4.2 collective-permute-start.48
  697.0 2.0 collective-permute-start.49
  699.1 1.5 collective-permute-done.49
  700.9 41.2 %all-gather.4 = f32[32,12,16]{2,1,0:T(8,128)S(1)} all-gather(f32[1,12,16]{2,1,0:T(8,128)S(1)} %reshape.644), channel_id=1, replica_groups=mesh['gx'=4,'gy'=4,'gz'=2] {'gx','gy','gz'}, dimensions={0}, use_global_device_ids=true | all-gather | bytes 25344 | tf_op jit(solution)/shard_map/all_gather | solution.py:86
  747.8 3.4 collective-permute-done.51
  (196 shorter events, 79.9 us)
Async XLA Ops:
  0.6 14.2 %copy-start = (f32[1,1,2,6,6,256]{5,2,4,3,1,0:T(2,128)S(1)}, f32[1,1,2,6,6,256]{5,2,4,3,1,0:T(2,128)}, u32[]{:S(2)}) copy-start(f32[1,1,2,6,6,256]{5,2,4,3,1,0:T(2,128)} %param.10) | copy-start | bytes 221188
  3.1 10.2 %collective-permute-start.2 = (f32[1,1,1,16,256]{4,3,2,1,0:T(8,128)S(1)}, f32[1,1,1,16,256]{4,3,2,1,0:T(8,128)S(1)}, u32[]{:S(2)}, u32[]{:S(2)}) collective-permute-start(f32[1,1,1,16,256]{4,3,2,1,0:T(8,128)S(1)} %get-tuple-element.100), channel_id=1, source_target_pairs={{0,1},{2,3},{4,5},{6,7},{8,9},{10,11},{12,13},{14,15},{16,17},{18,... | collective-permute-start | bytes 49160 | tf_op jit(solution)/shard_map/ppermute | solution.py:15
  5.5 7.8 %collective-permute-start = (f32[1,1,2,16,256]{4,3,2,1,0:T(8,128)S(1)}, f32[1,1,2,16,256]{4,3,2,1,0:T(8,128)S(1)}, u32[]{:S(2)}, u32[]{:S(2)}) collective-permute-start(f32[1,1,2,16,256]{4,3,2,1,0:T(8,128)S(1)} %get-tuple-element.63), channel_id=1, source_target_pairs={{0,8},{8,16},{16,24},{1,9},{9,17},{17,25},{2,10},{10,18},{18,26},{... | collective-permute-start | bytes 98312 | tf_op jit(solution)/shard_map/ppermute | solution.py:15
  9.7 5.1 collective-permute-start.1
  58.8 29.9 %copy-start.2 = (bf16[1,1,2,6,6,256,256]{6,5,4,3,2,1,0:T(8,128)(2,1)S(1)}, bf16[1,1,2,6,6,256,256]{6,5,4,3,2,1,0:T(8,128)(2,1)}, u32[]{:S(2)}) copy-start(bf16[1,1,2,6,6,256,256]{6,5,4,3,2,1,0:T(8,128)(2,1)} %param.7) | copy-start | bytes 28311556
  59.3 4.4 collective-permute-start.5
  60.9 6.1 collective-permute-start.3
  62.3 6.0 collective-permute-start.4
  71.6 8.6 %collective-permute-start.8 = (f32[1,1,1,16,256]{4,3,2,1,0:T(8,128)S(1)}, f32[1,1,1,16,256]{4,3,2,1,0:T(8,128)S(1)}, u32[]{:S(2)}, u32[]{:S(2)}) collective-permute-start(f32[1,1,1,16,256]{4,3,2,1,0:T(8,128)S(1)} %get-tuple-element.96), channel_id=1, source_target_pairs={{0,1},{2,3},{4,5},{6,7},{8,9},{10,11},{12,13},{14,15},{16,17},{18,... | collective-permute-start | bytes 49160 | tf_op jit(solution)/shard_map/ppermute | solution.py:15
  74.3 6.0 collective-permute-start.6
  78.8 3.0 collective-permute-start.7
  81.8 72.0 %copy-start.1 = (f32[12,384]{1,0:T(8,128)S(1)}, f32[12,384]{1,0:T(8,128)}, u32[]{:S(2)}) copy-start(f32[12,384]{1,0:T(8,128)} %param.11) | copy-start | bytes 55300
  90.5 3.9 collective-permute-start.11
  91.8 6.2 collective-permute-start.9
  93.1 6.1 collective-permute-start.10
  101.2 11.1 %collective-permute-start.14 = (f32[1,1,1,16,256]{4,3,2,1,0:T(8,128)S(1)}, f32[1,1,1,16,256]{4,3,2,1,0:T(8,128)S(1)}, u32[]{:S(2)}, u32[]{:S(2)}) collective-permute-start(f32[1,1,1,16,256]{4,3,2,1,0:T(8,128)S(1)} %get-tuple-element.92), channel_id=1, source_target_pairs={{0,1},{2,3},{4,5},{6,7},{8,9},{10,11},{12,13},{14,15},{16,17},{18,... | collective-permute-start | bytes 49160 | tf_op jit(solution)/shard_map/ppermute | solution.py:15
  103.3 8.9 %collective-permute-start.12 = (f32[1,1,2,16,256]{4,3,2,1,0:T(8,128)S(1)}, f32[1,1,2,16,256]{4,3,2,1,0:T(8,128)S(1)}, u32[]{:S(2)}, u32[]{:S(2)}) collective-permute-start(f32[1,1,2,16,256]{4,3,2,1,0:T(8,128)S(1)} %get-tuple-element.57), channel_id=1, source_target_pairs={{0,8},{8,16},{16,24},{1,9},{9,17},{17,25},{2,10},{10,18},{18,26},{... | collective-permute-start | bytes 98312 | tf_op jit(solution)/shard_map/ppermute | solution.py:15
  108.2 5.6 collective-permute-start.13
  154.8 44.2 %collective-permute-start.17 = (f32[1,1,1,16,256]{4,3,2,1,0:T(8,128)S(1)}, f32[1,1,1,16,256]{4,3,2,1,0:T(8,128)S(1)}, u32[]{:S(2)}, u32[]{:S(2)}) collective-permute-start(f32[1,1,1,16,256]{4,3,2,1,0:T(8,128)S(1)} %get-tuple-element.91), channel_id=1, source_target_pairs={{1,0},{3,2},{5,4},{7,6},{9,8},{11,10},{13,12},{15,14},{17,16},{19,... | collective-permute-start | bytes 49160 | tf_op jit(solution)/shard_map/ppermute | solution.py:15
  196.4 6.1 collective-permute-start.15
  197.7 6.7 collective-permute-start.16
  251.3 7.6 %collective-permute-start.20 = (f32[1,1,1,16,256]{4,3,2,1,0:T(8,128)S(1)}, f32[1,1,1,16,256]{4,3,2,1,0:T(8,128)S(1)}, u32[]{:S(2)}, u32[]{:S(2)}) collective-permute-start(f32[1,1,1,16,256]{4,3,2,1,0:T(8,128)S(1)} %get-tuple-element.88), channel_id=1, source_target_pairs={{0,1},{2,3},{4,5},{6,7},{8,9},{10,11},{12,13},{14,15},{16,17},{18,... | collective-permute-start | bytes 49160 | tf_op jit(solution)/shard_map/ppermute | solution.py:15
  252.6 6.3 collective-permute-start.18
  256.8 3.5 collective-permute-start.19
  272.6 3.9 collective-permute-start.23
  273.9 6.0 collective-permute-start.21
  275.2 6.1 collective-permute-start.22
  283.3 10.6 %collective-permute-start.26 = (f32[1,1,1,16,256]{4,3,2,1,0:T(8,128)S(1)}, f32[1,1,1,16,256]{4,3,2,1,0:T(8,128)S(1)}, u32[]{:S(2)}, u32[]{:S(2)}) collective-permute-start(f32[1,1,1,16,256]{4,3,2,1,0:T(8,128)S(1)} %get-tuple-element.84), channel_id=1, source_target_pairs={{0,1},{2,3},{4,5},{6,7},{8,9},{10,11},{12,13},{14,15},{16,17},{18,... | collective-permute-start | bytes 49160 | tf_op jit(solution)/shard_map/ppermute | solution.py:15
  285.4 8.5 %collective-permute-start.24 = (f32[1,1,2,16,256]{4,3,2,1,0:T(8,128)S(1)}, f32[1,1,2,16,256]{4,3,2,1,0:T(8,128)S(1)}, u32[]{:S(2)}, u32[]{:S(2)}) collective-permute-start(f32[1,1,2,16,256]{4,3,2,1,0:T(8,128)S(1)} %get-tuple-element.49), channel_id=1, source_target_pairs={{0,8},{8,16},{16,24},{1,9},{9,17},{17,25},{2,10},{10,18},{18,26},{... | collective-permute-start | bytes 98312 | tf_op jit(solution)/shard_map/ppermute | solution.py:15
  290.1 5.4 collective-permute-start.25
  336.5 44.5 %collective-permute-start.29 = (f32[1,1,1,16,256]{4,3,2,1,0:T(8,128)S(1)}, f32[1,1,1,16,256]{4,3,2,1,0:T(8,128)S(1)}, u32[]{:S(2)}, u32[]{:S(2)}) collective-permute-start(f32[1,1,1,16,256]{4,3,2,1,0:T(8,128)S(1)} %get-tuple-element.83), channel_id=1, source_target_pairs={{1,0},{3,2},{5,4},{7,6},{9,8},{11,10},{13,12},{15,14},{17,16},{19,... | collective-permute-start | bytes 49160 | tf_op jit(solution)/shard_map/ppermute | solution.py:15
  378.3 6.1 collective-permute-start.27
  379.6 6.7 collective-permute-start.28
  433.3 7.6 %collective-permute-start.32 = (f32[1,1,1,16,256]{4,3,2,1,0:T(8,128)S(1)}, f32[1,1,1,16,256]{4,3,2,1,0:T(8,128)S(1)}, u32[]{:S(2)}, u32[]{:S(2)}) collective-permute-start(f32[1,1,1,16,256]{4,3,2,1,0:T(8,128)S(1)} %get-tuple-element.80), channel_id=1, source_target_pairs={{0,1},{2,3},{4,5},{6,7},{8,9},{10,11},{12,13},{14,15},{16,17},{18,... | collective-permute-start | bytes 49160 | tf_op jit(solution)/shard_map/ppermute | solution.py:15
  434.6 6.4 collective-permute-start.30
  438.8 3.5 collective-permute-start.31
  454.6 3.9 collective-permute-start.35
  455.9 6.0 collective-permute-start.33
  457.2 6.1 collective-permute-start.34
  465.3 10.6 %collective-permute-start.38 = (f32[1,1,1,16,256]{4,3,2,1,0:T(8,128)S(1)}, f32[1,1,1,16,256]{4,3,2,1,0:T(8,128)S(1)}, u32[]{:S(2)}, u32[]{:S(2)}) collective-permute-start(f32[1,1,1,16,256]{4,3,2,1,0:T(8,128)S(1)} %get-tuple-element.76), channel_id=1, source_target_pairs={{0,1},{2,3},{4,5},{6,7},{8,9},{10,11},{12,13},{14,15},{16,17},{18,... | collective-permute-start | bytes 49160 | tf_op jit(solution)/shard_map/ppermute | solution.py:15
  467.4 8.5 %collective-permute-start.36 = (f32[1,1,2,16,256]{4,3,2,1,0:T(8,128)S(1)}, f32[1,1,2,16,256]{4,3,2,1,0:T(8,128)S(1)}, u32[]{:S(2)}, u32[]{:S(2)}) collective-permute-start(f32[1,1,2,16,256]{4,3,2,1,0:T(8,128)S(1)} %get-tuple-element.43), channel_id=1, source_target_pairs={{0,8},{8,16},{16,24},{1,9},{9,17},{17,25},{2,10},{10,18},{18,26},{... | collective-permute-start | bytes 98312 | tf_op jit(solution)/shard_map/ppermute | solution.py:15
  472.1 5.4 collective-permute-start.37
  518.5 44.5 %collective-permute-start.41 = (f32[1,1,1,16,256]{4,3,2,1,0:T(8,128)S(1)}, f32[1,1,1,16,256]{4,3,2,1,0:T(8,128)S(1)}, u32[]{:S(2)}, u32[]{:S(2)}) collective-permute-start(f32[1,1,1,16,256]{4,3,2,1,0:T(8,128)S(1)} %get-tuple-element.75), channel_id=1, source_target_pairs={{1,0},{3,2},{5,4},{7,6},{9,8},{11,10},{13,12},{15,14},{17,16},{19,... | collective-permute-start | bytes 49160 | tf_op jit(solution)/shard_map/ppermute | solution.py:15
  560.3 6.1 collective-permute-start.39
  561.6 6.7 collective-permute-start.40
  615.3 7.7 %collective-permute-start.44 = (f32[1,1,1,16,256]{4,3,2,1,0:T(8,128)S(1)}, f32[1,1,1,16,256]{4,3,2,1,0:T(8,128)S(1)}, u32[]{:S(2)}, u32[]{:S(2)}) collective-permute-start(f32[1,1,1,16,256]{4,3,2,1,0:T(8,128)S(1)} %get-tuple-element.72), channel_id=1, source_target_pairs={{0,1},{2,3},{4,5},{6,7},{8,9},{10,11},{12,13},{14,15},{16,17},{18,... | collective-permute-start | bytes 49160 | tf_op jit(solution)/shard_map/ppermute | solution.py:15
  616.6 6.4 collective-permute-start.42
  620.7 3.5 collective-permute-start.43
  636.6 3.9 collective-permute-start.47
  637.9 6.0 collective-permute-start.45
  639.2 6.1 collective-permute-start.46
  647.3 51.8 %collective-permute-start.50 = (f32[1,1,1,16,256]{4,3,2,1,0:T(8,128)S(1)}, f32[1,1,1,16,256]{4,3,2,1,0:T(8,128)S(1)}, u32[]{:S(2)}, u32[]{:S(2)}) collective-permute-start(f32[1,1,1,16,256]{4,3,2,1,0:T(8,128)S(1)} %get-tuple-element.68), channel_id=1, source_target_pairs={{0,1},{2,3},{4,5},{6,7},{8,9},{10,11},{12,13},{14,15},{16,17},{18,... | collective-permute-start | bytes 49160 | tf_op jit(solution)/shard_map/ppermute | solution.py:15
  692.8 6.2 collective-permute-start.48
  697.0 3.6 collective-permute-start.49
  743.2 4.6 collective-permute-start.53
  745.1 6.0 collective-permute-start.51
  746.4 6.0 collective-permute-start.52
where the time goes:
time: 766 us; the launch traced here: 754 us
  blocking collectives  490 us (64%)
  starting transfers between devices  117 us (15%)
  matrix products  74.7 us (10%)
  waiting for transfers between devices  57.8 us (8%)
  between operations  11.7 us (2%)
    all_gather x5, blocking collectives, project(): lax.all_gather(coarse_rhs, ('gx', 'gy', 'gz'), axis=0, tiled=True)  202 us
    psum x4, blocking collectives, squares_total(): return lax.psum(jnp.sum(residual * residual), ('gx', 'gy', 'gz'))  168 us
    psum x3, blocking collectives, per_device(): curvature = lax.psum(curve_part, ('gx', 'gy', 'gz'))  120 us
    ppermute x54, starting transfers between devices, shifted(): return lax.ppermute(block, axis, route)  117 us
    ppermute x54, waiting for transfers between devices, shifted(): return lax.ppermute(block, axis, route)  57.8 us
    dot_general x4, matrix products, per_device(): jnp.einsum('sijab,sjcb->sica', flat_w, flat_u, preferred_element_type=jnp...  27.7 us
    dot_general x4, matrix products, per_device(): jnp.einsum('sijab,sica->sjcb', flat_w, forward_half, preferred_element_ty...  17.9 us
  transfers between devices with their start and end apart: 54, of which 28 were waited for; matrix products, arithmetic and copies ran while one was open for 0% of the time, Pallas kernels for 0%

commit v1 on v0

v1 whole, which is shorter than its diff:
```python
import functools

import jax
import jax.numpy as jnp
import numpy as np
from jax import lax
from jax.experimental import pallas as pl
from jax.experimental.pallas import tpu as pltpu
from jax.sharding import PartitionSpec as P

ITERS = 4
AXES = ("gx", "gy", "gz")
LANES = 128
SLOT = 8
SLOTS = 12
RHO, FF, FD = SLOTS * SLOT, SLOTS * SLOT + 1, SLOTS * SLOT + 2
NT = (((1,), (1,)), ((), ()))
NN = (((1,), (0,)), ((), ()))
f32 = jnp.float32
bf16 = jnp.bfloat16


def own_slot(s):
    return s


def nbr_slot(s, f):
    if f == 0:
        return 4 + s
    if f == 3:
        return 2 + s
    if f == 1:
        return 8 + s
    if f == 4:
        return 6 + s
    if f == 2:
        return 1 if s == 0 else 11
    return 10 if s == 0 else 0


def slot_table(nx, ny, nz, nc):
    table = np.full((nx * ny * nz, LANES), -1, np.int32)
    sz = 2 * nz
    for x in range(nx):
        for y in range(ny):
            for z in range(nz):
                where = [(x, y, 2 * z), (x, y, 2 * z + 1)]
                where += [(x - 1, y, 2 * z), (x - 1, y, 2 * z + 1), (x + 1, y, 2 * z), (x + 1, y, 2 * z + 1)]
                where += [(x, y - 1, 2 * z), (x, y - 1, 2 * z + 1), (x, y + 1, 2 * z), (x, y + 1, 2 * z + 1)]
                where += [(x, y, 2 * z - 1), (x, y, 2 * z + 2)]
                for slot, (a, b, c) in enumerate(where):
                    if 0 <= a < nx and 0 <= b < ny and 0 <= c < sz:
                        first = ((a * ny + b) * sz + c) * 6
                        table[(x * ny + y) * nz + z, slot * SLOT : slot * SLOT + 6] = first + np.arange(6)
    return table


def split2(x):
    high = x.astype(bf16)
    low = (x - high.astype(f32)).astype(bf16)
    return jnp.concatenate([high, low], 0)


def split3(x):
    high = x.astype(bf16)
    rest = x - high.astype(f32)
    mid = rest.astype(bf16)
    low = (rest - mid.astype(f32)).astype(bf16)
    return jnp.concatenate([high, mid, low], 0)


def fold2(x):
    n = x.shape[0] // 2
    return x[:n] + x[n:]


def fold3(x):
    n = x.shape[0] // 3
    return x[:n] + (x[n : 2 * n] + x[2 * n :])


def mm(a, b, dims):
    return lax.dot_general(a, b, dims, preferred_element_type=f32)


def position(sizes):
    index = [lax.axis_index(a) for a in AXES]
    parity = [lax.rem(i, 2) == 1 for i in index]
    masks = []
    for s in range(2):
        row = []
        for f in range(6):
            d = f % 3
            if d == 2 and (s == 0) == (f == 2):
                row.append(None)
            else:
                inside = (index[d] < sizes[d] - 1) if f < 3 else (index[d] > 0)
                row.append(inside.astype(f32))
        masks.append(row)
    return parity, masks


def masked(value, mask):
    return value if mask is None else value * mask


def pick(cond, a, b):
    return jnp.where(cond, a, b)


def pack_kernel(rhs, modes, fmap, coarse, xa, xb, ya, yb, za, zb):
    parity, _ = position((1, 1, 1))
    slabs = -(-coarse.shape[1] // 256)
    for d, outs in ((0, (xa, xb)), (1, (ya, yb))):
        for s in range(2):
            up, down = modes[s, d], modes[s, d + 3]
            first = pick(parity[d], down, up)
            second = pick(parity[d], up, down)
            for out, piece in zip(outs, (first, second)):
                out[24 * s : 24 * s + 16, :] = rhs[s, d]
                out[24 * s + 16 : 24 * s + 24, :] = jnp.concatenate(
                    [piece, fmap[s, d : d + 1, :].astype(f32), jnp.zeros((1, 256), f32)], 0
                )
    up, down = modes[1, 2], modes[0, 5]
    for out, piece in zip((za, zb), (pick(parity[2], down, up), pick(parity[2], up, down))):
        out[0:16, :] = rhs[1, 2]
        out[16:24, :] = jnp.concatenate([piece, fmap[1, 2:3, :].astype(f32), jnp.zeros((1, 256), f32)], 0)
    for k in range(slabs):
        width = min(256, coarse.shape[1] - 256 * k)
        slab = coarse[:, 256 * k : 256 * k + width]
        if width < 256:
            slab = jnp.concatenate([slab, jnp.zeros((12, 256 - width), f32)], 1)
        gap = jnp.zeros((2, 256), f32)
        slab = jnp.concatenate([slab[:6], gap, slab[6:], gap], 0)
        for out, base in ((xa, 48), (xb, 48), (ya, 48), (yb, 48), (za, 24), (zb, 24)):
            out[base + 16 * k : base + 16 * k + 16, :] = slab


def setup_kernel(rhs, modes, fmap, coarse, table, xa, xb, ya, yb, za, zb, perm, lift, start, solve, send, work, rows):
    parity, _ = position((1, 1, 1))
    slabs = -(-coarse.shape[1] // 256)
    devices = table.shape[0]
    lane_row = lax.broadcasted_iota(jnp.int32, (256, 256), 0)

    plus, minus = [], []
    for d, (a, b) in enumerate(((xa, xb), (ya, yb), (za, zb))):
        va, vb = a[...], b[...]
        plus.append(pick(parity[d], vb, va))
        minus.append(pick(parity[d], va, vb))

    def onehot(row):
        return (lane_row == row.astype(jnp.int32)).astype(bf16)

    def to_upper_order(values, table_rows):
        return -fold3(mm(split3(values), table_rows, NT))

    zero2 = jnp.zeros((2, 256), f32)
    partial = [jnp.zeros((48, 256), f32) for _ in range(2)]
    up_perm = {}
    for s in range(2):
        for d in range(3):
            up_perm[s, d] = onehot(fmap[s, d : d + 1, :])
    tilde_low = {}
    for s in range(2):
        for d in range(3):
            if d == 2 and s == 1:
                table_rows = up_perm[0, 2]
            else:
                base = 24 * s if d < 2 else 0
                table_rows = onehot(minus[d][base + 22 : base + 23, :])
            perm[s * 3 + d] = table_rows
            tilde_low[s, d] = to_upper_order(modes[s, d + 3], table_rows)
    for s in range(2):
        for f in range(6):
            d = f % 3
            if f < 3:
                own = modes[s, f]
                value = rhs[s, f]
                if d == 2 and s == 0:
                    other = tilde_low[1, 2]
                else:
                    base = 24 * s if d < 2 else 0
                    other = to_upper_order(plus[d][base + 16 : base + 22, :], up_perm[s, d])
            else:
                own = tilde_low[s, d]
                if d == 2 and s == 1:
                    other = modes[0, 2]
                    value = rhs[0, 2]
                else:
                    base = 24 * s if d < 2 else 0
                    other = minus[d][base + 16 : base + 22, :]
                    inside = lax.axis_index(AXES[d]) > 0
                    value = minus[d][base : base + 16, :] * inside.astype(f32)
            start[s, f] = value
            work[...] = jnp.zeros(work.shape, f32)
            work[own_slot(s) * SLOT : own_slot(s) * SLOT + 8, :] = jnp.concatenate([own, zero2], 0)
            n = nbr_slot(s, f)
            work[n * SLOT : n * SLOT + 8, :] = jnp.concatenate([other, zero2], 0)
            both = split2(work[...])
            lift[s * 6 + f] = both
            partial[s] += mm(split3(value), both, NT)

    rows[...] = jnp.zeros(rows.shape, f32)
    pieces = [(2, minus[0], 48, 16), (4, plus[0], 48, 16), (6, minus[1], 48, 16), (8, plus[1], 48, 16)]
    pieces += [(10, minus[2], 24 + 8, 8), (11, plus[2], 24, 8)]
    for k in range(slabs):
        width = min(256, coarse.shape[1] - 256 * k)
        slab = coarse[:, 256 * k : 256 * k + width]
        if width < 256:
            slab = jnp.concatenate([slab, jnp.zeros((12, 256 - width), f32)], 1)
        slab = jnp.concatenate([slab[:6], zero2, slab[6:], zero2], 0)
        rows[0:16, 256 * k : 256 * k + 256] = slab
        for slot, source, base, count in pieces:
            rows[slot * SLOT : slot * SLOT + count, 256 * k : 256 * k + 256] = source[
                base + 16 * k : base + 16 * k + count, :
            ]
    both = split2(rows[...])
    index_row = lax.broadcasted_iota(jnp.int32, (256 * slabs, LANES), 0)
    line = lax.broadcasted_iota(jnp.int32, (LANES, LANES), 0)
    column = lax.broadcasted_iota(jnp.int32, (LANES, LANES), 1)
    passing = ((line == column) & (line >= RHO) & (line <= FD)).astype(f32)
    total = [fold3(part) for part in partial]
    total = [part[:, :LANES] + part[:, LANES:] for part in total]
    lane = lax.broadcasted_iota(jnp.int32, total[0].shape, 1)
    total = jnp.where(lane < SLOT, total[0], jnp.where(lane < 2 * SLOT, total[1], 0.0))

    def build(q2, carry):
        halves = []
        for q in range(2):
            choose = (index_row == table[2 * q2 + q]).astype(bf16)
            got = mm(both, choose, NN)
            halves.append(jnp.concatenate([got[:LANES] + passing, got[LANES:]], 0))
        solve[q2] = jnp.concatenate(halves, 1).astype(bf16)
        return carry

    lax.fori_loop(0, devices // 2, build, 0)
    spread_out(total, solve, send)


def spread_out(part, solve, send):
    left = split3(part)
    left = jnp.concatenate([left, left], 1)
    pairs = solve.shape[0]

    def one(q2):
        got = fold3(mm(left, solve[q2], NN))
        send[2 * q2] = got[:, :LANES]
        send[2 * q2 + 1] = got[:, LANES:]

    if pairs <= 16:
        for q2 in range(pairs):
            one(q2)
    else:

        def step(q2, carry):
            one(q2)
            return carry

        lax.fori_loop(0, pairs, step, 0)


def gather_sum(recv):
    devices = recv.shape[0]
    if devices <= 32:
        parts = [recv[q] for q in range(devices)]
        while len(parts) > 1:
            parts = [parts[i] + parts[i + 1] for i in range(0, len(parts), 2)]
        return parts[0]
    return lax.fori_loop(0, devices, lambda q, acc: acc + recv[q], jnp.zeros(recv.shape[1:], f32))


def lift_left(total):
    left = split3(total)
    return jnp.concatenate([left, left], 1)


def apply_factors(residual, pattern, factors, perm, lift, masks, parity, previous, forward, image, solve, sends):
    xa, xb, ya, yb, za, zb, send = sends
    partial = jnp.zeros((48, 256), f32)
    own_sum = jnp.zeros((16, 256), f32)
    square = jnp.zeros((16, 256), f32)
    cross = jnp.zeros((16, 256), f32)
    faces = {}
    for s in range(2):
        sides = []
        for j in range(6):
            value = residual[s][j]
            if j < 3:
                own_sum += value * value
                sides.append(split2(value))
            else:
                sides.append((-mm(split2(value), perm[s * 3 + j - 3], NN)).astype(bf16))
        present = [[pattern[s, i, j].astype(f32).astype(bf16) for j in range(6)] for i in range(6)]
        halves = []
        for i in range(6):
            acc = jnp.zeros((32, 256), f32)
            for j in range(6):
                acc += mm(sides[j] * present[i][j], factors[s, i, j], NT)
            got = fold2(acc)
            forward[s, i] = got
            square += got * got
            if previous is not None:
                cross += got * previous[s][i]
            halves.append(split2(got))
        for j in range(6):
            acc = jnp.zeros((32, 256), f32)
            for i in range(6):
                acc += mm(halves[i] * present[i][j], factors[s, i, j], NN)
            got = fold2(acc)
            if j >= 3:
                got = -fold3(mm(split3(got), perm[s * 3 + j - 3], NT))
            got = masked(got, masks[s][j])
            image[s, j] = got
            faces[s, j] = got
            partial += mm(split3(got), lift[s * 6 + j], NT)
    for s in range(2):
        xa[s] = pick(parity[0], faces[s, 3], faces[s, 0])
        xb[s] = pick(parity[0], faces[s, 0], faces[s, 3])
        ya[s] = pick(parity[1], faces[s, 4], faces[s, 1])
        yb[s] = pick(parity[1], faces[s, 1], faces[s, 4])
    za[...] = pick(parity[2], faces[0, 5], faces[1, 2])
    zb[...] = pick(parity[2], faces[1, 2], faces[0, 5])
    total = fold3(partial)
    total = total[:, :LANES] + total[:, LANES:]
    lane = lax.broadcasted_iota(jnp.int32, total.shape, 1)
    for where, values in ((RHO, own_sum), (FF, square), (FD, cross)):
        total = jnp.where(lane == where, jnp.sum(values, axis=1, keepdims=True), total)
    spread_out(total, solve, send)


def first_kernel(sizes, pattern, recv, start, factors, perm, lift, solve, residual, forward, image, *sends):
    parity, masks = position(sizes)
    left = lift_left(gather_sum(recv))
    now = [[None] * 6 for _ in range(2)]
    for s in range(2):
        for f in range(6):
            value = start[s, f] - masked(fold3(mm(left, lift[s * 6 + f], NN)), masks[s][f])
            residual[s, f] = value
            now[s][f] = value
    apply_factors(now, pattern, factors, perm, lift, masks, parity, None, forward, image, solve, sends)


def update(sizes, first, recvs, state, count):
    parity, masks = position(sizes)
    xa, xb, ya, yb, za, zb, recv = recvs
    residual, forward, image, lift, old = state
    total = gather_sum(recv)
    left = lift_left(total)
    sums = jnp.sum(total, axis=0, keepdims=True)
    lane = lax.broadcasted_iota(jnp.int32, sums.shape, 1)

    def scalar(at):
        return jnp.sum(jnp.where(lane == at, sums, 0.0), axis=1, keepdims=True)

    rho, curvature = scalar(RHO), scalar(FF)
    if first:
        beta = None
    else:
        direction, moved, along, multipliers, scalars = old
        beta = rho / scalars[0:1, 0:1]
        curvature = curvature + 2.0 * beta * scalar(FD) + beta * beta * scalars[1:2, 0:1]
    step = rho / curvature
    out = {}
    for s in range(2):
        for f in range(count):
            d = f % 3
            if d == 2 and (s == 0) == (f == 2):
                other = image[1 - s, 5 if f == 2 else 2]
            else:
                a, b = ((xa, xb), (ya, yb), (za, zb))[d]
                va = a[s] if d < 2 else a[...]
                vb = b[s] if d < 2 else b[...]
                other = pick(parity[d], vb, va) if f < 3 else pick(parity[d], va, vb)
            change = image[s, f] + other - fold3(mm(left, lift[s * 6 + f], NN))
            change = masked(change, masks[s][f])
            value = residual[s, f]
            towards = value
            if not first:
                towards = value + beta * direction[s, f]
                change = change + beta * moved[s, f]
            out[s, f] = (value - step * change, towards, change)
            if f < 3:
                gain = step * towards
                out[s, f] += (gain if first else multipliers[s, f] + gain,)
    return parity, masks, beta, rho, curvature, out


def middle_kernel(sizes, first, *refs):
    pattern, factors, perm, lift, solve = refs[:5]
    recvs = refs[5:12]
    residual, forward, image = refs[12:15]
    rest = refs[15:]
    if first:
        old = None
    else:
        old, rest = rest[:5], rest[5:]
    new_residual, new_forward, new_image, new_direction, new_moved, new_along, new_multipliers, new_scalars = rest[:8]
    sends = rest[8:]
    parity, masks, beta, rho, curvature, out = update(
        sizes, first, recvs, (residual, forward, image, lift, old), 6
    )
    row = lax.broadcasted_iota(jnp.int32, (8, LANES), 0)
    new_scalars[...] = jnp.where(row == 0, rho, curvature)
    now = [[None] * 6 for _ in range(2)]
    along = [[None] * 6 for _ in range(2)]
    for s in range(2):
        for f in range(6):
            values = out[s, f]
            now[s][f] = values[0]
            new_residual[s, f] = values[0]
            new_direction[s, f] = values[1]
            new_moved[s, f] = values[2]
            if f < 3:
                new_multipliers[s, f] = values[3]
            line = forward[s, f] if first else forward[s, f] + beta * old[2][s, f]
            along[s][f] = line
            new_along[s, f] = line
    apply_factors(now, pattern, factors, perm, lift, masks, parity, along, new_forward, new_image, solve, sends)


def last_kernel(sizes, lift, *refs):
    recvs = refs[:7]
    residual, forward, image = refs[7:10]
    old = refs[10:15]
    multipliers, final = refs[15:]
    out = update(sizes, False, recvs, (residual, forward, image, lift, old), 3)[5]
    for s in range(2):
        for f in range(3):
            final[s, f] = out[s, f][0]
            multipliers[s, f] = out[s, f][3]


def exchange(values, axis):
    size = lax.axis_size(axis)
    first = lax.ppermute(values[0], axis, [(i, i ^ 1) for i in range(size)])
    if size == 2:
        return first, first
    second = lax.ppermute(
        values[1], axis, [(i, (i + 1) % size if i % 2 else (i - 1) % size) for i in range(size)]
    )
    return first, second


def communicate(sends):
    xa, xb, ya, yb, za, zb, send = sends
    recv = lax.all_to_all(send, AXES, 0, 0, tiled=True)
    za, zb = exchange((za, zb), "gz")
    xa, xb = exchange((xa, xb), "gx")
    ya, yb = exchange((ya, yb), "gy")
    return xa, xb, ya, yb, za, zb, recv


def per_device(dual_rhs, factors, block_pattern, face_map, rigid_modes, coarse_solve):
    sizes = tuple(lax.axis_size(a) for a in AXES)
    devices = sizes[0] * sizes[1] * sizes[2]
    cases, dofs = dual_rhs.shape[4:]
    nc = coarse_solve.shape[1]
    slabs = -(-nc // 256)
    rhs = dual_rhs.reshape(dual_rhs.shape[2:])
    factors = factors.reshape(factors.shape[2:])
    pattern = block_pattern.reshape(block_pattern.shape[2:])
    fmap = face_map.reshape(face_map.shape[2:])
    modes = rigid_modes.reshape(rigid_modes.shape[2:])
    vmem = pl.BlockSpec(memory_space=pltpu.VMEM)
    smem = pl.BlockSpec(memory_space=pltpu.SMEM)
    params = pltpu.CompilerParams(vmem_limit_bytes=24 << 20)

    def shape(*dims, dtype=f32):
        return jax.ShapeDtypeStruct(dims, dtype)

    def call(kernel, outs, ins, first_smem=False, scratch=()):
        specs = [smem if i == 0 and first_smem else vmem for i in range(len(ins))]
        return pl.pallas_call(
            kernel,
            out_shape=outs,
            in_specs=specs,
            out_specs=[vmem] * len(outs),
            scratch_shapes=list(scratch),
            compiler_params=params,
        )(*ins)

    packs = [shape(48 + 16 * slabs, dofs)] * 4 + [shape(24 + 16 * slabs, dofs)] * 2
    xa, xb, ya, yb, za, zb = call(pack_kernel, packs, [rhs, modes, fmap, coarse_solve])
    za, zb = exchange((za, zb), "gz")
    xa, xb = exchange((xa, xb), "gx")
    ya, yb = exchange((ya, yb), "gy")

    table = jnp.asarray(slot_table(*sizes, nc)).reshape(devices, 1, LANES)
    faces = shape(2, 6, cases, dofs)
    sent = shape(devices, cases, LANES)
    perm, lift, start, solve, send = call(
        setup_kernel,
        [
            shape(6, dofs, dofs, dtype=bf16),
            shape(12, 2 * LANES, dofs, dtype=bf16),
            faces,
            shape(devices // 2, 2 * LANES, 2 * LANES, dtype=bf16),
            sent,
        ],
        [rhs, modes, fmap, coarse_solve, table, xa, xb, ya, yb, za, zb],
        scratch=(pltpu.VMEM((LANES, dofs), f32), pltpu.VMEM((LANES, 256 * slabs), f32)),
    )
    recv = lax.all_to_all(send, AXES, 0, 0, tiled=True)

    sends = [shape(2, cases, dofs)] * 4 + [shape(cases, dofs)] * 2 + [sent]
    residual, forward, image, *out = call(
        functools.partial(first_kernel, sizes),
        [faces, faces, faces] + sends,
        [pattern, recv, start, factors, perm, lift, solve],
        first_smem=True,
    )
    old = []
    for iteration in range(ITERS - 1):
        got = communicate(out)
        residual, forward, image, *out = call(
            functools.partial(middle_kernel, sizes, iteration == 0),
            [faces] * 6 + [shape(2, 3, cases, dofs), shape(8, LANES)] + sends,
            [pattern, factors, perm, lift, solve, *got, residual, forward, image, *old],
            first_smem=True,
        )
        old, out = out[:5], out[5:]
    got = communicate(out)
    multipliers, final = call(
        functools.partial(last_kernel, sizes),
        [shape(2, 3, cases, dofs)] * 2,
        [lift, *got, residual, forward, image, *old],
    )
    return multipliers.reshape(dual_rhs.shape), final.reshape(dual_rhs.shape)


def solution(mesh):
    return jax.shard_map(
        per_device,
        mesh=mesh,
        in_specs=(
            P("gx", "gy", "gz", None, None, None),
            P("gx", "gy", "gz", None, None, None, None),
            P("gx", "gy", "gz", None, None),
            P("gx", "gy", "gz", None, None),
            P("gx", "gy", "gz", None, None, None),
            P(("gx", "gy", "gz"), None),
        ),
        out_specs=(P("gx", "gy", "gz", None, None, None), P("gx", "gy", "gz", None, None, None)),
        check_vma=False,
    )
```

time: 766 us -> 192 us (0.25); the launches traced: 754 us -> 190 us
  blocking collectives: 490 us -> 0 us
  matrix products: 74.7 us -> 0 us
  local copies, waits for them, and re-layouts: 1.66 us -> 69.1 us
  starting transfers between devices: 117 us -> 54.5 us
  Pallas kernels: 0 us -> 41.6 us
  waiting for transfers between devices: 57.8 us -> 24 us
  between operations: 11.7 us -> 0.8 us
    psum x7 -> x0, blocking collectives: 288 us -> none  [the longest x4 168 us: squares_total(): return lax.psum(jnp.sum(residual * residual), ('gx', 'gy', 'gz'))]
    all_gather x5 -> x0, blocking collectives: 202 us -> none  [project(): lax.all_gather(coarse_rhs, ('gx', 'gy', 'gz'), axis=0, tiled=True)]
    ppermute x54 -> x25, starting transfers between devices: 117 us -> 36.9 us  [the longest x10 19.4 us: exchange(): lax.ppermute(values[1], axis, [(i, (i + 1) % size if i % 2 else (i - 1) %...]
    dot_general x41 -> x0, matrix products: 74.7 us -> none  [the longest x4 27.7 us: per_device(): jnp.einsum('sijab,sjcb->sica', flat_w, flat_u, preferred_element_type=jnp...]
    unnamed x16 -> x140, local copies, waits for them, and re-layouts: 0.14 us -> 68.4 us
    ppermute x54 -> x25, waiting for transfers between devices: 57.8 us -> 14.3 us  [the longest x10 8.1 us: exchange(): lax.ppermute(values[1], axis, [(i, (i + 1) % size if i % 2 else (i - 1) %...]
    pallas_call x0 -> x7, Pallas kernels: none -> 41.6 us  [call(): pl.pallas_call(kernel, out_shape=outs, in_specs=specs, out_specs=[vmem] *...]
    all_to_all x0 -> x5, starting transfers between devices: none -> 17.6 us  [the longest x4 13.7 us: communicate(): recv = lax.all_to_all(send, AXES, 0, 0, tiled=True)]
  transfers between devices with their start and end apart: 54 -> 30, of which waited for: 28 -> 11; matrix products, arithmetic and copies ran while one was open for 0% -> 0% of each run, Pallas kernels for 0% -> 0%
where the time goes in v1:
time: 192 us; the launch traced here: 190 us
  local copies, waits for them, and re-layouts  69.1 us (36%)
  starting transfers between devices  54.5 us (28%)
  Pallas kernels  41.6 us (22%)
  waiting for transfers between devices  24 us (12%)
    unnamed x140, local copies, waits for them, and re-layouts  68.4 us
    pallas_call x7, Pallas kernels, call(): pl.pallas_call(kernel, out_shape=outs, in_specs=specs, out_specs=[vmem] *...  41.6 us
    ppermute x10, starting transfers between devices, exchange(): lax.ppermute(values[1], axis, [(i, (i + 1) % size if i % 2 else (i - 1) %...  19.4 us
    ppermute x15, starting transfers between devices, exchange(): first = lax.ppermute(values[0], axis, [(i, i ^ 1) for i in range(size)])  17.5 us
    all_to_all x4, starting transfers between devices, communicate(): recv = lax.all_to_all(send, AXES, 0, 0, tiled=True)  13.7 us
    all_to_all x1, waiting for transfers between devices, per_device(): recv = lax.all_to_all(send, AXES, 0, 0, tiled=True)  9.69 us
    ppermute x10, waiting for transfers between devices, exchange(): lax.ppermute(values[1], axis, [(i, (i + 1) % size if i % 2 else (i - 1) %...  8.1 us
    ppermute x15, waiting for transfers between devices, exchange(): first = lax.ppermute(values[0], axis, [(i, i ^ 1) for i in range(size)])  6.2 us
  transfers between devices with their start and end apart: 30, of which 11 were waited for; matrix products, arithmetic and copies ran while one was open for 0% of the time, Pallas kernels for 0%

profile of v1, /device:TPU:0, one launch (start us, length us, event | category | flops | bytes accessed | tf_op | source)
XLA Modules:
  0.0 189.9 jit_solution(1034276130022145982)
XLA Ops:
  1.3 0.9 copy.17
  4.5 2.9 %collective-permute-start = (f32[80,256]{1,0:T(8,128)S(1)}, f32[80,256]{1,0:T(8,128)S(1)}, u32[]{:S(2)}, u32[]{:S(2)}) collective-permute-start(f32[80,256]{1,0:T(8,128)S(1)} %get-tuple-element.65), channel_id=1, source_target_pairs={{0,8},{8,0},{16,24},{24,16},{1,9},{9,1},{17,25},{25,17},{2,10},{10... | collective-permute-start | bytes 245768 | tf_op jit(solution)/shard_map/ppermute | solution.py:435
  7.5 1.5 collective-permute-start.1
  8.9 1.6 collective-permute-start.2
  10.5 2.5 %collective-permute-start.3 = (f32[80,256]{1,0:T(8,128)S(1)}, f32[80,256]{1,0:T(8,128)S(1)}, u32[]{:S(2)}, u32[]{:S(2)}) collective-permute-start(f32[80,256]{1,0:T(8,128)S(1)} %get-tuple-element.68), channel_id=1, source_target_pairs={{0,6},{2,4},{4,2},{6,0},{1,7},{3,5},{5,3},{7,1},{8,14},{10,12},{12... | collective-permute-start | bytes 245768 | tf_op jit(solution)/shard_map/ppermute | solution.py:438
  13.0 1.2 collective-permute-done.4.za.zb
  14.3 2.5 %collective-permute-done.3.yb = f32[80,256]{1,0:T(8,128)S(1)} collective-permute-done((f32[80,256]{1,0:T(8,128)S(1)}, f32[80,256]{1,0:T(8,128)S(1)}, u32[]{:S(2)}, u32[]{:S(2)}) %collective-permute-start.3) | collective-permute-done | bytes 81952 | tf_op jit(solution)/shard_map/ppermute | solution.py:438
  17.5 7.7 %shard_map.87 = (bf16[6,256,256]{2,1,0:T(8,128)(2,1)S(1)}, bf16[12,256,256]{2,1,0:T(8,128)(2,1)S(1)}, f32[2,6,16,256]{3,2,1,0:T(8,128)S(1)}, bf16[16,256,256]{2,1,0:T(8,128)(2,1)S(1)}, f32[32,16,128]{2,1,0:T(8,128)}) custom-call(f32[2,3,16,256]{3,2,1,0:T(8,128)S(1)} %bitcast.18, f32[2,6,6,256]{3,2,1,0:T(8,128)S(1)} %bitcast.16, s32[2,3,256]{2,1,0:T(4,128)S(1)} %bitcast.20, ...), custom_call_target="tpu_custom_call" | custom-call | tf_op jit(solution)/shard_map/pallas_call | solution.py:473
  25.1 1.3 copy-done.4
  26.5 3.9 %all-to-all-start = ((f32[32,16,128]{2,1,0:T(8,128)}), f32[32,16,128]{2,1,0:T(8,128)S(1)}, u32[]{:S(2)}, u32[]{:S(2)}) async-start(f32[32,16,128]{2,1,0:T(8,128)} %get-tuple-element.73), calls=%async_computation | async-start | bytes 524288 | tf_op jit(solution)/shard_map/all_to_all | solution.py:503
  31.0 9.7 %all-to-all-done.recv = f32[32,16,128]{2,1,0:T(8,128)S(1)} async-done(((f32[32,16,128]{2,1,0:T(8,128)}), f32[32,16,128]{2,1,0:T(8,128)S(1)}, u32[]{:S(2)}, u32[]{:S(2)}) %all-to-all-start) | async-done | bytes 262176 | tf_op jit(solution)/shard_map/all_to_all | solution.py:503
  40.7 3.7 %copy-done = bf16[1,1,2,6,6,256,256]{6,5,4,3,2,1,0:T(8,128)(2,1)S(1)} copy-done((bf16[1,1,2,6,6,256,256]{6,5,4,3,2,1,0:T(8,128)(2,1)S(1)}, bf16[1,1,2,6,6,256,256]{6,5,4,3,2,1,0:T(8,128)(2,1)}, u32[]{:S(2)}) %copy-start) | copy-done | bytes 9437208
  44.4 1.6 copy-done.5
  46.0 8.1 %shard_map.88 = (f32[2,6,16,256]{3,2,1,0:T(8,128)S(1)}, f32[2,6,16,256]{3,2,1,0:T(8,128)S(1)}, f32[2,6,16,256]{3,2,1,0:T(8,128)S(1)}, f32[2,16,256]{2,1,0:T(8,12...) custom-call(s32[2,6,6]{2,1,0:T(8,128)S(1)} %copy.14.pattern.refs_0_,, ...), custom_call_target="tpu_custom_call" | custom-call | tf_op jit(solution)/shard_map/pallas_call | solution.py:473
  54.7 2.6 %all-to-all-start.1 = ((f32[32,16,128]{2,1,0:T(8,128)}), f32[32,16,128]{2,1,0:T(8,128)S(1)}, u32[]{:S(2)}, u32[]{:S(2)}) async-start(f32[32,16,128]{2,1,0:T(8,128)} %get-tuple-element.80), calls=%async_computation.1 | async-start | bytes 524288 | tf_op jit(solution)/shard_map/all_to_all | solution.py:446
  57.3 1.8 collective-permute-start.5
  59.0 1.5 collective-permute-start.6
  60.5 1.5 collective-permute-start.7
  62.0 2.4 %collective-permute-start.8 = (f32[2,16,256]{2,1,0:T(8,128)S(1)}, f32[2,16,256]{2,1,0:T(8,128)S(1)}, u32[]{:S(2)}, u32[]{:S(2)}) collective-permute-start(f32[2,16,256]{2,1,0:T(8,128)S(1)} %get-tuple-element.78), channel_id=1, source_target_pairs={{0,6},{2,4},{4,2},{6,0},{1,7},{3,5},{5,3},{7,1},{8,14},{10,12},{12... | collective-permute-start | bytes 98312 | tf_op jit(solution)/shard_map/ppermute | solution.py:438
  64.4 1.4 collective-permute-done.9.refs_9_.refs_10_
  65.8 1.9 %collective-permute-done.8.refs_8_ = f32[2,16,256]{2,1,0:T(8,128)S(1)} collective-permute-done((f32[2,16,256]{2,1,0:T(8,128)S(1)}, f32[2,16,256]{2,1,0:T(8,128)S(1)}, u32[]{:S(2)}, u32[]{:S(2)}) %collective-permute-start.8) | collective-permute-done | bytes 32800 | tf_op jit(solution)/shard_map/ppermute | solution.py:438
  67.8 3.7 %copy-done.1 = bf16[1,1,2,6,6,256,256]{6,5,4,3,2,1,0:T(8,128)(2,1)S(1)} copy-done((bf16[1,1,2,6,6,256,256]{6,5,4,3,2,1,0:T(8,128)(2,1)S(1)}, bf16[1,1,2,6,6,256,256]{6,5,4,3,2,1,0:T(8,128)(2,1)}, u32[]{:S(2)}) %copy-start.1) | copy-done | bytes 9437208
  71.4 1.6 copy-done.6
  73.0 8.1 %shard_map.89 = (f32[2,6,16,256]{3,2,1,0:T(8,128)S(1)}, f32[2,6,16,256]{3,2,1,0:T(8,128)S(1)}, f32[2,6,16,256]{3,2,1,0:T(8,128)S(1)}, f32[2,6,16,256]{3,2,1,0:T(...) custom-call(s32[2,6,6]{2,1,0:T(8,128)S(1)} %copy.14.pattern.refs_0_,, ...), custom_call_target="tpu_custom_call" | custom-call | tf_op jit(solution)/shard_map/pallas_call | solution.py:473
  85.8 3.9 %all-to-all-start.2 = ((f32[32,16,128]{2,1,0:T(8,128)}), f32[32,16,128]{2,1,0:T(8,128)S(1)}, u32[]{:S(2)}, u32[]{:S(2)}) async-start(f32[32,16,128]{2,1,0:T(8,128)} %get-tuple-element.89), calls=%async_computation.2 | async-start | bytes 524288 | tf_op jit(solution)/shard_map/all_to_all | solution.py:446
  89.8 1.7 collective-permute-start.10
  91.4 1.5 collective-permute-start.11
  92.9 1.5 collective-permute-start.12
  94.4 2.4 %collective-permute-start.13 = (f32[2,16,256]{2,1,0:T(8,128)}, f32[2,16,256]{2,1,0:T(8,128)S(1)}, u32[]{:S(2)}, u32[]{:S(2)}) collective-permute-start(f32[2,16,256]{2,1,0:T(8,128)} %get-tuple-element.87), channel_id=1, source_target_pairs={{0,6},{2,4},{4,2},{6,0},{1,7},{3,5},{5,3},{7,1},{8,14},{10,12},{12... | collective-permute-start | bytes 98312 | tf_op jit(solution)/shard_map/ppermute | solution.py:438
  96.7 1.2 collective-permute-done.14.refs_9_.refs_10_
  101.0 3.7 %copy-done.2 = bf16[1,1,2,6,6,256,256]{6,5,4,3,2,1,0:T(8,128)(2,1)S(1)} copy-done((bf16[1,1,2,6,6,256,256]{6,5,4,3,2,1,0:T(8,128)(2,1)S(1)}, bf16[1,1,2,6,6,256,256]{6,5,4,3,2,1,0:T(8,128)(2,1)}, u32[]{:S(2)}) %copy-start.2) | copy-done | bytes 9437208
  104.7 1.6 copy-done.7
  106.3 0.9 copy-done.15
  107.2 0.9 copy-done.17
  108.1 0.9 copy-done.19
  109.1 0.9 copy-done.21
  110.0 0.9 copy-done.23
  110.9 0.9 copy-done.25
  115.8 8.1 %shard_map.90 = (f32[2,6,16,256]{3,2,1,0:T(8,128)S(1)}, f32[2,6,16,256]{3,2,1,0:T(8,128)S(1)}, f32[2,6,16,256]{3,2,1,0:T(8,128)S(1)}, f32[2,6,16,256]{3,2,1,0:T(...) custom-call(s32[2,6,6]{2,1,0:T(8,128)S(1)} %copy.14.pattern.refs_0_,, ...), custom_call_target="tpu_custom_call" | custom-call | tf_op jit(solution)/shard_map/pallas_call | solution.py:473
  127.7 3.6 %all-to-all-start.3 = ((f32[32,16,128]{2,1,0:T(8,128)}), f32[32,16,128]{2,1,0:T(8,128)S(1)}, u32[]{:S(2)}, u32[]{:S(2)}) async-start(f32[32,16,128]{2,1,0:T(8,128)} %get-tuple-element.103), calls=%async_computation.3 | async-start | bytes 524288 | tf_op jit(solution)/shard_map/all_to_all | solution.py:446
  131.3 1.8 collective-permute-start.15
  133.1 1.5 collective-permute-start.16
  134.6 1.5 collective-permute-start.17
  136.1 2.4 %collective-permute-start.18 = (f32[2,16,256]{2,1,0:T(8,128)}, f32[2,16,256]{2,1,0:T(8,128)S(1)}, u32[]{:S(2)}, u32[]{:S(2)}) collective-permute-start(f32[2,16,256]{2,1,0:T(8,128)} %copy-done.61), channel_id=1, source_target_pairs={{0,6},{2,4},{4,2},{6,0},{1,7},{3,5},{5,3},{7,1},{8,14},{10,12},{12... | collective-permute-start | bytes 98312 | tf_op jit(solution)/shard_map/ppermute | solution.py:438
  138.4 1.2 collective-permute-done.19.refs_9_.refs_10_
  142.7 3.7 %copy-done.3 = bf16[1,1,2,6,6,256,256]{6,5,4,3,2,1,0:T(8,128)(2,1)S(1)} copy-done((bf16[1,1,2,6,6,256,256]{6,5,4,3,2,1,0:T(8,128)(2,1)S(1)}, bf16[1,1,2,6,6,256,256]{6,5,4,3,2,1,0:T(8,128)(2,1)}, u32[]{:S(2)}) %copy-start.3) | copy-done | bytes 9437208
  146.4 1.6 copy-done.8
  148.0 0.9 copy-done.11
  148.9 0.9 copy-done.13
  152.9 8.1 %shard_map.91 = (f32[2,6,16,256]{3,2,1,0:T(8,128)S(1)}, f32[2,6,16,256]{3,2,1,0:T(8,128)S(1)}, f32[2,6,16,256]{3,2,1,0:T(8,128)S(1)}, f32[2,6,16,256]{3,2,1,0:T(...) custom-call(s32[2,6,6]{2,1,0:T(8,128)S(1)} %copy.14.pattern.refs_0_,, ...), custom_call_target="tpu_custom_call" | custom-call | tf_op jit(solution)/shard_map/pallas_call | solution.py:473
  168.2 3.6 %all-to-all-start.4 = ((f32[32,16,128]{2,1,0:T(8,128)}), f32[32,16,128]{2,1,0:T(8,128)S(1)}, u32[]{:S(2)}, u32[]{:S(2)}) async-start(f32[32,16,128]{2,1,0:T(8,128)} %get-tuple-element.117), calls=%async_computation.4 | async-start | bytes 524288 | tf_op jit(solution)/shard_map/all_to_all | solution.py:446
  171.8 1.8 collective-permute-start.20
  173.6 1.5 collective-permute-start.21
  175.1 1.5 collective-permute-start.22
  176.5 2.4 %collective-permute-start.23 = (f32[2,16,256]{2,1,0:T(8,128)}, f32[2,16,256]{2,1,0:T(8,128)S(1)}, u32[]{:S(2)}, u32[]{:S(2)}) collective-permute-start(f32[2,16,256]{2,1,0:T(8,128)} %copy-done.60), channel_id=1, source_target_pairs={{0,6},{2,4},{4,2},{6,0},{1,7},{3,5},{5,3},{7,1},{8,14},{10,12},{12... | collective-permute-start | bytes 98312 | tf_op jit(solution)/shard_map/ppermute | solution.py:438
  178.9 1.2 collective-permute-done.24.refs_4_.refs_5_
  180.1 2.5 %collective-permute-done.23.refs_3_ = f32[2,16,256]{2,1,0:T(8,128)S(1)} collective-permute-done((f32[2,16,256]{2,1,0:T(8,128)}, f32[2,16,256]{2,1,0:T(8,128)S(1)}, u32[]{:S(2)}, u32[]{:S(2)}) %collective-permute-start.23) | collective-permute-done | bytes 32800 | tf_op jit(solution)/shard_map/ppermute | solution.py:438
  182.6 0.9 copy-done.27
  183.5 0.9 copy-done.29
  184.4 0.9 copy-done.31
  185.4 0.9 copy-done.33
  186.3 0.9 copy-done.35
  187.2 0.9 copy-done.37
  189.0 0.9 shard_map.92
  (144 shorter events, 34.8 us)
Async XLA Ops:
  2.2 0.9 copy-start.9
  4.5 9.7 %collective-permute-start = (f32[80,256]{1,0:T(8,128)S(1)}, f32[80,256]{1,0:T(8,128)S(1)}, u32[]{:S(2)}, u32[]{:S(2)}) collective-permute-start(f32[80,256]{1,0:T(8,128)S(1)} %get-tuple-element.65), channel_id=1, source_target_pairs={{0,8},{8,0},{16,24},{24,16},{1,9},{9,1},{17,25},{25,17},{2,10},{10... | collective-permute-start | bytes 245768 | tf_op jit(solution)/shard_map/ppermute | solution.py:435
  7.5 6.8 %collective-permute-start.1 = (f32[80,256]{1,0:T(8,128)S(1)}, f32[80,256]{1,0:T(8,128)S(1)}, u32[]{:S(2)}, u32[]{:S(2)}) collective-permute-start(f32[80,256]{1,0:T(8,128)S(1)} %get-tuple-element.66), channel_id=1, source_target_pairs={{0,24},{8,16},{16,8},{24,0},{1,25},{9,17},{17,9},{25,1},{2,26},{10... | collective-permute-start | bytes 245768 | tf_op jit(solution)/shard_map/ppermute | solution.py:438
  8.9 5.3 %collective-permute-start.2 = (f32[80,256]{1,0:T(8,128)S(1)}, f32[80,256]{1,0:T(8,128)S(1)}, u32[]{:S(2)}, u32[]{:S(2)}) collective-permute-start(f32[80,256]{1,0:T(8,128)S(1)} %get-tuple-element.67), channel_id=1, source_target_pairs={{0,2},{2,0},{4,6},{6,4},{1,3},{3,1},{5,7},{7,5},{8,10},{10,8},{12,... | collective-permute-start | bytes 245768 | tf_op jit(solution)/shard_map/ppermute | solution.py:435
  10.5 6.2 %collective-permute-start.3 = (f32[80,256]{1,0:T(8,128)S(1)}, f32[80,256]{1,0:T(8,128)S(1)}, u32[]{:S(2)}, u32[]{:S(2)}) collective-permute-start(f32[80,256]{1,0:T(8,128)S(1)} %get-tuple-element.68), channel_id=1, source_target_pairs={{0,6},{2,4},{4,2},{6,0},{1,7},{3,5},{5,3},{7,1},{8,14},{10,12},{12... | collective-permute-start | bytes 245768 | tf_op jit(solution)/shard_map/ppermute | solution.py:438
  13.0 1.2 collective-permute-start.4
  25.1 1.3 copy-start.4
  26.5 14.3 %all-to-all-start = ((f32[32,16,128]{2,1,0:T(8,128)}), f32[32,16,128]{2,1,0:T(8,128)S(1)}, u32[]{:S(2)}, u32[]{:S(2)}) async-start(f32[32,16,128]{2,1,0:T(8,128)} %get-tuple-element.73), calls=%async_computation | async-start | bytes 524288 | tf_op jit(solution)/shard_map/all_to_all | solution.py:503
  40.7 3.7 %copy-start = (bf16[1,1,2,6,6,256,256]{6,5,4,3,2,1,0:T(8,128)(2,1)S(1)}, bf16[1,1,2,6,6,256,256]{6,5,4,3,2,1,0:T(8,128)(2,1)}, u32[]{:S(2)}) copy-start(bf16[1,1,2,6,6,256,256]{6,5,4,3,2,1,0:T(8,128)(2,1)} %param.8) | copy-start | bytes 28311556
  44.4 1.6 copy-start.5
  54.7 13.1 %all-to-all-start.1 = ((f32[32,16,128]{2,1,0:T(8,128)}), f32[32,16,128]{2,1,0:T(8,128)S(1)}, u32[]{:S(2)}, u32[]{:S(2)}) async-start(f32[32,16,128]{2,1,0:T(8,128)} %get-tuple-element.80), calls=%async_computation.1 | async-start | bytes 524288 | tf_op jit(solution)/shard_map/all_to_all | solution.py:446
  57.3 8.5 %collective-permute-start.5 = (f32[2,16,256]{2,1,0:T(8,128)S(1)}, f32[2,16,256]{2,1,0:T(8,128)S(1)}, u32[]{:S(2)}, u32[]{:S(2)}) collective-permute-start(f32[2,16,256]{2,1,0:T(8,128)S(1)} %get-tuple-element.75), channel_id=1, source_target_pairs={{0,8},{8,0},{16,24},{24,16},{1,9},{9,1},{17,25},{25,17},{2,10},{10... | collective-permute-start | bytes 98312 | tf_op jit(solution)/shard_map/ppermute | solution.py:435
  59.0 6.8 %collective-permute-start.6 = (f32[2,16,256]{2,1,0:T(8,128)S(1)}, f32[2,16,256]{2,1,0:T(8,128)S(1)}, u32[]{:S(2)}, u32[]{:S(2)}) collective-permute-start(f32[2,16,256]{2,1,0:T(8,128)S(1)} %get-tuple-element.76), channel_id=1, source_target_pairs={{0,24},{8,16},{16,8},{24,0},{1,25},{9,17},{17,9},{25,1},{2,26},{10... | collective-permute-start | bytes 98312 | tf_op jit(solution)/shard_map/ppermute | solution.py:438
  60.5 5.3 %collective-permute-start.7 = (f32[2,16,256]{2,1,0:T(8,128)S(1)}, f32[2,16,256]{2,1,0:T(8,128)S(1)}, u32[]{:S(2)}, u32[]{:S(2)}) collective-permute-start(f32[2,16,256]{2,1,0:T(8,128)S(1)} %get-tuple-element.77), channel_id=1, source_target_pairs={{0,2},{2,0},{4,6},{6,4},{1,3},{3,1},{5,7},{7,5},{8,10},{10,8},{12,... | collective-permute-start | bytes 98312 | tf_op jit(solution)/shard_map/ppermute | solution.py:435
  62.0 5.8 %collective-permute-start.8 = (f32[2,16,256]{2,1,0:T(8,128)S(1)}, f32[2,16,256]{2,1,0:T(8,128)S(1)}, u32[]{:S(2)}, u32[]{:S(2)}) collective-permute-start(f32[2,16,256]{2,1,0:T(8,128)S(1)} %get-tuple-element.78), channel_id=1, source_target_pairs={{0,6},{2,4},{4,2},{6,0},{1,7},{3,5},{5,3},{7,1},{8,14},{10,12},{12... | collective-permute-start | bytes 98312 | tf_op jit(solution)/shard_map/ppermute | solution.py:438
  64.4 1.4 collective-permute-start.9
  67.7 3.7 %copy-start.1 = (bf16[1,1,2,6,6,256,256]{6,5,4,3,2,1,0:T(8,128)(2,1)S(1)}, bf16[1,1,2,6,6,256,256]{6,5,4,3,2,1,0:T(8,128)(2,1)}, u32[]{:S(2)}) copy-start(bf16[1,1,2,6,6,256,256]{6,5,4,3,2,1,0:T(8,128)(2,1)} %param.8) | copy-start | bytes 28311556
  71.4 1.6 copy-start.6
  85.8 15.1 %all-to-all-start.2 = ((f32[32,16,128]{2,1,0:T(8,128)}), f32[32,16,128]{2,1,0:T(8,128)S(1)}, u32[]{:S(2)}, u32[]{:S(2)}) async-start(f32[32,16,128]{2,1,0:T(8,128)} %get-tuple-element.89), calls=%async_computation.2 | async-start | bytes 524288 | tf_op jit(solution)/shard_map/all_to_all | solution.py:446
  89.8 8.2 %collective-permute-start.10 = (f32[2,16,256]{2,1,0:T(8,128)}, f32[2,16,256]{2,1,0:T(8,128)S(1)}, u32[]{:S(2)}, u32[]{:S(2)}) collective-permute-start(f32[2,16,256]{2,1,0:T(8,128)} %get-tuple-element.84), channel_id=1, source_target_pairs={{0,8},{8,0},{16,24},{24,16},{1,9},{9,1},{17,25},{25,17},{2,10},{10... | collective-permute-start | bytes 98312 | tf_op jit(solution)/shard_map/ppermute | solution.py:435
  91.4 7.1 %collective-permute-start.11 = (f32[2,16,256]{2,1,0:T(8,128)}, f32[2,16,256]{2,1,0:T(8,128)S(1)}, u32[]{:S(2)}, u32[]{:S(2)}) collective-permute-start(f32[2,16,256]{2,1,0:T(8,128)} %get-tuple-element.85), channel_id=1, source_target_pairs={{0,24},{8,16},{16,8},{24,0},{1,25},{9,17},{17,9},{25,1},{2,26},{10... | collective-permute-start | bytes 98312 | tf_op jit(solution)/shard_map/ppermute | solution.py:438
  92.9 6.3 %collective-permute-start.12 = (f32[2,16,256]{2,1,0:T(8,128)}, f32[2,16,256]{2,1,0:T(8,128)S(1)}, u32[]{:S(2)}, u32[]{:S(2)}) collective-permute-start(f32[2,16,256]{2,1,0:T(8,128)} %get-tuple-element.86), channel_id=1, source_target_pairs={{0,2},{2,0},{4,6},{6,4},{1,3},{3,1},{5,7},{7,5},{8,10},{10,8},{12,... | collective-permute-start | bytes 98312 | tf_op jit(solution)/shard_map/ppermute | solution.py:435
  94.4 6.0 %collective-permute-start.13 = (f32[2,16,256]{2,1,0:T(8,128)}, f32[2,16,256]{2,1,0:T(8,128)S(1)}, u32[]{:S(2)}, u32[]{:S(2)}) collective-permute-start(f32[2,16,256]{2,1,0:T(8,128)} %get-tuple-element.87), channel_id=1, source_target_pairs={{0,6},{2,4},{4,2},{6,0},{1,7},{3,5},{5,3},{7,1},{8,14},{10,12},{12... | collective-permute-start | bytes 98312 | tf_op jit(solution)/shard_map/ppermute | solution.py:438
  96.7 1.2 collective-permute-start.14
  101.0 3.7 %copy-start.2 = (bf16[1,1,2,6,6,256,256]{6,5,4,3,2,1,0:T(8,128)(2,1)S(1)}, bf16[1,1,2,6,6,256,256]{6,5,4,3,2,1,0:T(8,128)(2,1)}, u32[]{:S(2)}) copy-start(bf16[1,1,2,6,6,256,256]{6,5,4,3,2,1,0:T(8,128)(2,1)} %param.8) | copy-start | bytes 28311556
  104.7 1.6 copy-start.7
  106.3 0.9 copy-start.15
  107.2 0.9 copy-start.17
  108.1 0.9 copy-start.19
  109.1 0.9 copy-start.21
  110.0 0.9 copy-start.23
  110.9 0.9 copy-start.25
  111.8 0.9 copy-start.39
  112.7 0.8 copy-start.46
  113.5 0.8 copy-start.50
  114.2 0.8 copy-start.54
  115.0 0.8 copy-start.58
  127.7 15.0 %all-to-all-start.3 = ((f32[32,16,128]{2,1,0:T(8,128)}), f32[32,16,128]{2,1,0:T(8,128)S(1)}, u32[]{:S(2)}, u32[]{:S(2)}) async-start(f32[32,16,128]{2,1,0:T(8,128)} %get-tuple-element.103), calls=%async_computation.3 | async-start | bytes 524288 | tf_op jit(solution)/shard_map/all_to_all | solution.py:446
  131.3 8.3 %collective-permute-start.15 = (f32[2,16,256]{2,1,0:T(8,128)}, f32[2,16,256]{2,1,0:T(8,128)S(1)}, u32[]{:S(2)}, u32[]{:S(2)}) collective-permute-start(f32[2,16,256]{2,1,0:T(8,128)} %copy-done.67), channel_id=1, source_target_pairs={{0,8},{8,0},{16,24},{24,16},{1,9},{9,1},{17,25},{25,17},{2,10},{10... | collective-permute-start | bytes 98312 | tf_op jit(solution)/shard_map/ppermute | solution.py:435
  133.1 7.1 %collective-permute-start.16 = (f32[2,16,256]{2,1,0:T(8,128)}, f32[2,16,256]{2,1,0:T(8,128)S(1)}, u32[]{:S(2)}, u32[]{:S(2)}) collective-permute-start(f32[2,16,256]{2,1,0:T(8,128)} %copy-done.65), channel_id=1, source_target_pairs={{0,24},{8,16},{16,8},{24,0},{1,25},{9,17},{17,9},{25,1},{2,26},{10... | collective-permute-start | bytes 98312 | tf_op jit(solution)/shard_map/ppermute | solution.py:438
  134.6 6.3 %collective-permute-start.17 = (f32[2,16,256]{2,1,0:T(8,128)}, f32[2,16,256]{2,1,0:T(8,128)S(1)}, u32[]{:S(2)}, u32[]{:S(2)}) collective-permute-start(f32[2,16,256]{2,1,0:T(8,128)} %copy-done.63), channel_id=1, source_target_pairs={{0,2},{2,0},{4,6},{6,4},{1,3},{3,1},{5,7},{7,5},{8,10},{10,8},{12,... | collective-permute-start | bytes 98312 | tf_op jit(solution)/shard_map/ppermute | solution.py:435
  136.1 6.0 %collective-permute-start.18 = (f32[2,16,256]{2,1,0:T(8,128)}, f32[2,16,256]{2,1,0:T(8,128)S(1)}, u32[]{:S(2)}, u32[]{:S(2)}) collective-permute-start(f32[2,16,256]{2,1,0:T(8,128)} %copy-done.61), channel_id=1, source_target_pairs={{0,6},{2,4},{4,2},{6,0},{1,7},{3,5},{5,3},{7,1},{8,14},{10,12},{12... | collective-permute-start | bytes 98312 | tf_op jit(solution)/shard_map/ppermute | solution.py:438
  138.4 1.2 collective-permute-start.19
  142.7 3.7 %copy-start.3 = (bf16[1,1,2,6,6,256,256]{6,5,4,3,2,1,0:T(8,128)(2,1)S(1)}, bf16[1,1,2,6,6,256,256]{6,5,4,3,2,1,0:T(8,128)(2,1)}, u32[]{:S(2)}) copy-start(bf16[1,1,2,6,6,256,256]{6,5,4,3,2,1,0:T(8,128)(2,1)} %param.8) | copy-start | bytes 28311556
  146.4 1.6 copy-start.8
  148.0 0.9 copy-start.11
  148.9 0.9 copy-start.13
  149.8 0.8 copy-start.44
  150.6 0.8 copy-start.48
  151.4 0.8 copy-start.52
  152.1 0.8 copy-start.56
  168.2 14.4 %all-to-all-start.4 = ((f32[32,16,128]{2,1,0:T(8,128)}), f32[32,16,128]{2,1,0:T(8,128)S(1)}, u32[]{:S(2)}, u32[]{:S(2)}) async-start(f32[32,16,128]{2,1,0:T(8,128)} %get-tuple-element.117), calls=%async_computation.4 | async-start | bytes 524288 | tf_op jit(solution)/shard_map/all_to_all | solution.py:446
  171.8 8.3 %collective-permute-start.20 = (f32[2,16,256]{2,1,0:T(8,128)}, f32[2,16,256]{2,1,0:T(8,128)S(1)}, u32[]{:S(2)}, u32[]{:S(2)}) collective-permute-start(f32[2,16,256]{2,1,0:T(8,128)} %copy-done.66), channel_id=1, source_target_pairs={{0,8},{8,0},{16,24},{24,16},{1,9},{9,1},{17,25},{25,17},{2,10},{10... | collective-permute-start | bytes 98312 | tf_op jit(solution)/shard_map/ppermute | solution.py:435
  173.6 6.5 %collective-permute-start.21 = (f32[2,16,256]{2,1,0:T(8,128)}, f32[2,16,256]{2,1,0:T(8,128)S(1)}, u32[]{:S(2)}, u32[]{:S(2)}) collective-permute-start(f32[2,16,256]{2,1,0:T(8,128)} %copy-done.64), channel_id=1, source_target_pairs={{0,24},{8,16},{16,8},{24,0},{1,25},{9,17},{17,9},{25,1},{2,26},{10... | collective-permute-start | bytes 98312 | tf_op jit(solution)/shard_map/ppermute | solution.py:438
  175.1 5.0 %collective-permute-start.22 = (f32[2,16,256]{2,1,0:T(8,128)}, f32[2,16,256]{2,1,0:T(8,128)S(1)}, u32[]{:S(2)}, u32[]{:S(2)}) collective-permute-start(f32[2,16,256]{2,1,0:T(8,128)} %copy-done.62), channel_id=1, source_target_pairs={{0,2},{2,0},{4,6},{6,4},{1,3},{3,1},{5,7},{7,5},{8,10},{10,8},{12,... | collective-permute-start | bytes 98312 | tf_op jit(solution)/shard_map/ppermute | solution.py:435
  176.5 6.0 %collective-permute-start.23 = (f32[2,16,256]{2,1,0:T(8,128)}, f32[2,16,256]{2,1,0:T(8,128)S(1)}, u32[]{:S(2)}, u32[]{:S(2)}) collective-permute-start(f32[2,16,256]{2,1,0:T(8,128)} %copy-done.60), channel_id=1, source_target_pairs={{0,6},{2,4},{4,2},{6,0},{1,7},{3,5},{5,3},{7,1},{8,14},{10,12},{12... | collective-permute-start | bytes 98312 | tf_op jit(solution)/shard_map/ppermute | solution.py:438
  178.9 1.2 collective-permute-start.24
  182.6 0.9 copy-start.27
  183.5 0.9 copy-start.29
  184.4 0.9 copy-start.31
  185.4 0.9 copy-start.33
  186.3 0.9 copy-start.35
  187.2 0.9 copy-start.37
  188.1 0.9 copy-start.41
  (35 other events, 22.7 us)

commit v2 on v1

--- a/solution.py
+++ b/solution.py
@@ -2,7 +2,6 @@
 
 import jax
 import jax.numpy as jnp
-import numpy as np
 from jax import lax
 from jax.experimental import pallas as pl
 from jax.experimental.pallas import tpu as pltpu
@@ -13,7 +12,7 @@
 LANES = 128
 SLOT = 8
 SLOTS = 12
-RHO, FF, FD = SLOTS * SLOT, SLOTS * SLOT + 1, SLOTS * SLOT + 2
+SCALARS = 3
 NT = (((1,), (1,)), ((), ()))
 NN = (((1,), (0,)), ((), ()))
 f32 = jnp.float32
@@ -22,6 +21,17 @@
 
 def own_slot(s):
     return s
+
+
+COLUMN_OF_FACE = {0: 2, 3: 1, 1: 4, 4: 3}
+
+
+def whole_lanes(nc):
+    return -(-(nc + SCALARS) // 256) * 256
+
+
+def column_lanes(levels):
+    return -(-(30 * levels + SCALARS) // LANES) * LANES
 
 
 def nbr_slot(s, f):
@@ -36,23 +46,6 @@
     if f == 2:
         return 1 if s == 0 else 11
     return 10 if s == 0 else 0
-
-
-def slot_table(nx, ny, nz, nc):
-    table = np.full((nx * ny * nz, LANES), -1, np.int32)
-    sz = 2 * nz
-    for x in range(nx):
-        for y in range(ny):
-            for z in range(nz):
-                where = [(x, y, 2 * z), (x, y, 2 * z + 1)]
-                where += [(x - 1, y, 2 * z), (x - 1, y, 2 * z + 1), (x + 1, y, 2 * z), (x + 1, y, 2 * z + 1)]
-                where += [(x, y - 1, 2 * z), (x, y - 1, 2 * z + 1), (x, y + 1, 2 * z), (x, y + 1, 2 * z + 1)]
-                where += [(x, y, 2 * z - 1), (x, y, 2 * z + 2)]
-                for slot, (a, b, c) in enumerate(where):
-                    if 0 <= a < nx and 0 <= b < ny and 0 <= c < sz:
-                        first = ((a * ny + b) * sz + c) * 6
-                        table[(x * ny + y) * nz + z, slot * SLOT : slot * SLOT + 6] = first + np.arange(6)
-    return table
 
 
 def split2(x):
@@ -136,10 +129,13 @@
             out[base + 16 * k : base + 16 * k + 16, :] = slab
 
 
-def setup_kernel(rhs, modes, fmap, coarse, table, xa, xb, ya, yb, za, zb, perm, lift, start, solve, send, work, rows):
+def setup_kernel(sizes, rhs, modes, fmap, coarse, xa, xb, ya, yb, za, zb, perm, lift, sums, start, solve, place, part, work, rows):
     parity, _ = position((1, 1, 1))
-    slabs = -(-coarse.shape[1] // 256)
-    devices = table.shape[0]
+    nc = coarse.shape[1]
+    slabs = -(-nc // 256)
+    levels = 2 * sizes[2]
+    lanes = column_lanes(levels)
+    gx, gy, gz = (lax.axis_index(a) for a in AXES)
     lane_row = lax.broadcasted_iota(jnp.int32, (256, 256), 0)
 
     plus, minus = [], []
@@ -155,7 +151,9 @@
         return -fold3(mm(split3(values), table_rows, NT))
 
     zero2 = jnp.zeros((2, 256), f32)
-    partial = [jnp.zeros((48, 256), f32) for _ in range(2)]
+    partial = jnp.zeros((48, lanes), f32)
+    lane_column = lax.broadcasted_iota(jnp.int32, (lanes, 16), 0)
+    source_row = lax.broadcasted_iota(jnp.int32, (lanes, 16), 1)
     up_perm = {}
     for s in range(2):
         for d in range(3):
@@ -196,9 +194,23 @@
             work[own_slot(s) * SLOT : own_slot(s) * SLOT + 8, :] = jnp.concatenate([own, zero2], 0)
             n = nbr_slot(s, f)
             work[n * SLOT : n * SLOT + 8, :] = jnp.concatenate([other, zero2], 0)
-            both = split2(work[...])
-            lift[s * 6 + f] = both
-            partial[s] += mm(split3(value), both, NT)
+            lift[s * 6 + f] = split2(work[...])
+            pair = split2(jnp.concatenate([own, zero2, other, zero2], 0))
+            level = 2 * gz + s
+            if d == 2:
+                target = (level + (1 if f == 2 else -1)) * 6
+            else:
+                target = COLUMN_OF_FACE[f] * 6 * levels + level * 6
+            mode = jnp.bitwise_and(source_row, 7)
+            aim = jnp.where(source_row < 8, level * 6, target) + mode
+            choose = (lane_column == aim) & (mode < 6)
+            both = choose.astype(bf16)
+            alone = (choose & (source_row < 8)).astype(bf16)
+            left = split3(value)
+            for h in range(2):
+                half = pair[16 * h : 16 * h + 16]
+                sums[s * 6 + f, h * lanes : h * lanes + lanes, :] = mm(both, half, NN).astype(bf16)
+                partial += mm(left, mm(alone, half, NN).astype(bf16), NT)
 
     rows[...] = jnp.zeros(rows.shape, f32)
     pieces = [(2, minus[0], 48, 16), (4, plus[0], 48, 16), (6, minus[1], 48, 16), (8, plus[1], 48, 16)]
@@ -214,59 +226,55 @@
             rows[slot * SLOT : slot * SLOT + count, 256 * k : 256 * k + 256] = source[
                 base + 16 * k : base + 16 * k + count, :
             ]
-    both = split2(rows[...])
-    index_row = lax.broadcasted_iota(jnp.int32, (256 * slabs, LANES), 0)
-    line = lax.broadcasted_iota(jnp.int32, (LANES, LANES), 0)
-    column = lax.broadcasted_iota(jnp.int32, (LANES, LANES), 1)
-    passing = ((line == column) & (line >= RHO) & (line <= FD)).astype(f32)
-    total = [fold3(part) for part in partial]
-    total = [part[:, :LANES] + part[:, LANES:] for part in total]
-    lane = lax.broadcasted_iota(jnp.int32, total[0].shape, 1)
-    total = jnp.where(lane < SLOT, total[0], jnp.where(lane < 2 * SLOT, total[1], 0.0))
-
-    def build(q2, carry):
-        halves = []
-        for q in range(2):
-            choose = (index_row == table[2 * q2 + q]).astype(bf16)
-            got = mm(both, choose, NN)
-            halves.append(jnp.concatenate([got[:LANES] + passing, got[LANES:]], 0))
-        solve[q2] = jnp.concatenate(halves, 1).astype(bf16)
-        return carry
-
-    lax.fori_loop(0, devices // 2, build, 0)
-    spread_out(total, solve, send)
-
-
-def spread_out(part, solve, send):
-    left = split3(part)
-    left = jnp.concatenate([left, left], 1)
-    pairs = solve.shape[0]
-
-    def one(q2):
-        got = fold3(mm(left, solve[q2], NN))
-        send[2 * q2] = got[:, :LANES]
-        send[2 * q2 + 1] = got[:, LANES:]
-
-    if pairs <= 16:
-        for q2 in range(pairs):
-            one(q2)
-    else:
-
-        def step(q2, carry):
-            one(q2)
-            return carry
-
-        lax.fori_loop(0, pairs, step, 0)
-
-
-def gather_sum(recv):
-    devices = recv.shape[0]
-    if devices <= 32:
-        parts = [recv[q] for q in range(devices)]
-        while len(parts) > 1:
-            parts = [parts[i] + parts[i + 1] for i in range(0, len(parts), 2)]
-        return parts[0]
-    return lax.fori_loop(0, devices, lambda q, acc: acc + recv[q], jnp.zeros(recv.shape[1:], f32))
+    solve[...] = split2(rows[...])
+    line = lax.broadcasted_iota(jnp.int32, (lanes, 1), 0)
+    whole = lax.broadcasted_iota(jnp.int32, (lanes, place.shape[1]), 1)
+    for k in range(sizes[1]):
+        y = jnp.bitwise_xor(gy, k)
+        aim = jnp.where(line >= 30 * levels, nc + line - 30 * levels, -1)
+        for t, (dx, dy) in enumerate(((0, 0), (-1, 0), (1, 0), (0, -1), (0, 1))):
+            inside = (gx + dx >= 0) & (gx + dx < sizes[0]) & (y + dy >= 0) & (y + dy < sizes[1])
+            first = jnp.where(inside, ((gx + dx) * sizes[1] + y + dy - t) * 6 * levels, -6 * nc)
+            aim = jnp.where((line >= t * 6 * levels) & (line < (t + 1) * 6 * levels), line + first, aim)
+        place[k * lanes : k * lanes + lanes, :] = (whole == aim).astype(bf16)
+    part[...] = fold3(partial)
+
+
+def tail(ref, lanes):
+    return ref[:, ref.shape[1] - lanes :]
+
+
+def beside(outs, faces, values):
+    if faces:
+        for out, face in zip(outs, faces):
+            width = face.shape[1]
+            out[:, :width] = face[...]
+            out[:, width:] = values
+    outs[-1][...] = values
+
+
+def column_kernel(count, *refs):
+    lanes = refs[0].shape[1]
+    total = refs[0][...]
+    for part in refs[1:count]:
+        total += tail(part, lanes)
+    split = count + (len(refs) - count) // 2
+    beside(refs[split:], refs[count:split], total)
+
+
+def place_kernel(count, place, *refs):
+    lanes = refs[0].shape[1]
+    left = jnp.concatenate([split3(tail(part, lanes)) for part in refs[:count]], 1)
+    split = count + (len(refs) - count) // 2
+    beside(refs[split:], refs[count:split], fold3(mm(left, place[...], NN)))
+
+
+def coarse(whole, parts, solve):
+    total = whole[...]
+    for part in parts:
+        total += tail(part, whole.shape[1])
+    got = fold3(mm(split3(total[:, : solve.shape[1]]), solve[...], NT))
+    return total, got[:, :LANES] + got[:, LANES:]
 
 
 def lift_left(total):
@@ -274,9 +282,10 @@
     return jnp.concatenate([left, left], 1)
 
 
-def apply_factors(residual, pattern, factors, perm, lift, masks, parity, previous, forward, image, solve, sends):
-    xa, xb, ya, yb, za, zb, send = sends
-    partial = jnp.zeros((48, 256), f32)
+def apply_factors(residual, pattern, factors, perm, sums, masks, parity, previous, forward, image, sends):
+    xa, xb, ya, yb, za, zb, part = sends
+    lanes = part.shape[1]
+    partial = jnp.zeros((48, 2 * lanes), f32)
     own_sum = jnp.zeros((16, 256), f32)
     square = jnp.zeros((16, 256), f32)
     cross = jnp.zeros((16, 256), f32)
@@ -312,53 +321,56 @@
             got = masked(got, masks[s][j])
             image[s, j] = got
             faces[s, j] = got
-            partial += mm(split3(got), lift[s * 6 + j], NT)
-    for s in range(2):
-        xa[s] = pick(parity[0], faces[s, 3], faces[s, 0])
-        xb[s] = pick(parity[0], faces[s, 0], faces[s, 3])
-        ya[s] = pick(parity[1], faces[s, 4], faces[s, 1])
-        yb[s] = pick(parity[1], faces[s, 1], faces[s, 4])
-    za[...] = pick(parity[2], faces[0, 5], faces[1, 2])
-    zb[...] = pick(parity[2], faces[1, 2], faces[0, 5])
+            partial += mm(split3(got), sums[s * 6 + j], NT)
+    for s in range(2):
+        at = slice(256 * s, 256 * s + 256)
+        xa[:, at] = pick(parity[0], faces[s, 3], faces[s, 0])
+        xb[:, at] = pick(parity[0], faces[s, 0], faces[s, 3])
+        ya[:, at] = pick(parity[1], faces[s, 4], faces[s, 1])
+        yb[:, at] = pick(parity[1], faces[s, 1], faces[s, 4])
     total = fold3(partial)
-    total = total[:, :LANES] + total[:, LANES:]
+    total = total[:, :lanes] + total[:, lanes:]
     lane = lax.broadcasted_iota(jnp.int32, total.shape, 1)
-    for where, values in ((RHO, own_sum), (FF, square), (FD, cross)):
-        total = jnp.where(lane == where, jnp.sum(values, axis=1, keepdims=True), total)
-    spread_out(total, solve, send)
-
-
-def first_kernel(sizes, pattern, recv, start, factors, perm, lift, solve, residual, forward, image, *sends):
+    scalars = 30 * 2 * lax.axis_size("gz")
+    for k, values in enumerate((own_sum, square, cross)):
+        total = jnp.where(lane == scalars + k, jnp.sum(values, axis=1, keepdims=True), total)
+    part[...] = total
+    for out, face in ((za, pick(parity[2], faces[0, 5], faces[1, 2])), (zb, pick(parity[2], faces[1, 2], faces[0, 5]))):
+        out[:, :256] = face
+        out[:, 256:] = total
+
+
+def first_kernel(sizes, count, pattern, factors, perm, lift, sums, solve, start, *refs):
     parity, masks = position(sizes)
-    left = lift_left(gather_sum(recv))
+    residual, forward, image = refs[count : count + 3]
+    left = lift_left(coarse(refs[0], refs[1:count], solve)[1])
     now = [[None] * 6 for _ in range(2)]
     for s in range(2):
         for f in range(6):
             value = start[s, f] - masked(fold3(mm(left, lift[s * 6 + f], NN)), masks[s][f])
             residual[s, f] = value
             now[s][f] = value
-    apply_factors(now, pattern, factors, perm, lift, masks, parity, None, forward, image, solve, sends)
-
-
-def update(sizes, first, recvs, state, count):
+    apply_factors(now, pattern, factors, perm, sums, masks, parity, None, forward, image, refs[count + 3 :])
+
+
+def update(sizes, nc, first, faces, parts, state, count):
     parity, masks = position(sizes)
-    xa, xb, ya, yb, za, zb, recv = recvs
-    residual, forward, image, lift, old = state
-    total = gather_sum(recv)
-    left = lift_left(total)
+    residual, forward, image, lift, solve, old = state
+    total, solution_part = coarse(parts[0], parts[1:], solve)
+    left = lift_left(solution_part)
     sums = jnp.sum(total, axis=0, keepdims=True)
     lane = lax.broadcasted_iota(jnp.int32, sums.shape, 1)
 
-    def scalar(at):
-        return jnp.sum(jnp.where(lane == at, sums, 0.0), axis=1, keepdims=True)
-
-    rho, curvature = scalar(RHO), scalar(FF)
+    def scalar(k):
+        return jnp.sum(jnp.where(lane == nc + k, sums, 0.0), axis=1, keepdims=True)
+
+    rho, curvature = scalar(0), scalar(1)
     if first:
         beta = None
     else:
         direction, moved, along, multipliers, scalars = old
         beta = rho / scalars[0:1, 0:1]
-        curvature = curvature + 2.0 * beta * scalar(FD) + beta * beta * scalars[1:2, 0:1]
+        curvature = curvature + 2.0 * beta * scalar(2) + beta * beta * scalars[1:2, 0:1]
     step = rho / curvature
     out = {}
     for s in range(2):
@@ -367,9 +379,8 @@
             if d == 2 and (s == 0) == (f == 2):
                 other = image[1 - s, 5 if f == 2 else 2]
             else:
-                a, b = ((xa, xb), (ya, yb), (za, zb))[d]
-                va = a[s] if d < 2 else a[...]
-                vb = b[s] if d < 2 else b[...]
+                at = 256 * s if d < 2 else 0
+                va, vb = (face[:, at : at + 256] for face in faces[2 * d : 2 * d + 2])
                 other = pick(parity[d], vb, va) if f < 3 else pick(parity[d], va, vb)
             change = image[s, f] + other - fold3(mm(left, lift[s * 6 + f], NN))
             change = masked(change, masks[s][f])
@@ -385,19 +396,18 @@
     return parity, masks, beta, rho, curvature, out
 
 
-def middle_kernel(sizes, first, *refs):
-    pattern, factors, perm, lift, solve = refs[:5]
-    recvs = refs[5:12]
-    residual, forward, image = refs[12:15]
-    rest = refs[15:]
+def middle_kernel(sizes, nc, first, count, *refs):
+    pattern, factors, perm, lift, sums, solve = refs[:6]
+    faces, parts = refs[6:12], refs[12 : 12 + count]
+    residual, forward, image = refs[12 + count : 15 + count]
+    rest = refs[15 + count :]
     if first:
         old = None
     else:
         old, rest = rest[:5], rest[5:]
     new_residual, new_forward, new_image, new_direction, new_moved, new_along, new_multipliers, new_scalars = rest[:8]
-    sends = rest[8:]
     parity, masks, beta, rho, curvature, out = update(
-        sizes, first, recvs, (residual, forward, image, lift, old), 6
+        sizes, nc, first, faces, parts, (residual, forward, image, lift, solve, old), 6
     )
     row = lax.broadcasted_iota(jnp.int32, (8, LANES), 0)
     new_scalars[...] = jnp.where(row == 0, rho, curvature)
@@ -415,44 +425,40 @@
             line = forward[s, f] if first else forward[s, f] + beta * old[2][s, f]
             along[s][f] = line
             new_along[s, f] = line
-    apply_factors(now, pattern, factors, perm, lift, masks, parity, along, new_forward, new_image, solve, sends)
-
-
-def last_kernel(sizes, lift, *refs):
-    recvs = refs[:7]
-    residual, forward, image = refs[7:10]
-    old = refs[10:15]
-    multipliers, final = refs[15:]
-    out = update(sizes, False, recvs, (residual, forward, image, lift, old), 3)[5]
+    apply_factors(now, pattern, factors, perm, sums, masks, parity, along, new_forward, new_image, rest[8:])
+
+
+def last_kernel(sizes, nc, count, lift, solve, *refs):
+    faces, parts = refs[:6], refs[6 : 6 + count]
+    residual, forward, image = refs[6 + count : 9 + count]
+    old = refs[9 + count : 14 + count]
+    multipliers, final = refs[14 + count :]
+    out = update(sizes, nc, False, faces, parts, (residual, forward, image, lift, solve, old), 3)[5]
     for s in range(2):
         for f in range(3):
             final[s, f] = out[s, f][0]
             multipliers[s, f] = out[s, f][3]
 
 
-def exchange(values, axis):
+def swap(values, axis, distance):
+    return lax.ppermute(values, axis, [(i, i ^ distance) for i in range(lax.axis_size(axis))])
+
+
+def exchange(first, second, axis, alone=None):
     size = lax.axis_size(axis)
-    first = lax.ppermute(values[0], axis, [(i, i ^ 1) for i in range(size)])
+    below = swap(first, axis, 1)
     if size == 2:
-        return first, first
-    second = lax.ppermute(
-        values[1], axis, [(i, (i + 1) % size if i % 2 else (i - 1) % size) for i in range(size)]
-    )
-    return first, second
-
-
-def communicate(sends):
-    xa, xb, ya, yb, za, zb, send = sends
-    recv = lax.all_to_all(send, AXES, 0, 0, tiled=True)
-    za, zb = exchange((za, zb), "gz")
-    xa, xb = exchange((xa, xb), "gx")
-    ya, yb = exchange((ya, yb), "gy")
-    return xa, xb, ya, yb, za, zb, recv
+        return below, below, [below]
+    above = lax.ppermute(second, axis, [(i, (i + 1) % size if i % 2 else (i - 1) % size) for i in range(size)])
+    others = [below]
+    if alone is not None:
+        for distance in range(2, size):
+            others.append(above if size == 4 and distance == 3 else swap(alone, axis, distance))
+    return below, above, others
 
 
 def per_device(dual_rhs, factors, block_pattern, face_map, rigid_modes, coarse_solve):
     sizes = tuple(lax.axis_size(a) for a in AXES)
-    devices = sizes[0] * sizes[1] * sizes[2]
     cases, dofs = dual_rhs.shape[4:]
     nc = coarse_solve.shape[1]
     slabs = -(-nc // 256)
@@ -463,7 +469,8 @@
     modes = rigid_modes.reshape(rigid_modes.shape[2:])
     vmem = pl.BlockSpec(memory_space=pltpu.VMEM)
     smem = pl.BlockSpec(memory_space=pltpu.SMEM)
-    params = pltpu.CompilerParams(vmem_limit_bytes=24 << 20)
+    table_bytes = 2 * sizes[1] * column_lanes(2 * sizes[2]) * whole_lanes(nc)
+    params = pltpu.CompilerParams(vmem_limit_bytes=(16 << 20) + table_bytes)
 
     def shape(*dims, dtype=f32):
         return jax.ShapeDtypeStruct(dims, dtype)
@@ -479,51 +486,67 @@
             compiler_params=params,
         )(*ins)
 
+    levels = 2 * sizes[2]
+    lanes, whole = column_lanes(levels), whole_lanes(nc)
     packs = [shape(48 + 16 * slabs, dofs)] * 4 + [shape(24 + 16 * slabs, dofs)] * 2
     xa, xb, ya, yb, za, zb = call(pack_kernel, packs, [rhs, modes, fmap, coarse_solve])
-    za, zb = exchange((za, zb), "gz")
-    xa, xb = exchange((xa, xb), "gx")
-    ya, yb = exchange((ya, yb), "gy")
-
-    table = jnp.asarray(slot_table(*sizes, nc)).reshape(devices, 1, LANES)
+    za, zb, _ = exchange(za, zb, "gz")
+    xa, xb, _ = exchange(xa, xb, "gx")
+    ya, yb, _ = exchange(ya, yb, "gy")
     faces = shape(2, 6, cases, dofs)
-    sent = shape(devices, cases, LANES)
-    perm, lift, start, solve, send = call(
-        setup_kernel,
+    perm, lift, sums, start, solve, place, part = call(
+        functools.partial(setup_kernel, sizes),
         [
             shape(6, dofs, dofs, dtype=bf16),
             shape(12, 2 * LANES, dofs, dtype=bf16),
+            shape(12, 2 * lanes, dofs, dtype=bf16),
             faces,
-            shape(devices // 2, 2 * LANES, 2 * LANES, dtype=bf16),
-            sent,
+            shape(2 * LANES, 256 * slabs, dtype=bf16),
+            shape(sizes[1] * lanes, whole, dtype=bf16),
+            shape(cases, lanes),
         ],
-        [rhs, modes, fmap, coarse_solve, table, xa, xb, ya, yb, za, zb],
+        [rhs, modes, fmap, coarse_solve, xa, xb, ya, yb, za, zb],
         scratch=(pltpu.VMEM((LANES, dofs), f32), pltpu.VMEM((LANES, 256 * slabs), f32)),
     )
-    recv = lax.all_to_all(send, AXES, 0, 0, tiled=True)
-
-    sends = [shape(2, cases, dofs)] * 4 + [shape(cases, dofs)] * 2 + [sent]
+
+    def reduce(part, za, zb, along_y, along_x):
+        za, zb, others = exchange(za, zb, "gz", part)
+        outs = [shape(cases, face.shape[1] + lanes) for face in along_y] + [shape(cases, lanes)]
+        ins = [part, *others, *along_y]
+        *along_y, part = call(functools.partial(column_kernel, 1 + len(others)), outs, ins)
+        ya, yb, others = exchange(*(along_y or (part, part)), "gy", part)
+        outs = [shape(cases, face.shape[1] + whole) for face in along_x] + [shape(cases, whole)]
+        ins = [place, part, *others, *along_x]
+        *along_x, part = call(functools.partial(place_kernel, 1 + len(others)), outs, ins)
+        xa, xb, others = exchange(*(along_x or (part, part)), "gx", part)
+        return [xa, xb, ya, yb, za, zb], [part, *others]
+
+    parts = reduce(part, part, part, (), ())[1]
+    wide = shape(cases, 2 * dofs)
+    sends = [wide] * 4 + [shape(cases, dofs + lanes)] * 2 + [shape(cases, lanes)]
     residual, forward, image, *out = call(
-        functools.partial(first_kernel, sizes),
+        functools.partial(first_kernel, sizes, len(parts)),
         [faces, faces, faces] + sends,
-        [pattern, recv, start, factors, perm, lift, solve],
+        [pattern, factors, perm, lift, sums, solve, start, *parts],
         first_smem=True,
     )
     old = []
     for iteration in range(ITERS - 1):
-        got = communicate(out)
+        xa, xb, ya, yb, za, zb, part = out
+        got, parts = reduce(part, za, zb, (ya, yb), (xa, xb))
         residual, forward, image, *out = call(
-            functools.partial(middle_kernel, sizes, iteration == 0),
+            functools.partial(middle_kernel, sizes, nc, iteration == 0, len(parts)),
             [faces] * 6 + [shape(2, 3, cases, dofs), shape(8, LANES)] + sends,
-            [pattern, factors, perm, lift, solve, *got, residual, forward, image, *old],
+            [pattern, factors, perm, lift, sums, solve, *got, *parts, residual, forward, image, *old],
             first_smem=True,
         )
         old, out = out[:5], out[5:]
-    got = communicate(out)
+    xa, xb, ya, yb, za, zb, part = out
+    got, parts = reduce(part, za, zb, (ya, yb), (xa, xb))
     multipliers, final = call(
-        functools.partial(last_kernel, sizes),
+        functools.partial(last_kernel, sizes, nc, len(parts)),
         [shape(2, 3, cases, dofs)] * 2,
-        [lift, *got, residual, forward, image, *old],
+        [lift, solve, *got, *parts, residual, forward, image, *old],
     )
     return multipliers.reshape(dual_rhs.shape), final.reshape(dual_rhs.shape)
 

time: 192 us -> 133 us (0.69); the launches traced: 190 us -> 133 us
  local copies, waits for them, and re-layouts: 69.1 us -> 6.91 us
  waiting for transfers between devices: 24 us -> 42.4 us
  starting transfers between devices: 54.5 us -> 44.6 us
  Pallas kernels: 41.6 us -> 38.4 us
    unnamed x140 -> x12, local copies, waits for them, and re-layouts: 68.4 us -> 6.91 us
    ppermute x25 -> x40, waiting for transfers between devices: 14.3 us -> 42.4 us  [the longest x28 37.4 us: swap(): lax.ppermute(values, axis, [(i, i ^ distance) for i in range(lax.axis_siz...]
    all_to_all x5 -> x0, starting transfers between devices: 17.6 us -> none  [the longest x4 13.7 us: communicate(): recv = lax.all_to_all(send, AXES, 0, 0, tiled=True)]
    all_to_all x5 -> x0, waiting for transfers between devices: 9.7 us -> none  [the longest x1 9.69 us: per_device(): recv = lax.all_to_all(send, AXES, 0, 0, tiled=True)]
    ppermute x25 -> x40, starting transfers between devices: 36.9 us -> 44.6 us  [the longest x12 22.9 us: exchange(): lax.ppermute(second, axis, [(i, (i + 1) % size if i % 2 else (i - 1) % si...]
    pallas_call x7 -> x17, Pallas kernels: 41.6 us -> 38.4 us  [call(): pl.pallas_call(kernel, out_shape=outs, in_specs=specs, out_specs=[vmem] *...]
  transfers between devices with their start and end apart: 30 -> 40, of which waited for: 11 -> 20; matrix products, arithmetic and copies ran while one was open for 0% -> 0% of each run, Pallas kernels for 0% -> 0%
where the time goes in v2:
time: 133 us
  starting transfers between devices  44.6 us (34%)
  waiting for transfers between devices  42.4 us (32%)
  Pallas kernels  38.4 us (29%)
  local copies, waits for them, and re-layouts  6.91 us (5%)
    pallas_call x17, Pallas kernels, call(): pl.pallas_call(kernel, out_shape=outs, in_specs=specs, out_specs=[vmem] *...  38.4 us
    ppermute x28, waiting for transfers between devices, swap(): lax.ppermute(values, axis, [(i, i ^ distance) for i in range(lax.axis_siz...  37.4 us
    ppermute x12, starting transfers between devices, exchange(): lax.ppermute(second, axis, [(i, (i + 1) % size if i % 2 else (i - 1) % si...  22.9 us
    ppermute x28, starting transfers between devices, swap(): lax.ppermute(values, axis, [(i, i ^ distance) for i in range(lax.axis_siz...  21.7 us
    unnamed x12, local copies, waits for them, and re-layouts  6.91 us
    ppermute x12, waiting for transfers between devices, exchange(): lax.ppermute(second, axis, [(i, (i + 1) % size if i % 2 else (i - 1) % si...  4.91 us
  transfers between devices with their start and end apart: 40, of which 20 were waited for; matrix products, arithmetic and copies ran while one was open for 0% of the time, Pallas kernels for 0%

profile of v2, /device:TPU:0, one launch (start us, length us, event | category | flops | bytes accessed | tf_op | source)
XLA Modules:
  0.0 133.0 jit_solution(4920221234819173665)
XLA Ops:
  0.6 0.7 copy.17
  1.3 0.9 copy.16
  2.3 0.9 copy-done.2
  3.1 0.7 copy-done.3
  3.9 0.7 shard_map.77
  4.5 2.9 %collective-permute-start = (f32[80,256]{1,0:T(8,128)S(1)}, f32[80,256]{1,0:T(8,128)S(1)}, u32[]{:S(2)}, u32[]{:S(2)}) collective-permute-start(f32[80,256]{1,0:T(8,128)S(1)} %get-tuple-element.91), channel_id=1, source_target_pairs={{0,8},{8,0},{16,24},{24,16},{1,9},{9,1},{17,25},{25,17},{2,10},{10... | collective-permute-start | bytes 245768 | tf_op jit(solution)/shard_map/ppermute | solution.py:444
  7.5 1.5 %collective-permute-start.1 = (f32[80,256]{1,0:T(8,128)S(1)}, f32[80,256]{1,0:T(8,128)S(1)}, u32[]{:S(2)}, u32[]{:S(2)}) collective-permute-start(f32[80,256]{1,0:T(8,128)S(1)} %get-tuple-element.92), channel_id=1, source_target_pairs={{0,24},{8,16},{16,8},{24,0},{1,25},{9,17},{17,9},{25,1},{2,26},{10... | collective-permute-start | bytes 245768 | tf_op jit(solution)/shard_map/ppermute | solution.py:452
  9.0 1.6 %collective-permute-start.2 = (f32[80,256]{1,0:T(8,128)S(1)}, f32[80,256]{1,0:T(8,128)S(1)}, u32[]{:S(2)}, u32[]{:S(2)}) collective-permute-start(f32[80,256]{1,0:T(8,128)S(1)} %get-tuple-element.93), channel_id=1, source_target_pairs={{0,2},{2,0},{4,6},{6,4},{1,3},{3,1},{5,7},{7,5},{8,10},{10,8},{12,... | collective-permute-start | bytes 245768 | tf_op jit(solution)/shard_map/ppermute | solution.py:444
  10.5 2.5 %collective-permute-start.3 = (f32[80,256]{1,0:T(8,128)S(1)}, f32[80,256]{1,0:T(8,128)S(1)}, u32[]{:S(2)}, u32[]{:S(2)}) collective-permute-start(f32[80,256]{1,0:T(8,128)S(1)} %get-tuple-element.94), channel_id=1, source_target_pairs={{0,6},{2,4},{4,2},{6,0},{1,7},{3,5},{5,3},{7,1},{8,14},{10,12},{12... | collective-permute-start | bytes 245768 | tf_op jit(solution)/shard_map/ppermute | solution.py:452
  13.0 1.2 collective-permute-done.4.za.zb
  14.3 2.5 %collective-permute-done.3.yb = f32[80,256]{1,0:T(8,128)S(1)} collective-permute-done((f32[80,256]{1,0:T(8,128)S(1)}, f32[80,256]{1,0:T(8,128)S(1)}, u32[]{:S(2)}, u32[]{:S(2)}) %collective-permute-start.3) | collective-permute-done | bytes 81952 | tf_op jit(solution)/shard_map/ppermute | solution.py:452
  16.8 4.1 %shard_map.78 = (bf16[6,256,256]{2,1,0:T(8,128)(2,1)S(1)}, bf16[12,256,256]{2,1,0:T(8,128)(2,1)S(1)}, bf16[12,256,256]{2,1,0:T(8,128)(2,1)S(1)}, f32[2,6,16,256]...) custom-call(f32[2,3,16,256]{3,2,1,0:T(8,128)S(1)} %bitcast.18, ...), custom_call_target="tpu_custom_call" | custom-call | tf_op jit(solution)/shard_map/pallas_call | solution.py:480
  20.8 1.2 collective-permute-done.5.refs_1_
  22.0 2.6 %collective-permute-start.8 = (f32[16,128]{1,0:T(8,128)S(1)}, f32[16,128]{1,0:T(8,128)S(1)}, u32[]{:S(2)}, u32[]{:S(2)}) collective-permute-start(f32[16,128]{1,0:T(8,128)S(1)} %shard_map.79.refs_0_), channel_id=1, source_target_pairs={{0,6},{2,4},{4,2},{6,0},{1,7},{3,5},{5,3},{7,1},{8,14},{10,12},{12... | collective-permute-start | bytes 24584 | tf_op jit(solution)/shard_map/ppermute | solution.py:452
  24.6 1.8 %collective-permute-start.6 = (f32[16,128]{1,0:T(8,128)S(1)}, f32[16,128]{1,0:T(8,128)S(1)}, u32[]{:S(2)}, u32[]{:S(2)}) collective-permute-start(f32[16,128]{1,0:T(8,128)S(1)} %shard_map.79.refs_0_), channel_id=1, source_target_pairs={{0,2},{2,0},{4,6},{6,4},{1,3},{3,1},{5,7},{7,5},{8,10},{10,8},{12,... | collective-permute-start | bytes 24584 | tf_op jit(solution)/shard_map/ppermute | solution.py:444
  26.4 1.1 collective-permute-done.8.refs_3_
  27.5 1.7 %collective-permute-done.7.refs_2_ = f32[16,128]{1,0:T(8,128)S(1)} collective-permute-done((f32[16,128]{1,0:T(8,128)S(1)}, f32[16,128]{1,0:T(8,128)S(1)}, u32[]{:S(2)}, u32[]{:S(2)}) %collective-permute-start.7) | collective-permute-done | bytes 8224 | tf_op jit(solution)/shard_map/ppermute | solution.py:444
  29.3 1.5 %collective-permute-start.11 = (f32[16,512]{1,0:T(8,128)S(1)}, f32[16,512]{1,0:T(8,128)S(1)}, u32[]{:S(2)}, u32[]{:S(2)}) collective-permute-start(f32[16,512]{1,0:T(8,128)S(1)} %shard_map.80.refs_0_), channel_id=1, source_target_pairs={{0,24},{8,16},{16,8},{24,0},{1,25},{9,17},{17,9},{25,1},{2,26},{10... | collective-permute-start | bytes 98312 | tf_op jit(solution)/shard_map/ppermute | solution.py:452
  30.8 1.5 %collective-permute-start.10 = (f32[16,512]{1,0:T(8,128)S(1)}, f32[16,512]{1,0:T(8,128)S(1)}, u32[]{:S(2)}, u32[]{:S(2)}) collective-permute-start(f32[16,512]{1,0:T(8,128)S(1)} %shard_map.80.refs_0_), channel_id=1, source_target_pairs={{0,16},{8,24},{16,0},{24,8},{1,17},{9,25},{17,1},{25,9},{2,18},{10... | collective-permute-start | bytes 98312 | tf_op jit(solution)/shard_map/ppermute | solution.py:444
  32.3 0.5 collective-permute-start.9
  32.9 1.3 collective-permute-done.11.refs_3_
  34.2 0.5 collective-permute-done.10.refs_2_
  34.7 1.5 %collective-permute-done.9.refs_1_ = f32[16,512]{1,0:T(8,128)S(1)} collective-permute-done((f32[16,512]{1,0:T(8,128)S(1)}, f32[16,512]{1,0:T(8,128)S(1)}, u32[]{:S(2)}, u32[]{:S(2)}) %collective-permute-start.9) | collective-permute-done | bytes 32800 | tf_op jit(solution)/shard_map/ppermute | solution.py:444
  36.2 3.7 %copy-done = bf16[1,1,2,6,6,256,256]{6,5,4,3,2,1,0:T(8,128)(2,1)S(1)} copy-done((bf16[1,1,2,6,6,256,256]{6,5,4,3,2,1,0:T(8,128)(2,1)S(1)}, bf16[1,1,2,6,6,256,256]{6,5,4,3,2,1,0:T(8,128)(2,1)}, u32[]{:S(2)}) %copy-start) | copy-done | bytes 9437208
  39.9 7.8 %shard_map.81 = (f32[2,6,16,256]{3,2,1,0:T(8,128)S(1)}, f32[2,6,16,256]{3,2,1,0:T(8,128)S(1)}, f32[2,6,16,256]{3,2,1,0:T(8,128)S(1)}, f32[16,512]{1,0:T(8,128)S(...) custom-call(s32[2,6,6]{2,1,0:T(8,128)S(1)} %copy.13.pattern.refs_0_,, ...), custom_call_target="tpu_custom_call" | custom-call | tf_op jit(solution)/shard_map/pallas_call | solution.py:480
  47.7 1.2 collective-permute-done.12.refs_1_.refs_10_.refs_11_
  48.9 1.0 collective-permute-start.13
  49.9 2.6 %collective-permute-start.15 = (f32[16,640]{1,0:T(8,128)S(1)}, f32[16,640]{1,0:T(8,128)S(1)}, u32[]{:S(2)}, u32[]{:S(2)}) collective-permute-start(f32[16,640]{1,0:T(8,128)S(1)} %get-tuple-element.109), channel_id=1, source_target_pairs={{0,6},{2,4},{4,2},{6,0},{1,7},{3,5},{5,3},{7,1},{8,14},{10,12},{12... | collective-permute-start | bytes 122888 | tf_op jit(solution)/shard_map/ppermute | solution.py:452
  52.4 4.5 %collective-permute-done.14.refs_2_ = f32[16,128]{1,0:T(8,128)S(1)} collective-permute-done((f32[16,128]{1,0:T(8,128)S(1)}, f32[16,128]{1,0:T(8,128)S(1)}, u32[]{:S(2)}, u32[]{:S(2)}) %collective-permute-start.14) | collective-permute-done | bytes 8224 | tf_op jit(solution)/shard_map/ppermute | solution.py:444
  57.2 0.6 collective-permute-start.16
  57.7 1.4 %collective-permute-start.17 = (f32[16,1024]{1,0:T(8,128)S(1)}, f32[16,1024]{1,0:T(8,128)S(1)}, u32[]{:S(2)}, u32[]{:S(2)}) collective-permute-start(f32[16,1024]{1,0:T(8,128)S(1)} %get-tuple-element.113), channel_id=1, source_target_pairs={{0,24},{8,16},{16,8},{24,0},{1,25},{9,17},{17,9},{25,1},{2,26},{10... | collective-permute-start | bytes 196616 | tf_op jit(solution)/shard_map/ppermute | solution.py:452
  59.2 1.5 %collective-permute-start.18 = (f32[16,512]{1,0:T(8,128)S(1)}, f32[16,512]{1,0:T(8,128)S(1)}, u32[]{:S(2)}, u32[]{:S(2)}) collective-permute-start(f32[16,512]{1,0:T(8,128)S(1)} %get-tuple-element.114.refs_12_), channel_id=1, source_target_pairs={{0,16},{8,24},{16,0},{24,8},{1,17},{9,25},{17,1},{25,9},{2,18},{10... | collective-permute-start | bytes 98312 | tf_op jit(solution)/shard_map/ppermute | solution.py:444
  60.7 2.6 %collective-permute-done.18.refs_14_ = f32[16,512]{1,0:T(8,128)S(1)} collective-permute-done((f32[16,512]{1,0:T(8,128)S(1)}, f32[16,512]{1,0:T(8,128)S(1)}, u32[]{:S(2)}, u32[]{:S(2)}) %collective-permute-start.18) | collective-permute-done | bytes 32800 | tf_op jit(solution)/shard_map/ppermute | solution.py:444
  63.3 7.9 %shard_map.84 = (f32[2,6,16,256]{3,2,1,0:T(8,128)S(1)}, f32[2,6,16,256]{3,2,1,0:T(8,128)S(1)}, f32[2,6,16,256]{3,2,1,0:T(8,128)S(1)}, f32[2,6,16,256]{3,2,1,0:T(...) custom-call(s32[2,6,6]{2,1,0:T(8,128)S(1)} %copy.13.pattern.refs_0_,, ...), custom_call_target="tpu_custom_call" | custom-call | tf_op jit(solution)/shard_map/pallas_call | solution.py:480
  71.1 1.2 collective-permute-done.19.refs_1_.refs_10_.refs_11_
  72.4 1.9 %collective-permute-start.22 = (f32[16,640]{1,0:T(8,128)S(1)}, f32[16,640]{1,0:T(8,128)S(1)}, u32[]{:S(2)}, u32[]{:S(2)}) collective-permute-start(f32[16,640]{1,0:T(8,128)S(1)} %get-tuple-element.124), channel_id=1, source_target_pairs={{0,6},{2,4},{4,2},{6,0},{1,7},{3,5},{5,3},{7,1},{8,14},{10,12},{12... | collective-permute-start | bytes 122888 | tf_op jit(solution)/shard_map/ppermute | solution.py:452
  74.3 1.6 %collective-permute-start.21 = (f32[16,128]{1,0:T(8,128)S(1)}, f32[16,128]{1,0:T(8,128)S(1)}, u32[]{:S(2)}, u32[]{:S(2)}) collective-permute-start(f32[16,128]{1,0:T(8,128)S(1)} %get-tuple-element.122.refs_0_), channel_id=1, source_target_pairs={{0,4},{2,6},{4,0},{6,2},{1,5},{3,7},{5,1},{7,3},{8,12},{10,14},{12... | collective-permute-start | bytes 24584 | tf_op jit(solution)/shard_map/ppermute | solution.py:444
  75.9 3.0 %collective-permute-done.21.refs_2_ = f32[16,128]{1,0:T(8,128)S(1)} collective-permute-done((f32[16,128]{1,0:T(8,128)S(1)}, f32[16,128]{1,0:T(8,128)S(1)}, u32[]{:S(2)}, u32[]{:S(2)}) %collective-permute-start.21) | collective-permute-done | bytes 8224 | tf_op jit(solution)/shard_map/ppermute | solution.py:444
  78.9 0.4 shard_map.86
  79.3 1.1 collective-permute-start.23
  80.4 1.7 %collective-permute-start.24 = (f32[16,1024]{1,0:T(8,128)S(1)}, f32[16,1024]{1,0:T(8,128)S(1)}, u32[]{:S(2)}, u32[]{:S(2)}) collective-permute-start(f32[16,1024]{1,0:T(8,128)S(1)} %get-tuple-element.128), channel_id=1, source_target_pairs={{0,24},{8,16},{16,8},{24,0},{1,25},{9,17},{17,9},{25,1},{2,26},{10... | collective-permute-start | bytes 196616 | tf_op jit(solution)/shard_map/ppermute | solution.py:452
  82.1 0.7 collective-permute-start.25
  82.8 3.2 %collective-permute-done.25.refs_14_ = f32[16,512]{1,0:T(8,128)S(1)} collective-permute-done((f32[16,512]{1,0:T(8,128)S(1)}, f32[16,512]{1,0:T(8,128)S(1)}, u32[]{:S(2)}, u32[]{:S(2)}) %collective-permute-start.25) | collective-permute-done | bytes 32800 | tf_op jit(solution)/shard_map/ppermute | solution.py:444
  86.0 7.8 %shard_map.87 = (f32[2,6,16,256]{3,2,1,0:T(8,128)S(1)}, f32[2,6,16,256]{3,2,1,0:T(8,128)S(1)}, f32[2,6,16,256]{3,2,1,0:T(8,128)S(1)}, f32[2,6,16,256]{3,2,1,0:T(...) custom-call(s32[2,6,6]{2,1,0:T(8,128)S(1)} %copy.13.pattern.refs_0_,, ...), custom_call_target="tpu_custom_call" | custom-call | tf_op jit(solution)/shard_map/pallas_call | solution.py:480
  93.9 1.2 collective-permute-done.26.refs_1_.refs_10_.refs_11_
  95.1 0.7 collective-permute-start.27
  95.8 2.4 %collective-permute-start.29 = (f32[16,640]{1,0:T(8,128)S(1)}, f32[16,640]{1,0:T(8,128)S(1)}, u32[]{:S(2)}, u32[]{:S(2)}) collective-permute-start(f32[16,640]{1,0:T(8,128)S(1)} %get-tuple-element.144), channel_id=1, source_target_pairs={{0,6},{2,4},{4,2},{6,0},{1,7},{3,5},{5,3},{7,1},{8,14},{10,12},{12... | collective-permute-start | bytes 122888 | tf_op jit(solution)/shard_map/ppermute | solution.py:452
  98.2 0.5 collective-permute-start.28
  98.6 4.1 %collective-permute-done.28.refs_2_ = f32[16,128]{1,0:T(8,128)S(1)} collective-permute-done((f32[16,128]{1,0:T(8,128)S(1)}, f32[16,128]{1,0:T(8,128)S(1)}, u32[]{:S(2)}, u32[]{:S(2)}) %collective-permute-start.28) | collective-permute-done | bytes 8224 | tf_op jit(solution)/shard_map/ppermute | solution.py:444
  102.7 0.2 shard_map.89
  102.9 0.8 collective-permute-start.30
  103.7 1.4 %collective-permute-start.31 = (f32[16,1024]{1,0:T(8,128)S(1)}, f32[16,1024]{1,0:T(8,128)S(1)}, u32[]{:S(2)}, u32[]{:S(2)}) collective-permute-start(f32[16,1024]{1,0:T(8,128)S(1)} %get-tuple-element.148), channel_id=1, source_target_pairs={{0,24},{8,16},{16,8},{24,0},{1,25},{9,17},{17,9},{25,1},{2,26},{10... | collective-permute-start | bytes 196616 | tf_op jit(solution)/shard_map/ppermute | solution.py:452
  105.2 1.3 collective-permute-start.32
  106.4 2.8 %collective-permute-done.32.refs_14_ = f32[16,512]{1,0:T(8,128)S(1)} collective-permute-done((f32[16,512]{1,0:T(8,128)S(1)}, f32[16,512]{1,0:T(8,128)S(1)}, u32[]{:S(2)}, u32[]{:S(2)}) %collective-permute-start.32) | collective-permute-done | bytes 32800 | tf_op jit(solution)/shard_map/ppermute | solution.py:444
  109.3 7.9 %shard_map.90 = (f32[2,6,16,256]{3,2,1,0:T(8,128)S(1)}, f32[2,6,16,256]{3,2,1,0:T(8,128)S(1)}, f32[2,6,16,256]{3,2,1,0:T(8,128)S(1)}, f32[2,6,16,256]{3,2,1,0:T(...) custom-call(s32[2,6,6]{2,1,0:T(8,128)S(1)} %copy.13.pattern.refs_0_,, ...), custom_call_target="tpu_custom_call" | custom-call | tf_op jit(solution)/shard_map/pallas_call | solution.py:480
  117.1 1.2 collective-permute-done.33.refs_1_.refs_4_.refs_5_
  118.5 1.9 %collective-permute-start.36 = (f32[16,640]{1,0:T(8,128)S(1)}, f32[16,640]{1,0:T(8,128)S(1)}, u32[]{:S(2)}, u32[]{:S(2)}) collective-permute-start(f32[16,640]{1,0:T(8,128)S(1)} %get-tuple-element.164), channel_id=1, source_target_pairs={{0,6},{2,4},{4,2},{6,0},{1,7},{3,5},{5,3},{7,1},{8,14},{10,12},{12... | collective-permute-start | bytes 122888 | tf_op jit(solution)/shard_map/ppermute | solution.py:452
  120.3 1.6 %collective-permute-start.35 = (f32[16,128]{1,0:T(8,128)S(1)}, f32[16,128]{1,0:T(8,128)S(1)}, u32[]{:S(2)}, u32[]{:S(2)}) collective-permute-start(f32[16,128]{1,0:T(8,128)S(1)} %get-tuple-element.162.refs_0_), channel_id=1, source_target_pairs={{0,4},{2,6},{4,0},{6,2},{1,5},{3,7},{5,1},{7,3},{8,12},{10,14},{12... | collective-permute-start | bytes 24584 | tf_op jit(solution)/shard_map/ppermute | solution.py:444
  121.9 3.0 %collective-permute-done.35.refs_2_ = f32[16,128]{1,0:T(8,128)S(1)} collective-permute-done((f32[16,128]{1,0:T(8,128)S(1)}, f32[16,128]{1,0:T(8,128)S(1)}, u32[]{:S(2)}, u32[]{:S(2)}) %collective-permute-start.35) | collective-permute-done | bytes 8224 | tf_op jit(solution)/shard_map/ppermute | solution.py:444
  125.1 1.2 collective-permute-start.37
  126.3 1.6 %collective-permute-start.38 = (f32[16,1024]{1,0:T(8,128)S(1)}, f32[16,1024]{1,0:T(8,128)S(1)}, u32[]{:S(2)}, u32[]{:S(2)}) collective-permute-start(f32[16,1024]{1,0:T(8,128)S(1)} %get-tuple-element.168), channel_id=1, source_target_pairs={{0,24},{8,16},{16,8},{24,0},{1,25},{9,17},{17,9},{25,1},{2,26},{10... | collective-permute-start | bytes 196616 | tf_op jit(solution)/shard_map/ppermute | solution.py:452
  127.9 0.7 collective-permute-start.39
  128.6 3.2 %collective-permute-done.39.refs_8_ = f32[16,512]{1,0:T(8,128)S(1)} collective-permute-done((f32[16,512]{1,0:T(8,128)S(1)}, f32[16,512]{1,0:T(8,128)S(1)}, u32[]{:S(2)}, u32[]{:S(2)}) %collective-permute-start.39) | collective-permute-done | bytes 32800 | tf_op jit(solution)/shard_map/ppermute | solution.py:444
  131.8 1.2 shard_map.93
  (46 shorter events, 0.9 us)
Async XLA Ops:
  0.6 32.2 %copy-start.4 = (s32[1,1,2,6,6]{4,2,3,1,0:T(2,128)S(1)}, s32[1,1,2,6,6]{4,2,3,1,0:T(2,128)}, u32[]{:S(2)}) copy-start(s32[1,1,2,6,6]{4,2,3,1,0:T(2,128)} %param.8) | copy-start | bytes 868
  2.2 0.9 copy-start.2
  3.1 0.7 copy-start.3
  4.5 9.7 %collective-permute-start = (f32[80,256]{1,0:T(8,128)S(1)}, f32[80,256]{1,0:T(8,128)S(1)}, u32[]{:S(2)}, u32[]{:S(2)}) collective-permute-start(f32[80,256]{1,0:T(8,128)S(1)} %get-tuple-element.91), channel_id=1, source_target_pairs={{0,8},{8,0},{16,24},{24,16},{1,9},{9,1},{17,25},{25,17},{2,10},{10... | collective-permute-start | bytes 245768 | tf_op jit(solution)/shard_map/ppermute | solution.py:444
  7.5 6.8 %collective-permute-start.1 = (f32[80,256]{1,0:T(8,128)S(1)}, f32[80,256]{1,0:T(8,128)S(1)}, u32[]{:S(2)}, u32[]{:S(2)}) collective-permute-start(f32[80,256]{1,0:T(8,128)S(1)} %get-tuple-element.92), channel_id=1, source_target_pairs={{0,24},{8,16},{16,8},{24,0},{1,25},{9,17},{17,9},{25,1},{2,26},{10... | collective-permute-start | bytes 245768 | tf_op jit(solution)/shard_map/ppermute | solution.py:452
  9.0 5.3 %collective-permute-start.2 = (f32[80,256]{1,0:T(8,128)S(1)}, f32[80,256]{1,0:T(8,128)S(1)}, u32[]{:S(2)}, u32[]{:S(2)}) collective-permute-start(f32[80,256]{1,0:T(8,128)S(1)} %get-tuple-element.93), channel_id=1, source_target_pairs={{0,2},{2,0},{4,6},{6,4},{1,3},{3,1},{5,7},{7,5},{8,10},{10,8},{12,... | collective-permute-start | bytes 245768 | tf_op jit(solution)/shard_map/ppermute | solution.py:444
  10.5 6.2 %collective-permute-start.3 = (f32[80,256]{1,0:T(8,128)S(1)}, f32[80,256]{1,0:T(8,128)S(1)}, u32[]{:S(2)}, u32[]{:S(2)}) collective-permute-start(f32[80,256]{1,0:T(8,128)S(1)} %get-tuple-element.94), channel_id=1, source_target_pairs={{0,6},{2,4},{4,2},{6,0},{1,7},{3,5},{5,3},{7,1},{8,14},{10,12},{12... | collective-permute-start | bytes 245768 | tf_op jit(solution)/shard_map/ppermute | solution.py:452
  13.0 1.2 collective-permute-start.4
  20.8 1.2 collective-permute-start.5
  22.0 5.4 %collective-permute-start.8 = (f32[16,128]{1,0:T(8,128)S(1)}, f32[16,128]{1,0:T(8,128)S(1)}, u32[]{:S(2)}, u32[]{:S(2)}) collective-permute-start(f32[16,128]{1,0:T(8,128)S(1)} %shard_map.79.refs_0_), channel_id=1, source_target_pairs={{0,6},{2,4},{4,2},{6,0},{1,7},{3,5},{5,3},{7,1},{8,14},{10,12},{12... | collective-permute-start | bytes 24584 | tf_op jit(solution)/shard_map/ppermute | solution.py:452
  24.6 4.5 %collective-permute-start.7 = (f32[16,128]{1,0:T(8,128)S(1)}, f32[16,128]{1,0:T(8,128)S(1)}, u32[]{:S(2)}, u32[]{:S(2)}) collective-permute-start(f32[16,128]{1,0:T(8,128)S(1)} %shard_map.79.refs_0_), channel_id=1, source_target_pairs={{0,4},{2,6},{4,0},{6,2},{1,5},{3,7},{5,1},{7,3},{8,12},{10,14},{12... | collective-permute-start | bytes 24584 | tf_op jit(solution)/shard_map/ppermute | solution.py:444
  24.6 4.5 %collective-permute-start.6 = (f32[16,128]{1,0:T(8,128)S(1)}, f32[16,128]{1,0:T(8,128)S(1)}, u32[]{:S(2)}, u32[]{:S(2)}) collective-permute-start(f32[16,128]{1,0:T(8,128)S(1)} %shard_map.79.refs_0_), channel_id=1, source_target_pairs={{0,2},{2,0},{4,6},{6,4},{1,3},{3,1},{5,7},{7,5},{8,10},{10,8},{12,... | collective-permute-start | bytes 24584 | tf_op jit(solution)/shard_map/ppermute | solution.py:444
  29.3 4.8 %collective-permute-start.11 = (f32[16,512]{1,0:T(8,128)S(1)}, f32[16,512]{1,0:T(8,128)S(1)}, u32[]{:S(2)}, u32[]{:S(2)}) collective-permute-start(f32[16,512]{1,0:T(8,128)S(1)} %shard_map.80.refs_0_), channel_id=1, source_target_pairs={{0,24},{8,16},{16,8},{24,0},{1,25},{9,17},{17,9},{25,1},{2,26},{10... | collective-permute-start | bytes 98312 | tf_op jit(solution)/shard_map/ppermute | solution.py:452
  30.8 3.9 %collective-permute-start.10 = (f32[16,512]{1,0:T(8,128)S(1)}, f32[16,512]{1,0:T(8,128)S(1)}, u32[]{:S(2)}, u32[]{:S(2)}) collective-permute-start(f32[16,512]{1,0:T(8,128)S(1)} %shard_map.80.refs_0_), channel_id=1, source_target_pairs={{0,16},{8,24},{16,0},{24,8},{1,17},{9,25},{17,1},{25,9},{2,18},{10... | collective-permute-start | bytes 98312 | tf_op jit(solution)/shard_map/ppermute | solution.py:444
  32.3 3.9 %collective-permute-start.9 = (f32[16,512]{1,0:T(8,128)S(1)}, f32[16,512]{1,0:T(8,128)S(1)}, u32[]{:S(2)}, u32[]{:S(2)}) collective-permute-start(f32[16,512]{1,0:T(8,128)S(1)} %shard_map.80.refs_0_), channel_id=1, source_target_pairs={{0,8},{8,0},{16,24},{24,16},{1,9},{9,1},{17,25},{25,17},{2,10},{10... | collective-permute-start | bytes 98312 | tf_op jit(solution)/shard_map/ppermute | solution.py:444
  36.2 3.7 %copy-start = (bf16[1,1,2,6,6,256,256]{6,5,4,3,2,1,0:T(8,128)(2,1)S(1)}, bf16[1,1,2,6,6,256,256]{6,5,4,3,2,1,0:T(8,128)(2,1)}, u32[]{:S(2)}) copy-start(bf16[1,1,2,6,6,256,256]{6,5,4,3,2,1,0:T(8,128)(2,1)} %param.7) | copy-start | bytes 28311556
  39.9 23.4 %copy-start.1 = (bf16[1,1,2,6,6,256,256]{6,5,4,3,2,1,0:T(8,128)(2,1)S(1)}, bf16[1,1,2,6,6,256,256]{6,5,4,3,2,1,0:T(8,128)(2,1)}, u32[]{:S(2)}) copy-start(bf16[1,1,2,6,6,256,256]{6,5,4,3,2,1,0:T(8,128)(2,1)} %param.7) | copy-start | bytes 28311556
  47.7 1.2 collective-permute-start.12
  48.9 8.1 %collective-permute-start.13 = (f32[16,640]{1,0:T(8,128)S(1)}, f32[16,640]{1,0:T(8,128)S(1)}, u32[]{:S(2)}, u32[]{:S(2)}) collective-permute-start(f32[16,640]{1,0:T(8,128)S(1)} %get-tuple-element.108), channel_id=1, source_target_pairs={{0,2},{2,0},{4,6},{6,4},{1,3},{3,1},{5,7},{7,5},{8,10},{10,8},{12,... | collective-permute-start | bytes 122888 | tf_op jit(solution)/shard_map/ppermute | solution.py:444
  49.9 7.1 %collective-permute-start.15 = (f32[16,640]{1,0:T(8,128)S(1)}, f32[16,640]{1,0:T(8,128)S(1)}, u32[]{:S(2)}, u32[]{:S(2)}) collective-permute-start(f32[16,640]{1,0:T(8,128)S(1)} %get-tuple-element.109), channel_id=1, source_target_pairs={{0,6},{2,4},{4,2},{6,0},{1,7},{3,5},{5,3},{7,1},{8,14},{10,12},{12... | collective-permute-start | bytes 122888 | tf_op jit(solution)/shard_map/ppermute | solution.py:452
  52.4 4.5 %collective-permute-start.14 = (f32[16,128]{1,0:T(8,128)S(1)}, f32[16,128]{1,0:T(8,128)S(1)}, u32[]{:S(2)}, u32[]{:S(2)}) collective-permute-start(f32[16,128]{1,0:T(8,128)S(1)} %get-tuple-element.107.refs_0_), channel_id=1, source_target_pairs={{0,4},{2,6},{4,0},{6,2},{1,5},{3,7},{5,1},{7,3},{8,12},{10,14},{12... | collective-permute-start | bytes 24584 | tf_op jit(solution)/shard_map/ppermute | solution.py:444
  57.2 6.1 %collective-permute-start.16 = (f32[16,1024]{1,0:T(8,128)S(1)}, f32[16,1024]{1,0:T(8,128)S(1)}, u32[]{:S(2)}, u32[]{:S(2)}) collective-permute-start(f32[16,1024]{1,0:T(8,128)S(1)} %get-tuple-element.112), channel_id=1, source_target_pairs={{0,8},{8,0},{16,24},{24,16},{1,9},{9,1},{17,25},{25,17},{2,10},{10... | collective-permute-start | bytes 196616 | tf_op jit(solution)/shard_map/ppermute | solution.py:444
  57.7 5.5 %collective-permute-start.17 = (f32[16,1024]{1,0:T(8,128)S(1)}, f32[16,1024]{1,0:T(8,128)S(1)}, u32[]{:S(2)}, u32[]{:S(2)}) collective-permute-start(f32[16,1024]{1,0:T(8,128)S(1)} %get-tuple-element.113), channel_id=1, source_target_pairs={{0,24},{8,16},{16,8},{24,0},{1,25},{9,17},{17,9},{25,1},{2,26},{10... | collective-permute-start | bytes 196616 | tf_op jit(solution)/shard_map/ppermute | solution.py:452
  59.2 4.1 %collective-permute-start.18 = (f32[16,512]{1,0:T(8,128)S(1)}, f32[16,512]{1,0:T(8,128)S(1)}, u32[]{:S(2)}, u32[]{:S(2)}) collective-permute-start(f32[16,512]{1,0:T(8,128)S(1)} %get-tuple-element.114.refs_12_), channel_id=1, source_target_pairs={{0,16},{8,24},{16,0},{24,8},{1,17},{9,25},{17,1},{25,9},{2,18},{10... | collective-permute-start | bytes 98312 | tf_op jit(solution)/shard_map/ppermute | solution.py:444
  71.1 1.2 collective-permute-start.19
  72.4 6.6 %collective-permute-start.20 = (f32[16,640]{1,0:T(8,128)S(1)}, f32[16,640]{1,0:T(8,128)S(1)}, u32[]{:S(2)}, u32[]{:S(2)}) collective-permute-start(f32[16,640]{1,0:T(8,128)S(1)} %get-tuple-element.123), channel_id=1, source_target_pairs={{0,2},{2,0},{4,6},{6,4},{1,3},{3,1},{5,7},{7,5},{8,10},{10,8},{12,... | collective-permute-start | bytes 122888 | tf_op jit(solution)/shard_map/ppermute | solution.py:444
  72.4 6.5 %collective-permute-start.22 = (f32[16,640]{1,0:T(8,128)S(1)}, f32[16,640]{1,0:T(8,128)S(1)}, u32[]{:S(2)}, u32[]{:S(2)}) collective-permute-start(f32[16,640]{1,0:T(8,128)S(1)} %get-tuple-element.124), channel_id=1, source_target_pairs={{0,6},{2,4},{4,2},{6,0},{1,7},{3,5},{5,3},{7,1},{8,14},{10,12},{12... | collective-permute-start | bytes 122888 | tf_op jit(solution)/shard_map/ppermute | solution.py:452
  74.3 4.6 %collective-permute-start.21 = (f32[16,128]{1,0:T(8,128)S(1)}, f32[16,128]{1,0:T(8,128)S(1)}, u32[]{:S(2)}, u32[]{:S(2)}) collective-permute-start(f32[16,128]{1,0:T(8,128)S(1)} %get-tuple-element.122.refs_0_), channel_id=1, source_target_pairs={{0,4},{2,6},{4,0},{6,2},{1,5},{3,7},{5,1},{7,3},{8,12},{10,14},{12... | collective-permute-start | bytes 24584 | tf_op jit(solution)/shard_map/ppermute | solution.py:444
  79.3 6.8 %collective-permute-start.23 = (f32[16,1024]{1,0:T(8,128)S(1)}, f32[16,1024]{1,0:T(8,128)S(1)}, u32[]{:S(2)}, u32[]{:S(2)}) collective-permute-start(f32[16,1024]{1,0:T(8,128)S(1)} %get-tuple-element.127), channel_id=1, source_target_pairs={{0,8},{8,0},{16,24},{24,16},{1,9},{9,1},{17,25},{25,17},{2,10},{10... | collective-permute-start | bytes 196616 | tf_op jit(solution)/shard_map/ppermute | solution.py:444
  80.4 5.6 %collective-permute-start.24 = (f32[16,1024]{1,0:T(8,128)S(1)}, f32[16,1024]{1,0:T(8,128)S(1)}, u32[]{:S(2)}, u32[]{:S(2)}) collective-permute-start(f32[16,1024]{1,0:T(8,128)S(1)} %get-tuple-element.128), channel_id=1, source_target_pairs={{0,24},{8,16},{16,8},{24,0},{1,25},{9,17},{17,9},{25,1},{2,26},{10... | collective-permute-start | bytes 196616 | tf_op jit(solution)/shard_map/ppermute | solution.py:452
  82.1 3.9 %collective-permute-start.25 = (f32[16,512]{1,0:T(8,128)S(1)}, f32[16,512]{1,0:T(8,128)S(1)}, u32[]{:S(2)}, u32[]{:S(2)}) collective-permute-start(f32[16,512]{1,0:T(8,128)S(1)} %get-tuple-element.129.refs_12_), channel_id=1, source_target_pairs={{0,16},{8,24},{16,0},{24,8},{1,17},{9,25},{17,1},{25,9},{2,18},{10... | collective-permute-start | bytes 98312 | tf_op jit(solution)/shard_map/ppermute | solution.py:444
  93.9 1.2 collective-permute-start.26
  95.1 7.6 %collective-permute-start.27 = (f32[16,640]{1,0:T(8,128)S(1)}, f32[16,640]{1,0:T(8,128)S(1)}, u32[]{:S(2)}, u32[]{:S(2)}) collective-permute-start(f32[16,640]{1,0:T(8,128)S(1)} %get-tuple-element.143), channel_id=1, source_target_pairs={{0,2},{2,0},{4,6},{6,4},{1,3},{3,1},{5,7},{7,5},{8,10},{10,8},{12,... | collective-permute-start | bytes 122888 | tf_op jit(solution)/shard_map/ppermute | solution.py:444
  95.8 6.9 %collective-permute-start.29 = (f32[16,640]{1,0:T(8,128)S(1)}, f32[16,640]{1,0:T(8,128)S(1)}, u32[]{:S(2)}, u32[]{:S(2)}) collective-permute-start(f32[16,640]{1,0:T(8,128)S(1)} %get-tuple-element.144), channel_id=1, source_target_pairs={{0,6},{2,4},{4,2},{6,0},{1,7},{3,5},{5,3},{7,1},{8,14},{10,12},{12... | collective-permute-start | bytes 122888 | tf_op jit(solution)/shard_map/ppermute | solution.py:452
  98.2 4.5 %collective-permute-start.28 = (f32[16,128]{1,0:T(8,128)S(1)}, f32[16,128]{1,0:T(8,128)S(1)}, u32[]{:S(2)}, u32[]{:S(2)}) collective-permute-start(f32[16,128]{1,0:T(8,128)S(1)} %get-tuple-element.142.refs_0_), channel_id=1, source_target_pairs={{0,4},{2,6},{4,0},{6,2},{1,5},{3,7},{5,1},{7,3},{8,12},{10,14},{12... | collective-permute-start | bytes 24584 | tf_op jit(solution)/shard_map/ppermute | solution.py:444
  102.9 6.3 %collective-permute-start.30 = (f32[16,1024]{1,0:T(8,128)S(1)}, f32[16,1024]{1,0:T(8,128)S(1)}, u32[]{:S(2)}, u32[]{:S(2)}) collective-permute-start(f32[16,1024]{1,0:T(8,128)S(1)} %get-tuple-element.147), channel_id=1, source_target_pairs={{0,8},{8,0},{16,24},{24,16},{1,9},{9,1},{17,25},{25,17},{2,10},{10... | collective-permute-start | bytes 196616 | tf_op jit(solution)/shard_map/ppermute | solution.py:444
  103.7 5.5 %collective-permute-start.31 = (f32[16,1024]{1,0:T(8,128)S(1)}, f32[16,1024]{1,0:T(8,128)S(1)}, u32[]{:S(2)}, u32[]{:S(2)}) collective-permute-start(f32[16,1024]{1,0:T(8,128)S(1)} %get-tuple-element.148), channel_id=1, source_target_pairs={{0,24},{8,16},{16,8},{24,0},{1,25},{9,17},{17,9},{25,1},{2,26},{10... | collective-permute-start | bytes 196616 | tf_op jit(solution)/shard_map/ppermute | solution.py:452
  105.2 4.1 %collective-permute-start.32 = (f32[16,512]{1,0:T(8,128)S(1)}, f32[16,512]{1,0:T(8,128)S(1)}, u32[]{:S(2)}, u32[]{:S(2)}) collective-permute-start(f32[16,512]{1,0:T(8,128)S(1)} %get-tuple-element.149.refs_12_), channel_id=1, source_target_pairs={{0,16},{8,24},{16,0},{24,8},{1,17},{9,25},{17,1},{25,9},{2,18},{10... | collective-permute-start | bytes 98312 | tf_op jit(solution)/shard_map/ppermute | solution.py:444
  117.1 1.2 collective-permute-start.33
  118.3 6.6 %collective-permute-start.34 = (f32[16,640]{1,0:T(8,128)S(1)}, f32[16,640]{1,0:T(8,128)S(1)}, u32[]{:S(2)}, u32[]{:S(2)}) collective-permute-start(f32[16,640]{1,0:T(8,128)S(1)} %get-tuple-element.163), channel_id=1, source_target_pairs={{0,2},{2,0},{4,6},{6,4},{1,3},{3,1},{5,7},{7,5},{8,10},{10,8},{12,... | collective-permute-start | bytes 122888 | tf_op jit(solution)/shard_map/ppermute | solution.py:444
  118.5 6.4 %collective-permute-start.36 = (f32[16,640]{1,0:T(8,128)S(1)}, f32[16,640]{1,0:T(8,128)S(1)}, u32[]{:S(2)}, u32[]{:S(2)}) collective-permute-start(f32[16,640]{1,0:T(8,128)S(1)} %get-tuple-element.164), channel_id=1, source_target_pairs={{0,6},{2,4},{4,2},{6,0},{1,7},{3,5},{5,3},{7,1},{8,14},{10,12},{12... | collective-permute-start | bytes 122888 | tf_op jit(solution)/shard_map/ppermute | solution.py:452
  120.3 4.5 %collective-permute-start.35 = (f32[16,128]{1,0:T(8,128)S(1)}, f32[16,128]{1,0:T(8,128)S(1)}, u32[]{:S(2)}, u32[]{:S(2)}) collective-permute-start(f32[16,128]{1,0:T(8,128)S(1)} %get-tuple-element.162.refs_0_), channel_id=1, source_target_pairs={{0,4},{2,6},{4,0},{6,2},{1,5},{3,7},{5,1},{7,3},{8,12},{10,14},{12... | collective-permute-start | bytes 24584 | tf_op jit(solution)/shard_map/ppermute | solution.py:444
  125.1 6.8 %collective-permute-start.37 = (f32[16,1024]{1,0:T(8,128)S(1)}, f32[16,1024]{1,0:T(8,128)S(1)}, u32[]{:S(2)}, u32[]{:S(2)}) collective-permute-start(f32[16,1024]{1,0:T(8,128)S(1)} %get-tuple-element.167), channel_id=1, source_target_pairs={{0,8},{8,0},{16,24},{24,16},{1,9},{9,1},{17,25},{25,17},{2,10},{10... | collective-permute-start | bytes 196616 | tf_op jit(solution)/shard_map/ppermute | solution.py:444
  126.3 5.5 %collective-permute-start.38 = (f32[16,1024]{1,0:T(8,128)S(1)}, f32[16,1024]{1,0:T(8,128)S(1)}, u32[]{:S(2)}, u32[]{:S(2)}) collective-permute-start(f32[16,1024]{1,0:T(8,128)S(1)} %get-tuple-element.168), channel_id=1, source_target_pairs={{0,24},{8,16},{16,8},{24,0},{1,25},{9,17},{17,9},{25,1},{2,26},{10... | collective-permute-start | bytes 196616 | tf_op jit(solution)/shard_map/ppermute | solution.py:452
  127.9 3.9 %collective-permute-start.39 = (f32[16,512]{1,0:T(8,128)S(1)}, f32[16,512]{1,0:T(8,128)S(1)}, u32[]{:S(2)}, u32[]{:S(2)}) collective-permute-start(f32[16,512]{1,0:T(8,128)S(1)} %get-tuple-element.169.refs_6_), channel_id=1, source_target_pairs={{0,16},{8,24},{16,0},{24,8},{1,17},{9,25},{17,1},{25,9},{2,18},{10... | collective-permute-start | bytes 98312 | tf_op jit(solution)/shard_map/ppermute | solution.py:444

commit v3 on v2

--- a/solution.py
+++ b/solution.py
@@ -15,6 +15,7 @@
 SCALARS = 3
 NT = (((1,), (1,)), ((), ()))
 NN = (((1,), (0,)), ((), ()))
+TN = (((0,), (0,)), ((), ()))
 f32 = jnp.float32
 bf16 = jnp.bfloat16
 
@@ -101,23 +102,29 @@
     return jnp.where(cond, a, b)
 
 
-def pack_kernel(rhs, modes, fmap, coarse, xa, xb, ya, yb, za, zb):
+def pack_kernel(rhs_in, modes_in, fmap_in, coarse_in, rhs, modes, fmap, coarse, xa, xb, ya, yb, za, zb, sems):
     parity, _ = position((1, 1, 1))
+    loads = ((rhs_in, rhs), (modes_in, modes), (fmap_in, fmap), (coarse_in, coarse))
+    copies = [pltpu.make_async_copy(source, target, sems.at[k]) for k, (source, target) in enumerate(loads)]
+    for copy in copies:
+        copy.start()
+    for copy in copies:
+        copy.wait()
     slabs = -(-coarse.shape[1] // 256)
     for d, outs in ((0, (xa, xb)), (1, (ya, yb))):
         for s in range(2):
-            up, down = modes[s, d], modes[s, d + 3]
+            up, down = modes[d, :, s, :], modes[d + 3, :, s, :]
             first = pick(parity[d], down, up)
             second = pick(parity[d], up, down)
             for out, piece in zip(outs, (first, second)):
                 out[24 * s : 24 * s + 16, :] = rhs[s, d]
                 out[24 * s + 16 : 24 * s + 24, :] = jnp.concatenate(
-                    [piece, fmap[s, d : d + 1, :].astype(f32), jnp.zeros((1, 256), f32)], 0
+                    [piece, fmap[d, s : s + 1, :].astype(f32), jnp.zeros((1, 256), f32)], 0
                 )
-    up, down = modes[1, 2], modes[0, 5]
+    up, down = modes[2, :, 1, :], modes[5, :, 0, :]
     for out, piece in zip((za, zb), (pick(parity[2], down, up), pick(parity[2], up, down))):
         out[0:16, :] = rhs[1, 2]
-        out[16:24, :] = jnp.concatenate([piece, fmap[1, 2:3, :].astype(f32), jnp.zeros((1, 256), f32)], 0)
+        out[16:24, :] = jnp.concatenate([piece, fmap[2, 1:2, :].astype(f32), jnp.zeros((1, 256), f32)], 0)
     for k in range(slabs):
         width = min(256, coarse.shape[1] - 256 * k)
         slab = coarse[:, 256 * k : 256 * k + width]
@@ -129,73 +136,141 @@
             out[base + 16 * k : base + 16 * k + 16, :] = slab
 
 
-def setup_kernel(sizes, rhs, modes, fmap, coarse, xa, xb, ya, yb, za, zb, perm, lift, sums, start, solve, place, part, work, rows):
+def sides_of(parity, packs):
+    plus, minus = [], []
+    for d in range(3):
+        va, vb = packs[2 * d][...], packs[2 * d + 1][...]
+        plus.append(pick(parity[d], vb, va))
+        minus.append(pick(parity[d], va, vb))
+    return plus, minus
+
+
+def onehot(row):
+    line = lax.broadcasted_iota(jnp.int32, (256, 256), 0)
+    return (line == row.astype(jnp.int32)).astype(bf16)
+
+
+def lower_map(fmap, minus, s, d):
+    if d == 2 and s == 1:
+        return fmap[2, 0:1, :]
+    base = 24 * s if d < 2 else 0
+    return minus[d][base + 22 : base + 23, :]
+
+
+def lower_values(rhs, minus, s, d):
+    if d == 2 and s == 1:
+        return rhs[0, 2]
+    base = 24 * s if d < 2 else 0
+    inside = lax.axis_index(AXES[d]) > 0
+    return minus[d][base : base + 16, :] * inside.astype(f32)
+
+
+def begin_kernel(sizes, rhs, modes, fmap, xa, xb, ya, yb, za, zb, touched, part):
+    parity, _ = position((1, 1, 1))
+    levels = 2 * sizes[2]
+    lanes = part.shape[1]
+    _, minus = sides_of(parity, (xa, xb, ya, yb, za, zb))
+    zero2 = jnp.zeros((2, 256), f32)
+    total = jnp.zeros((16, lanes), f32)
+    for s in range(2):
+        sums = jnp.zeros((48, 16), f32)
+        for f in range(6):
+            d = f % 3
+            if f < 3:
+                left = split3(rhs[s, f])
+            else:
+                table_rows = onehot(lower_map(fmap, minus, s, d))
+                left = -mm(split3(lower_values(rhs, minus, s, d)), table_rows, NN)
+                left = left.astype(bf16)
+            sums += mm(left, split2(jnp.concatenate([modes[f, :, s, :], zero2], 0)), NT)
+        own = fold3(sums)
+        own = own[:, :8] + own[:, 8:]
+        mode = lax.broadcasted_iota(jnp.int32, (8, lanes), 0)
+        lane = lax.broadcasted_iota(jnp.int32, (8, lanes), 1)
+        level = 2 * lax.axis_index("gz") + s
+        choose = ((lane == level * 6 + mode) & (mode < 6)).astype(bf16)
+        total += fold3(mm(split3(own), choose, NN))
+    part[...] = total
+
+
+def place_rows(sizes, nc, lanes, width, k):
+    gx, gy = lax.axis_index("gx"), lax.axis_index("gy")
+    levels = 2 * sizes[2]
+    line = lax.broadcasted_iota(jnp.int32, (lanes, 1), 0)
+    whole = lax.broadcasted_iota(jnp.int32, (lanes, width), 1)
+    y = jnp.bitwise_xor(gy, k)
+    aim = jnp.where(line >= 30 * levels, nc + line - 30 * levels, -1)
+    for t, (dx, dy) in enumerate(((0, 0), (-1, 0), (1, 0), (0, -1), (0, 1))):
+        inside = (gx + dx >= 0) & (gx + dx < sizes[0]) & (y + dy >= 0) & (y + dy < sizes[1])
+        first = jnp.where(inside, ((gx + dx) * sizes[1] + y + dy - t) * 6 * levels, -6 * nc)
+        aim = jnp.where((line >= t * 6 * levels) & (line < (t + 1) * 6 * levels), line + first, aim)
+    return (whole == aim).astype(bf16)
+
+
+def place_table_kernel(sizes, nc, lanes, place):
+    for k in range(sizes[1]):
+        place[k * lanes : k * lanes + lanes, :] = place_rows(sizes, nc, lanes, place.shape[1], k)
+
+
+def touch_kernel(factors, out):
+    out[...] = factors[0, 0, 0, 0:16, 0:LANES].astype(f32)[:8]
+
+
+def turn_kernel(factors, turned):
+    for s in range(factors.shape[0]):
+        for i in range(factors.shape[1]):
+            for j in range(factors.shape[2]):
+                turned[s, i, j] = factors[s, i, j].T
+
+
+def setup_kernel(sizes, rhs, modes, fmap, coarse, xa, xb, ya, yb, za, zb, *refs):
+    perm, back, lift, sums, start, solve, work, rows = refs
     parity, _ = position((1, 1, 1))
     nc = coarse.shape[1]
     slabs = -(-nc // 256)
     levels = 2 * sizes[2]
     lanes = column_lanes(levels)
-    gx, gy, gz = (lax.axis_index(a) for a in AXES)
-    lane_row = lax.broadcasted_iota(jnp.int32, (256, 256), 0)
-
-    plus, minus = [], []
-    for d, (a, b) in enumerate(((xa, xb), (ya, yb), (za, zb))):
-        va, vb = a[...], b[...]
-        plus.append(pick(parity[d], vb, va))
-        minus.append(pick(parity[d], va, vb))
-
-    def onehot(row):
-        return (lane_row == row.astype(jnp.int32)).astype(bf16)
+    gz = lax.axis_index("gz")
+    plus, minus = sides_of(parity, (xa, xb, ya, yb, za, zb))
 
     def to_upper_order(values, table_rows):
         return -fold3(mm(split3(values), table_rows, NT))
 
     zero2 = jnp.zeros((2, 256), f32)
-    partial = jnp.zeros((48, lanes), f32)
-    lane_column = lax.broadcasted_iota(jnp.int32, (lanes, 16), 0)
-    source_row = lax.broadcasted_iota(jnp.int32, (lanes, 16), 1)
-    up_perm = {}
+    lane_column = lax.broadcasted_iota(jnp.int32, (16, lanes), 1)
+    source_row = lax.broadcasted_iota(jnp.int32, (16, lanes), 0)
+    tilde_low = {}
     for s in range(2):
         for d in range(3):
-            up_perm[s, d] = onehot(fmap[s, d : d + 1, :])
-    tilde_low = {}
-    for s in range(2):
-        for d in range(3):
-            if d == 2 and s == 1:
-                table_rows = up_perm[0, 2]
-            else:
-                base = 24 * s if d < 2 else 0
-                table_rows = onehot(minus[d][base + 22 : base + 23, :])
+            table_rows = onehot(lower_map(fmap, minus, s, d))
             perm[s * 3 + d] = table_rows
-            tilde_low[s, d] = to_upper_order(modes[s, d + 3], table_rows)
+            back[s * 3 + d] = table_rows.T
+            tilde_low[s, d] = to_upper_order(modes[d + 3, :, s, :], table_rows)
+    work[...] = jnp.zeros(work.shape, f32)
     for s in range(2):
         for f in range(6):
             d = f % 3
+            base = 24 * s if d < 2 else 0
             if f < 3:
-                own = modes[s, f]
-                value = rhs[s, f]
+                own = modes[f, :, s, :]
+                start[s, f] = rhs[s, f]
                 if d == 2 and s == 0:
                     other = tilde_low[1, 2]
                 else:
-                    base = 24 * s if d < 2 else 0
-                    other = to_upper_order(plus[d][base + 16 : base + 22, :], up_perm[s, d])
+                    other = to_upper_order(plus[d][base + 16 : base + 22, :], onehot(fmap[d, s : s + 1, :]))
             else:
                 own = tilde_low[s, d]
-                if d == 2 and s == 1:
-                    other = modes[0, 2]
-                    value = rhs[0, 2]
-                else:
-                    base = 24 * s if d < 2 else 0
-                    other = minus[d][base + 16 : base + 22, :]
-                    inside = lax.axis_index(AXES[d]) > 0
-                    value = minus[d][base : base + 16, :] * inside.astype(f32)
-            start[s, f] = value
-            work[...] = jnp.zeros(work.shape, f32)
-            work[own_slot(s) * SLOT : own_slot(s) * SLOT + 8, :] = jnp.concatenate([own, zero2], 0)
-            n = nbr_slot(s, f)
-            work[n * SLOT : n * SLOT + 8, :] = jnp.concatenate([other, zero2], 0)
+                start[s, f] = lower_values(rhs, minus, s, d)
+                other = modes[2, :, 0, :] if d == 2 and s == 1 else minus[d][base + 16 : base + 22, :]
+            own = jnp.concatenate([own, zero2], 0)
+            other = jnp.concatenate([other, zero2], 0)
+            at, n = own_slot(s) * SLOT, nbr_slot(s, f) * SLOT
+            work[at : at + 8, :] = own
+            work[n : n + 8, :] = other
             lift[s * 6 + f] = split2(work[...])
-            pair = split2(jnp.concatenate([own, zero2, other, zero2], 0))
+            work[at : at + 8, :] = jnp.zeros((8, 256), f32)
+            work[n : n + 8, :] = jnp.zeros((8, 256), f32)
+            pair = split2(jnp.concatenate([own, other], 0))
             level = 2 * gz + s
             if d == 2:
                 target = (level + (1 if f == 2 else -1)) * 6
@@ -203,20 +278,16 @@
                 target = COLUMN_OF_FACE[f] * 6 * levels + level * 6
             mode = jnp.bitwise_and(source_row, 7)
             aim = jnp.where(source_row < 8, level * 6, target) + mode
-            choose = (lane_column == aim) & (mode < 6)
-            both = choose.astype(bf16)
-            alone = (choose & (source_row < 8)).astype(bf16)
-            left = split3(value)
+            both = ((lane_column == aim) & (mode < 6)).astype(bf16)
             for h in range(2):
                 half = pair[16 * h : 16 * h + 16]
-                sums[s * 6 + f, h * lanes : h * lanes + lanes, :] = mm(both, half, NN).astype(bf16)
-                partial += mm(left, mm(alone, half, NN).astype(bf16), NT)
+                sums[s * 6 + f, :, h * lanes : h * lanes + lanes] = mm(half, both, TN).astype(bf16)
 
     rows[...] = jnp.zeros(rows.shape, f32)
     pieces = [(2, minus[0], 48, 16), (4, plus[0], 48, 16), (6, minus[1], 48, 16), (8, plus[1], 48, 16)]
     pieces += [(10, minus[2], 24 + 8, 8), (11, plus[2], 24, 8)]
     for k in range(slabs):
-        width = min(256, coarse.shape[1] - 256 * k)
+        width = min(256, nc - 256 * k)
         slab = coarse[:, 256 * k : 256 * k + width]
         if width < 256:
             slab = jnp.concatenate([slab, jnp.zeros((12, 256 - width), f32)], 1)
@@ -227,17 +298,6 @@
                 base + 16 * k : base + 16 * k + count, :
             ]
     solve[...] = split2(rows[...])
-    line = lax.broadcasted_iota(jnp.int32, (lanes, 1), 0)
-    whole = lax.broadcasted_iota(jnp.int32, (lanes, place.shape[1]), 1)
-    for k in range(sizes[1]):
-        y = jnp.bitwise_xor(gy, k)
-        aim = jnp.where(line >= 30 * levels, nc + line - 30 * levels, -1)
-        for t, (dx, dy) in enumerate(((0, 0), (-1, 0), (1, 0), (0, -1), (0, 1))):
-            inside = (gx + dx >= 0) & (gx + dx < sizes[0]) & (y + dy >= 0) & (y + dy < sizes[1])
-            first = jnp.where(inside, ((gx + dx) * sizes[1] + y + dy - t) * 6 * levels, -6 * nc)
-            aim = jnp.where((line >= t * 6 * levels) & (line < (t + 1) * 6 * levels), line + first, aim)
-        place[k * lanes : k * lanes + lanes, :] = (whole == aim).astype(bf16)
-    part[...] = fold3(partial)
 
 
 def tail(ref, lanes):
@@ -262,11 +322,19 @@
     beside(refs[split:], refs[count:split], total)
 
 
-def place_kernel(count, place, *refs):
-    lanes = refs[0].shape[1]
-    left = jnp.concatenate([split3(tail(part, lanes)) for part in refs[:count]], 1)
-    split = count + (len(refs) - count) // 2
-    beside(refs[split:], refs[count:split], fold3(mm(left, place[...], NN)))
+def place_kernel(sizes, nc, count, *refs):
+    lanes, width = refs[0].shape[1], refs[-1].shape[1]
+    lefts = [split3(tail(part, lanes)) for part in refs[:count]]
+    faces = (len(refs) - count) // 2
+    if (len(refs) - count) % 2:
+        total = jnp.zeros((lefts[0].shape[0], width), f32)
+        for k, left in enumerate(lefts):
+            total += mm(left, place_rows(sizes, nc, lanes, width, k), NN)
+        split = count + faces
+    else:
+        total = mm(jnp.concatenate(lefts, 1), refs[count][...], NN)
+        count, split = count + 1, count + faces
+    beside(refs[split:], refs[count:split], fold3(total))
 
 
 def coarse(whole, parts, solve):
@@ -282,7 +350,7 @@
     return jnp.concatenate([left, left], 1)
 
 
-def apply_factors(residual, pattern, factors, perm, sums, masks, parity, previous, forward, image, sends):
+def apply_factors(residual, pattern, factors, turned, perm, back, sums, masks, parity, previous, forward, image, sends):
     xa, xb, ya, yb, za, zb, part = sends
     lanes = part.shape[1]
     partial = jnp.zeros((48, 2 * lanes), f32)
@@ -299,12 +367,12 @@
                 sides.append(split2(value))
             else:
                 sides.append((-mm(split2(value), perm[s * 3 + j - 3], NN)).astype(bf16))
-        present = [[pattern[s, i, j].astype(f32).astype(bf16) for j in range(6)] for i in range(6)]
+        present = [[pattern[i, s, j].astype(f32).astype(bf16) for j in range(6)] for i in range(6)]
         halves = []
         for i in range(6):
             acc = jnp.zeros((32, 256), f32)
             for j in range(6):
-                acc += mm(sides[j] * present[i][j], factors[s, i, j], NT)
+                acc += mm(sides[j] * present[i][j], turned[s, i, j], NN)
             got = fold2(acc)
             forward[s, i] = got
             square += got * got
@@ -317,11 +385,11 @@
                 acc += mm(halves[i] * present[i][j], factors[s, i, j], NN)
             got = fold2(acc)
             if j >= 3:
-                got = -fold3(mm(split3(got), perm[s * 3 + j - 3], NT))
+                got = -fold3(mm(split3(got), back[s * 3 + j - 3], NN))
             got = masked(got, masks[s][j])
             image[s, j] = got
             faces[s, j] = got
-            partial += mm(split3(got), sums[s * 6 + j], NT)
+            partial += mm(split3(got), sums[s * 6 + j], NN)
     for s in range(2):
         at = slice(256 * s, 256 * s + 256)
         xa[:, at] = pick(parity[0], faces[s, 3], faces[s, 0])
@@ -340,7 +408,7 @@
         out[:, 256:] = total
 
 
-def first_kernel(sizes, count, pattern, factors, perm, lift, sums, solve, start, *refs):
+def first_kernel(sizes, count, pattern, factors, turned, perm, back, lift, sums, solve, start, *refs):
     parity, masks = position(sizes)
     residual, forward, image = refs[count : count + 3]
     left = lift_left(coarse(refs[0], refs[1:count], solve)[1])
@@ -350,7 +418,7 @@
             value = start[s, f] - masked(fold3(mm(left, lift[s * 6 + f], NN)), masks[s][f])
             residual[s, f] = value
             now[s][f] = value
-    apply_factors(now, pattern, factors, perm, sums, masks, parity, None, forward, image, refs[count + 3 :])
+    apply_factors(now, pattern, factors, turned, perm, back, sums, masks, parity, None, forward, image, refs[count + 3 :])
 
 
 def update(sizes, nc, first, faces, parts, state, count):
@@ -397,10 +465,10 @@
 
 
 def middle_kernel(sizes, nc, first, count, *refs):
-    pattern, factors, perm, lift, sums, solve = refs[:6]
-    faces, parts = refs[6:12], refs[12 : 12 + count]
-    residual, forward, image = refs[12 + count : 15 + count]
-    rest = refs[15 + count :]
+    pattern, factors, turned, perm, back, lift, sums, solve = refs[:8]
+    faces, parts = refs[8:14], refs[14 : 14 + count]
+    residual, forward, image = refs[14 + count : 17 + count]
+    rest = refs[17 + count :]
     if first:
         old = None
     else:
@@ -425,7 +493,7 @@
             line = forward[s, f] if first else forward[s, f] + beta * old[2][s, f]
             along[s][f] = line
             new_along[s, f] = line
-    apply_factors(now, pattern, factors, perm, sums, masks, parity, along, new_forward, new_image, rest[8:])
+    apply_factors(now, pattern, factors, turned, perm, back, sums, masks, parity, along, new_forward, new_image, rest[8:])
 
 
 def last_kernel(sizes, nc, count, lift, solve, *refs):
@@ -444,12 +512,17 @@
     return lax.ppermute(values, axis, [(i, i ^ distance) for i in range(lax.axis_size(axis))])
 
 
-def exchange(first, second, axis, alone=None):
+def exchange(first, second, axis, alone=None, ends=True):
     size = lax.axis_size(axis)
     below = swap(first, axis, 1)
     if size == 2:
         return below, below, [below]
-    above = lax.ppermute(second, axis, [(i, (i + 1) % size if i % 2 else (i - 1) % size) for i in range(size)])
+    pairs = [(i, i + 1 if i % 2 else i - 1) for i in range(size)]
+    if ends:
+        pairs = [(i, j % size) for i, j in pairs]
+    else:
+        pairs = [(i, j) for i, j in pairs if 0 <= j < size]
+    above = lax.ppermute(second, axis, pairs)
     others = [below]
     if alone is not None:
         for distance in range(2, size):
@@ -464,85 +537,118 @@
     slabs = -(-nc // 256)
     rhs = dual_rhs.reshape(dual_rhs.shape[2:])
     factors = factors.reshape(factors.shape[2:])
-    pattern = block_pattern.reshape(block_pattern.shape[2:])
-    fmap = face_map.reshape(face_map.shape[2:])
-    modes = rigid_modes.reshape(rigid_modes.shape[2:])
+    pattern = block_pattern.reshape(block_pattern.shape[2:]).transpose(1, 0, 2)
+    fmap = face_map.reshape(face_map.shape[2:]).transpose(1, 0, 2)
+    modes = rigid_modes.reshape(rigid_modes.shape[2:]).transpose(1, 2, 0, 3)
     vmem = pl.BlockSpec(memory_space=pltpu.VMEM)
     smem = pl.BlockSpec(memory_space=pltpu.SMEM)
-    table_bytes = 2 * sizes[1] * column_lanes(2 * sizes[2]) * whole_lanes(nc)
-    params = pltpu.CompilerParams(vmem_limit_bytes=(16 << 20) + table_bytes)
+    params = pltpu.CompilerParams(vmem_limit_bytes=24 << 20)
 
     def shape(*dims, dtype=f32):
         return jax.ShapeDtypeStruct(dims, dtype)
 
-    def call(kernel, outs, ins, first_smem=False, scratch=()):
-        specs = [smem if i == 0 and first_smem else vmem for i in range(len(ins))]
+    anywhere = pl.BlockSpec(memory_space=pl.ANY)
+
+    def call(kernel, outs, ins, specs=None, scratch=(), cost=None):
+        specs = specs or {}
         return pl.pallas_call(
             kernel,
             out_shape=outs,
-            in_specs=specs,
+            in_specs=[specs.get(i, vmem) for i in range(len(ins))],
             out_specs=[vmem] * len(outs),
             scratch_shapes=list(scratch),
             compiler_params=params,
+            cost_estimate=cost,
         )(*ins)
 
     levels = 2 * sizes[2]
     lanes, whole = column_lanes(levels), whole_lanes(nc)
     packs = [shape(48 + 16 * slabs, dofs)] * 4 + [shape(24 + 16 * slabs, dofs)] * 2
-    xa, xb, ya, yb, za, zb = call(pack_kernel, packs, [rhs, modes, fmap, coarse_solve])
-    za, zb, _ = exchange(za, zb, "gz")
-    xa, xb, _ = exchange(xa, xb, "gx")
-    ya, yb, _ = exchange(ya, yb, "gy")
+    raw = [rhs, modes, fmap, coarse_solve]
+    rhs, modes, fmap, coarse_rows, xa, xb, ya, yb, za, zb = call(
+        pack_kernel,
+        [jax.ShapeDtypeStruct(x.shape, x.dtype) for x in raw] + packs,
+        raw,
+        specs={i: anywhere for i in range(4)},
+        scratch=(pltpu.SemaphoreType.DMA((4,)),),
+    )
+    place = []
+    if sizes[1] * lanes * whole <= 1 << 20:
+        place = call(
+            functools.partial(place_table_kernel, sizes, nc, lanes),
+            [shape(sizes[1] * lanes, whole, dtype=bf16)],
+            [],
+            cost=pl.CostEstimate(flops=0, bytes_accessed=4 << 20, transcendentals=0),
+        )
+    za, zb, _ = exchange(za, zb, "gz", ends=False)
+    xa, xb, _ = exchange(xa, xb, "gx", ends=False)
+    ya, yb, _ = exchange(ya, yb, "gy", ends=False)
+    packs = [xa, xb, ya, yb, za, zb]
+    (turned,) = call(
+        turn_kernel,
+        [jax.ShapeDtypeStruct(factors.shape, factors.dtype)],
+        [factors],
+        cost=pl.CostEstimate(flops=0, bytes_accessed=9 << 20, transcendentals=0),
+    )
     faces = shape(2, 6, cases, dofs)
-    perm, lift, sums, start, solve, place, part = call(
+    (touched,) = call(
+        touch_kernel,
+        [shape(8, LANES)],
+        [factors],
+        cost=pl.CostEstimate(flops=0, bytes_accessed=9 << 20, transcendentals=0),
+    )
+    (part,) = call(functools.partial(begin_kernel, sizes), [shape(cases, lanes)], [rhs, modes, fmap, *packs, touched])
+    perm, back, lift, sums, start, solve = call(
         functools.partial(setup_kernel, sizes),
         [
             shape(6, dofs, dofs, dtype=bf16),
+            shape(6, dofs, dofs, dtype=bf16),
             shape(12, 2 * LANES, dofs, dtype=bf16),
-            shape(12, 2 * lanes, dofs, dtype=bf16),
+            shape(12, dofs, 2 * lanes, dtype=bf16),
             faces,
             shape(2 * LANES, 256 * slabs, dtype=bf16),
-            shape(sizes[1] * lanes, whole, dtype=bf16),
-            shape(cases, lanes),
         ],
-        [rhs, modes, fmap, coarse_solve, xa, xb, ya, yb, za, zb],
+        [rhs, modes, fmap, coarse_rows, *packs],
         scratch=(pltpu.VMEM((LANES, dofs), f32), pltpu.VMEM((LANES, 256 * slabs), f32)),
-    )
-
-    def reduce(part, za, zb, along_y, along_x):
+        cost=pl.CostEstimate(flops=0, bytes_accessed=9 << 20, transcendentals=0),
+    )
+
+    def reduce(part, za, zb, along_y, along_x, also=None):
         za, zb, others = exchange(za, zb, "gz", part)
         outs = [shape(cases, face.shape[1] + lanes) for face in along_y] + [shape(cases, lanes)]
         ins = [part, *others, *along_y]
         *along_y, part = call(functools.partial(column_kernel, 1 + len(others)), outs, ins)
         ya, yb, others = exchange(*(along_y or (part, part)), "gy", part)
         outs = [shape(cases, face.shape[1] + whole) for face in along_x] + [shape(cases, whole)]
-        ins = [place, part, *others, *along_x]
-        *along_x, part = call(functools.partial(place_kernel, 1 + len(others)), outs, ins)
+        if also is not None:
+            part, also = lax.optimization_barrier((part, also))
+        ins = [part, *others, *place, *along_x]
+        *along_x, part = call(functools.partial(place_kernel, sizes, nc, 1 + len(others)), outs, ins)
         xa, xb, others = exchange(*(along_x or (part, part)), "gx", part)
-        return [xa, xb, ya, yb, za, zb], [part, *others]
-
-    parts = reduce(part, part, part, (), ())[1]
+        return [xa, xb, ya, yb, za, zb], [part, *others], also
+
+    _, parts, turned = reduce(part, part, part, (), (), turned)
     wide = shape(cases, 2 * dofs)
     sends = [wide] * 4 + [shape(cases, dofs + lanes)] * 2 + [shape(cases, lanes)]
     residual, forward, image, *out = call(
         functools.partial(first_kernel, sizes, len(parts)),
         [faces, faces, faces] + sends,
-        [pattern, factors, perm, lift, sums, solve, start, *parts],
-        first_smem=True,
+        [pattern, factors, turned, perm, back, lift, sums, solve, start, *parts],
+        specs={0: smem},
     )
     old = []
     for iteration in range(ITERS - 1):
         xa, xb, ya, yb, za, zb, part = out
-        got, parts = reduce(part, za, zb, (ya, yb), (xa, xb))
+        got, parts, _ = reduce(part, za, zb, (ya, yb), (xa, xb))
         residual, forward, image, *out = call(
             functools.partial(middle_kernel, sizes, nc, iteration == 0, len(parts)),
             [faces] * 6 + [shape(2, 3, cases, dofs), shape(8, LANES)] + sends,
-            [pattern, factors, perm, lift, sums, solve, *got, *parts, residual, forward, image, *old],
-            first_smem=True,
+            [pattern, factors, turned, perm, back, lift, sums, solve, *got, *parts, residual, forward, image, *old],
+            specs={0: smem},
         )
         old, out = out[:5], out[5:]
     xa, xb, ya, yb, za, zb, part = out
-    got, parts = reduce(part, za, zb, (ya, yb), (xa, xb))
+    got, parts, _ = reduce(part, za, zb, (ya, yb), (xa, xb))
     multipliers, final = call(
         functools.partial(last_kernel, sizes, nc, len(parts)),
         [shape(2, 3, cases, dofs)] * 2,

time: 133 us -> 126 us (0.947)
  waiting for transfers between devices: 42.4 us -> 34.5 us
  starting transfers between devices: 44.6 us -> 46.4 us
  Pallas kernels: 38.4 us -> 36.7 us
    ppermute x28, starting transfers between devices: 21.7 us -> 28.4 us  [swap(): lax.ppermute(values, axis, [(i, i ^ distance) for i in range(lax.axis_siz...]
    ppermute x12, starting transfers between devices: 22.9 us -> 18 us  [exchange(): above = lax.ppermute(second, axis, pairs)]
    ppermute x12, waiting for transfers between devices: 4.91 us -> 0.03 us  [exchange(): above = lax.ppermute(second, axis, pairs)]
    ppermute x28, waiting for transfers between devices: 37.4 us -> 34.5 us  [swap(): lax.ppermute(values, axis, [(i, i ^ distance) for i in range(lax.axis_siz...]
    pallas_call x17 -> x21, Pallas kernels: 38.4 us -> 36.7 us  [call(): pl.pallas_call(kernel, out_shape=outs, in_specs=[specs.get(i, vmem) for i...]
    unnamed x12 -> x14, local copies, waits for them, and re-layouts: 6.91 us -> 6.88 us
  transfers between devices with their start and end apart: 40 -> 40, of which waited for: 20 -> 15; matrix products, arithmetic and copies ran while one was open for 0% -> 0% of each run, Pallas kernels for 0% -> 4%
where the time goes in v3:
time: 126 us; the launch traced here: 125 us
  starting transfers between devices  46.4 us (37%)
  Pallas kernels  36.7 us (29%)
  waiting for transfers between devices  34.5 us (27%)
  local copies, waits for them, and re-layouts  6.88 us (5%)
    pallas_call x21, Pallas kernels, call(): pl.pallas_call(kernel, out_shape=outs, in_specs=[specs.get(i, vmem) for i...  36.7 us
    ppermute x28, waiting for transfers between devices, swap(): lax.ppermute(values, axis, [(i, i ^ distance) for i in range(lax.axis_siz...  34.5 us
    ppermute x28, starting transfers between devices, swap(): lax.ppermute(values, axis, [(i, i ^ distance) for i in range(lax.axis_siz...  28.4 us
    ppermute x12, starting transfers between devices, exchange(): above = lax.ppermute(second, axis, pairs)  18 us
    unnamed x14, local copies, waits for them, and re-layouts  6.88 us
  transfers between devices with their start and end apart: 40, of which 15 were waited for; matrix products, arithmetic and copies ran while one was open for 0% of the time, Pallas kernels for 4%

profile of v3, /device:TPU:0, one launch (start us, length us, event | category | flops | bytes accessed | tf_op | source)
XLA Modules:
  0.0 125.3 jit_solution(2530352729786403400)
XLA Ops:
  0.6 0.9 copy-done.3
  1.5 0.9 copy-done.4
  2.4 0.7 copy-done.5
  3.1 0.7 copy-done.6
  3.8 0.9 shard_map.77
  4.8 3.0 %collective-permute-start = (f32[80,256]{1,0:T(8,128)S(1)}, f32[80,256]{1,0:T(8,128)S(1)}, u32[]{:S(2)}, u32[]{:S(2)}) collective-permute-start(f32[80,256]{1,0:T(8,128)S(1)} %get-tuple-element.100), channel_id=1, source_target_pairs={{0,8},{8,0},{16,24},{24,16},{1,9},{9,1},{17,25},{25,17},{2,10},{10... | collective-permute-start | bytes 245768 | tf_op jit(solution)/shard_map/ppermute | solution.py:512
  7.8 0.7 collective-permute-start.1
  8.4 1.6 %collective-permute-start.2 = (f32[80,256]{1,0:T(8,128)S(1)}, f32[80,256]{1,0:T(8,128)S(1)}, u32[]{:S(2)}, u32[]{:S(2)}) collective-permute-start(f32[80,256]{1,0:T(8,128)S(1)} %get-tuple-element.102), channel_id=1, source_target_pairs={{0,2},{2,0},{4,6},{6,4},{1,3},{3,1},{5,7},{7,5},{8,10},{10,8},{12,... | collective-permute-start | bytes 245768 | tf_op jit(solution)/shard_map/ppermute | solution.py:512
  10.1 0.7 collective-permute-start.3
  10.8 3.7 %copy-done = bf16[1,1,2,6,6,256,256]{6,5,4,3,2,1,0:T(8,128)(2,1)S(1)} copy-done((bf16[1,1,2,6,6,256,256]{6,5,4,3,2,1,0:T(8,128)(2,1)S(1)}, bf16[1,1,2,6,6,256,256]{6,5,4,3,2,1,0:T(8,128)(2,1)}, u32[]{:S(2)}) %copy-start) | copy-done | bytes 9437208
  14.5 1.2 shard_map.80.refs_0_
  15.7 0.5 collective-permute-start.5
  16.2 0.8 collective-permute-done.5.refs_1_
  17.1 2.5 %collective-permute-start.8 = (f32[16,128]{1,0:T(8,128)S(1)}, f32[16,128]{1,0:T(8,128)S(1)}, u32[]{:S(2)}, u32[]{:S(2)}) collective-permute-start(f32[16,128]{1,0:T(8,128)S(1)} %shard_map.81.refs_0_), channel_id=1, source_target_pairs={{0,6},{2,4},{4,2},{6,0},{1,7},{3,5},{5,3},{7,1},{8,14},{10,12},{12... | collective-permute-start | bytes 24584 | tf_op jit(solution)/shard_map/ppermute | solution.py:525
  19.6 3.4 %collective-permute-start.7 = (f32[16,128]{1,0:T(8,128)S(1)}, f32[16,128]{1,0:T(8,128)S(1)}, u32[]{:S(2)}, u32[]{:S(2)}) collective-permute-start(f32[16,128]{1,0:T(8,128)S(1)} %shard_map.81.refs_0_), channel_id=1, source_target_pairs={{0,4},{2,6},{4,0},{6,2},{1,5},{3,7},{5,1},{7,3},{8,12},{10,14},{12... | collective-permute-start | bytes 24584 | tf_op jit(solution)/shard_map/ppermute | solution.py:512
  23.1 2.5 %shard_map.82.turned.refs_2_ = bf16[2,6,6,256,256]{4,3,2,1,0:T(8,128)(2,1)S(1)} custom-call(bf16[2,6,6,256,256]{4,3,2,1,0:T(8,128)(2,1)S(1)} %bitcast.14), custom_call_target="tpu_custom_call" | custom-call | bytes 9437184 | tf_op jit(solution)/shard_map/pallas_call | solution.py:554
  25.6 1.0 collective-permute-done.6.refs_1_
  26.8 1.5 %collective-permute-start.11 = (f32[16,512]{1,0:T(8,128)S(1)}, f32[16,512]{1,0:T(8,128)S(1)}, u32[]{:S(2)}, u32[]{:S(2)}) collective-permute-start(f32[16,512]{1,0:T(8,128)S(1)} %shard_map.84.refs_0_), channel_id=1, source_target_pairs={{0,24},{8,16},{16,8},{24,0},{1,25},{9,17},{17,9},{25,1},{2,26},{10... | collective-permute-start | bytes 98312 | tf_op jit(solution)/shard_map/ppermute | solution.py:525
  28.3 4.2 %collective-permute-start.10 = (f32[16,512]{1,0:T(8,128)S(1)}, f32[16,512]{1,0:T(8,128)S(1)}, u32[]{:S(2)}, u32[]{:S(2)}) collective-permute-start(f32[16,512]{1,0:T(8,128)S(1)} %shard_map.84.refs_0_), channel_id=1, source_target_pairs={{0,16},{8,24},{16,0},{24,8},{1,17},{9,25},{17,1},{25,9},{2,18},{10... | collective-permute-start | bytes 98312 | tf_op jit(solution)/shard_map/ppermute | solution.py:512
  32.5 2.0 %shard_map.78 = (bf16[6,256,256]{2,1,0:T(8,128)(2,1)S(1)}, bf16[6,256,256]{2,1,0:T(8,128)(2,1)S(1)}, bf16[12,256,256]{2,1,0:T(8,128)(2,1)S(1)}, bf16[12,256,256]...) custom-call(f32[2,3,16,256]{3,2,1,0:T(8,128)S(1)} %get-tuple-element.96.rhs, ...), custom_call_target="tpu_custom_call" | custom-call | bytes 9437184 | tf_op jit(solution)/shard_map/pallas_call | solution.py:554
  34.6 1.8 %collective-permute-done.9.refs_1_ = f32[16,512]{1,0:T(8,128)S(1)} collective-permute-done((f32[16,512]{1,0:T(8,128)S(1)}, f32[16,512]{1,0:T(8,128)S(1)}, u32[]{:S(2)}, u32[]{:S(2)}) %collective-permute-start.9) | collective-permute-done | bytes 32800 | tf_op jit(solution)/shard_map/ppermute | solution.py:512
  36.4 6.8 %shard_map.85 = (f32[2,6,16,256]{3,2,1,0:T(8,128)S(1)}, f32[2,6,16,256]{3,2,1,0:T(8,128)S(1)}, f32[2,6,16,256]{3,2,1,0:T(8,128)S(1)}, f32[16,512]{1,0:T(8,128)S(...) custom-call(s32[6,2,6]{2,1,0:T(2,128)S(1)} %bitcast.19, ...), custom_call_target="tpu_custom_call" | custom-call | tf_op jit(solution)/shard_map/pallas_call | solution.py:554
  43.2 1.2 collective-permute-done.12.refs_1_.refs_12_.refs_13_
  44.4 1.1 collective-permute-start.13
  45.5 1.3 %collective-permute-start.15 = (f32[16,640]{1,0:T(8,128)S(1)}, f32[16,640]{1,0:T(8,128)S(1)}, u32[]{:S(2)}, u32[]{:S(2)}) collective-permute-start(f32[16,640]{1,0:T(8,128)S(1)} %get-tuple-element.119), channel_id=1, source_target_pairs={{0,6},{2,4},{4,2},{6,0},{1,7},{3,5},{5,3},{7,1},{8,14},{10,12},{12... | collective-permute-start | bytes 122888 | tf_op jit(solution)/shard_map/ppermute | solution.py:525
  46.9 1.1 collective-permute-start.14
  48.0 3.5 %collective-permute-done.14.refs_2_ = f32[16,128]{1,0:T(8,128)S(1)} collective-permute-done((f32[16,128]{1,0:T(8,128)S(1)}, f32[16,128]{1,0:T(8,128)S(1)}, u32[]{:S(2)}, u32[]{:S(2)}) %collective-permute-start.14) | collective-permute-done | bytes 8224 | tf_op jit(solution)/shard_map/ppermute | solution.py:512
  51.7 0.2 collective-permute-start.16
  51.9 1.2 collective-permute-start.17
  53.2 2.0 %collective-permute-start.18 = (f32[16,512]{1,0:T(8,128)S(1)}, f32[16,512]{1,0:T(8,128)S(1)}, u32[]{:S(2)}, u32[]{:S(2)}) collective-permute-start(f32[16,512]{1,0:T(8,128)S(1)} %get-tuple-element.124.refs_14_), channel_id=1, source_target_pairs={{0,16},{8,24},{16,0},{24,8},{1,17},{9,25},{17,1},{25,9},{2,18},{10... | collective-permute-start | bytes 98312 | tf_op jit(solution)/shard_map/ppermute | solution.py:512
  55.2 2.2 %collective-permute-done.18.refs_16_ = f32[16,512]{1,0:T(8,128)S(1)} collective-permute-done((f32[16,512]{1,0:T(8,128)S(1)}, f32[16,512]{1,0:T(8,128)S(1)}, u32[]{:S(2)}, u32[]{:S(2)}) %collective-permute-start.18) | collective-permute-done | bytes 32800 | tf_op jit(solution)/shard_map/ppermute | solution.py:512
  57.4 7.1 %shard_map.88 = (f32[2,6,16,256]{3,2,1,0:T(8,128)S(1)}, f32[2,6,16,256]{3,2,1,0:T(8,128)S(1)}, f32[2,6,16,256]{3,2,1,0:T(8,128)S(1)}, f32[2,6,16,256]{3,2,1,0:T(...) custom-call(s32[6,2,6]{2,1,0:T(2,128)S(1)} %bitcast.20, ...), custom_call_target="tpu_custom_call" | custom-call | tf_op jit(solution)/shard_map/pallas_call | solution.py:554
  64.5 1.2 collective-permute-done.19.refs_1_.refs_12_.refs_13_
  65.7 0.5 collective-permute-start.20
  66.3 2.0 %collective-permute-start.22 = (f32[16,640]{1,0:T(8,128)S(1)}, f32[16,640]{1,0:T(8,128)S(1)}, u32[]{:S(2)}, u32[]{:S(2)}) collective-permute-start(f32[16,640]{1,0:T(8,128)S(1)} %get-tuple-element.134), channel_id=1, source_target_pairs={{0,6},{2,4},{4,2},{6,0},{1,7},{3,5},{5,3},{7,1},{8,14},{10,12},{12... | collective-permute-start | bytes 122888 | tf_op jit(solution)/shard_map/ppermute | solution.py:525
  68.3 1.0 collective-permute-start.21
  69.3 3.6 %collective-permute-done.21.refs_2_ = f32[16,128]{1,0:T(8,128)S(1)} collective-permute-done((f32[16,128]{1,0:T(8,128)S(1)}, f32[16,128]{1,0:T(8,128)S(1)}, u32[]{:S(2)}, u32[]{:S(2)}) %collective-permute-start.21) | collective-permute-done | bytes 8224 | tf_op jit(solution)/shard_map/ppermute | solution.py:512
  72.9 0.2 shard_map.90
  73.1 1.5 %collective-permute-start.23 = (f32[16,1024]{1,0:T(8,128)S(1)}, f32[16,1024]{1,0:T(8,128)S(1)}, u32[]{:S(2)}, u32[]{:S(2)}) collective-permute-start(f32[16,1024]{1,0:T(8,128)S(1)} %get-tuple-element.137), channel_id=1, source_target_pairs={{0,8},{8,0},{16,24},{24,16},{1,9},{9,1},{17,25},{25,17},{2,10},{10... | collective-permute-start | bytes 196616 | tf_op jit(solution)/shard_map/ppermute | solution.py:512
  74.5 1.7 %collective-permute-start.24 = (f32[16,1024]{1,0:T(8,128)S(1)}, f32[16,1024]{1,0:T(8,128)S(1)}, u32[]{:S(2)}, u32[]{:S(2)}) collective-permute-start(f32[16,1024]{1,0:T(8,128)S(1)} %get-tuple-element.138), channel_id=1, source_target_pairs={{0,24},{8,16},{16,8},{24,0},{1,25},{9,17},{17,9},{25,1},{2,26},{10... | collective-permute-start | bytes 196616 | tf_op jit(solution)/shard_map/ppermute | solution.py:525
  76.2 0.4 collective-permute-start.25
  76.6 3.6 %collective-permute-done.25.refs_16_ = f32[16,512]{1,0:T(8,128)S(1)} collective-permute-done((f32[16,512]{1,0:T(8,128)S(1)}, f32[16,512]{1,0:T(8,128)S(1)}, u32[]{:S(2)}, u32[]{:S(2)}) %collective-permute-start.25) | collective-permute-done | bytes 32800 | tf_op jit(solution)/shard_map/ppermute | solution.py:512
  80.1 6.9 %shard_map.91 = (f32[2,6,16,256]{3,2,1,0:T(8,128)S(1)}, f32[2,6,16,256]{3,2,1,0:T(8,128)S(1)}, f32[2,6,16,256]{3,2,1,0:T(8,128)S(1)}, f32[2,6,16,256]{3,2,1,0:T(...) custom-call(s32[6,2,6]{2,1,0:T(2,128)S(1)} %bitcast.21, ...), custom_call_target="tpu_custom_call" | custom-call | tf_op jit(solution)/shard_map/pallas_call | solution.py:554
  87.1 1.2 collective-permute-done.26.refs_1_.refs_12_.refs_13_
  88.3 1.1 collective-permute-start.27
  89.4 1.4 %collective-permute-start.29 = (f32[16,640]{1,0:T(8,128)S(1)}, f32[16,640]{1,0:T(8,128)S(1)}, u32[]{:S(2)}, u32[]{:S(2)}) collective-permute-start(f32[16,640]{1,0:T(8,128)S(1)} %get-tuple-element.154), channel_id=1, source_target_pairs={{0,6},{2,4},{4,2},{6,0},{1,7},{3,5},{5,3},{7,1},{8,14},{10,12},{12... | collective-permute-start | bytes 122888 | tf_op jit(solution)/shard_map/ppermute | solution.py:525
  90.8 1.0 collective-permute-start.28
  91.8 3.5 %collective-permute-done.28.refs_2_ = f32[16,128]{1,0:T(8,128)S(1)} collective-permute-done((f32[16,128]{1,0:T(8,128)S(1)}, f32[16,128]{1,0:T(8,128)S(1)}, u32[]{:S(2)}, u32[]{:S(2)}) %collective-permute-start.28) | collective-permute-done | bytes 8224 | tf_op jit(solution)/shard_map/ppermute | solution.py:512
  95.4 0.2 shard_map.93
  95.6 0.5 collective-permute-start.30
  96.1 1.3 %collective-permute-start.31 = (f32[16,1024]{1,0:T(8,128)S(1)}, f32[16,1024]{1,0:T(8,128)S(1)}, u32[]{:S(2)}, u32[]{:S(2)}) collective-permute-start(f32[16,1024]{1,0:T(8,128)S(1)} %get-tuple-element.158), channel_id=1, source_target_pairs={{0,24},{8,16},{16,8},{24,0},{1,25},{9,17},{17,9},{25,1},{2,26},{10... | collective-permute-start | bytes 196616 | tf_op jit(solution)/shard_map/ppermute | solution.py:525
  97.4 1.7 %collective-permute-start.32 = (f32[16,512]{1,0:T(8,128)S(1)}, f32[16,512]{1,0:T(8,128)S(1)}, u32[]{:S(2)}, u32[]{:S(2)}) collective-permute-start(f32[16,512]{1,0:T(8,128)S(1)} %get-tuple-element.159.refs_14_), channel_id=1, source_target_pairs={{0,16},{8,24},{16,0},{24,8},{1,17},{9,25},{17,1},{25,9},{2,18},{10... | collective-permute-start | bytes 98312 | tf_op jit(solution)/shard_map/ppermute | solution.py:512
  99.1 2.5 %collective-permute-done.32.refs_16_ = f32[16,512]{1,0:T(8,128)S(1)} collective-permute-done((f32[16,512]{1,0:T(8,128)S(1)}, f32[16,512]{1,0:T(8,128)S(1)}, u32[]{:S(2)}, u32[]{:S(2)}) %collective-permute-start.32) | collective-permute-done | bytes 32800 | tf_op jit(solution)/shard_map/ppermute | solution.py:512
  101.6 7.0 %shard_map.94 = (f32[2,6,16,256]{3,2,1,0:T(8,128)S(1)}, f32[2,6,16,256]{3,2,1,0:T(8,128)S(1)}, f32[2,6,16,256]{3,2,1,0:T(8,128)S(1)}, f32[2,6,16,256]{3,2,1,0:T(...) custom-call(s32[6,2,6]{2,1,0:T(2,128)S(1)} %bitcast.22, ...), custom_call_target="tpu_custom_call" | custom-call | tf_op jit(solution)/shard_map/pallas_call | solution.py:554
  108.5 1.2 collective-permute-done.33.refs_1_.refs_4_.refs_5_
  109.8 0.5 collective-permute-start.34
  110.3 2.0 %collective-permute-start.36 = (f32[16,640]{1,0:T(8,128)S(1)}, f32[16,640]{1,0:T(8,128)S(1)}, u32[]{:S(2)}, u32[]{:S(2)}) collective-permute-start(f32[16,640]{1,0:T(8,128)S(1)} %get-tuple-element.174), channel_id=1, source_target_pairs={{0,6},{2,4},{4,2},{6,0},{1,7},{3,5},{5,3},{7,1},{8,14},{10,12},{12... | collective-permute-start | bytes 122888 | tf_op jit(solution)/shard_map/ppermute | solution.py:525
  112.3 1.0 collective-permute-start.35
  113.3 3.6 %collective-permute-done.35.refs_2_ = f32[16,128]{1,0:T(8,128)S(1)} collective-permute-done((f32[16,128]{1,0:T(8,128)S(1)}, f32[16,128]{1,0:T(8,128)S(1)}, u32[]{:S(2)}, u32[]{:S(2)}) %collective-permute-start.35) | collective-permute-done | bytes 8224 | tf_op jit(solution)/shard_map/ppermute | solution.py:512
  117.1 1.6 %collective-permute-start.37 = (f32[16,1024]{1,0:T(8,128)S(1)}, f32[16,1024]{1,0:T(8,128)S(1)}, u32[]{:S(2)}, u32[]{:S(2)}) collective-permute-start(f32[16,1024]{1,0:T(8,128)S(1)} %get-tuple-element.177), channel_id=1, source_target_pairs={{0,8},{8,0},{16,24},{24,16},{1,9},{9,1},{17,25},{25,17},{2,10},{10... | collective-permute-start | bytes 196616 | tf_op jit(solution)/shard_map/ppermute | solution.py:512
  118.6 1.6 %collective-permute-start.38 = (f32[16,1024]{1,0:T(8,128)S(1)}, f32[16,1024]{1,0:T(8,128)S(1)}, u32[]{:S(2)}, u32[]{:S(2)}) collective-permute-start(f32[16,1024]{1,0:T(8,128)S(1)} %get-tuple-element.178), channel_id=1, source_target_pairs={{0,24},{8,16},{16,8},{24,0},{1,25},{9,17},{17,9},{25,1},{2,26},{10... | collective-permute-start | bytes 196616 | tf_op jit(solution)/shard_map/ppermute | solution.py:525
  120.2 0.4 collective-permute-start.39
  120.6 3.6 %collective-permute-done.39.refs_8_ = f32[16,512]{1,0:T(8,128)S(1)} collective-permute-done((f32[16,512]{1,0:T(8,128)S(1)}, f32[16,512]{1,0:T(8,128)S(1)}, u32[]{:S(2)}, u32[]{:S(2)}) %collective-permute-start.39) | collective-permute-done | bytes 32800 | tf_op jit(solution)/shard_map/ppermute | solution.py:512
  124.1 1.2 shard_map.97
  (51 shorter events, 0.9 us)
Async XLA Ops:
  0.6 0.9 copy-start.3
  1.5 0.9 copy-start.4
  2.4 0.7 copy-start.5
  3.1 0.7 copy-start.6
  4.8 9.7 %collective-permute-start = (f32[80,256]{1,0:T(8,128)S(1)}, f32[80,256]{1,0:T(8,128)S(1)}, u32[]{:S(2)}, u32[]{:S(2)}) collective-permute-start(f32[80,256]{1,0:T(8,128)S(1)} %get-tuple-element.100), channel_id=1, source_target_pairs={{0,8},{8,0},{16,24},{24,16},{1,9},{9,1},{17,25},{25,17},{2,10},{10... | collective-permute-start | bytes 245768 | tf_op jit(solution)/shard_map/ppermute | solution.py:512
  7.8 6.7 %collective-permute-start.1 = (f32[80,256]{1,0:T(8,128)S(1)}, f32[80,256]{1,0:T(8,128)S(1)}, u32[]{:S(2)}, u32[]{:S(2)}) collective-permute-start(f32[80,256]{1,0:T(8,128)S(1)} %get-tuple-element.101), channel_id=1, source_target_pairs={{8,16},{16,8},{9,17},{17,9},{10,18},{18,10},{11,19},{19,11},{12,20... | collective-permute-start | bytes 245768 | tf_op jit(solution)/shard_map/ppermute | solution.py:525
  8.4 6.1 %collective-permute-start.2 = (f32[80,256]{1,0:T(8,128)S(1)}, f32[80,256]{1,0:T(8,128)S(1)}, u32[]{:S(2)}, u32[]{:S(2)}) collective-permute-start(f32[80,256]{1,0:T(8,128)S(1)} %get-tuple-element.102), channel_id=1, source_target_pairs={{0,2},{2,0},{4,6},{6,4},{1,3},{3,1},{5,7},{7,5},{8,10},{10,8},{12,... | collective-permute-start | bytes 245768 | tf_op jit(solution)/shard_map/ppermute | solution.py:512
  10.1 4.5 %collective-permute-start.3 = (f32[80,256]{1,0:T(8,128)S(1)}, f32[80,256]{1,0:T(8,128)S(1)}, u32[]{:S(2)}, u32[]{:S(2)}) collective-permute-start(f32[80,256]{1,0:T(8,128)S(1)} %get-tuple-element.103), channel_id=1, source_target_pairs={{2,4},{4,2},{3,5},{5,3},{10,12},{12,10},{11,13},{13,11},{18,20},{2... | collective-permute-start | bytes 245768 | tf_op jit(solution)/shard_map/ppermute | solution.py:525
  10.7 3.8 %collective-permute-start.4 = (f32[56,256]{1,0:T(8,128)S(1)}, f32[56,256]{1,0:T(8,128)S(1)}, u32[]{:S(2)}, u32[]{:S(2)}) collective-permute-start(f32[56,256]{1,0:T(8,128)S(1)} %get-tuple-element.104), channel_id=1, source_target_pairs={{0,1},{1,0},{2,3},{3,2},{4,5},{5,4},{6,7},{7,6},{8,9},{9,8},{10,11... | collective-permute-start | bytes 172040 | tf_op jit(solution)/shard_map/ppermute | solution.py:512
  10.8 3.7 %copy-start = (bf16[1,1,2,6,6,256,256]{6,5,4,3,2,1,0:T(8,128)(2,1)S(1)}, bf16[1,1,2,6,6,256,256]{6,5,4,3,2,1,0:T(8,128)(2,1)}, u32[]{:S(2)}) copy-start(bf16[1,1,2,6,6,256,256]{6,5,4,3,2,1,0:T(8,128)(2,1)} %param.7) | copy-start | bytes 28311556
  14.5 8.6 %copy-start.1 = (bf16[1,1,2,6,6,256,256]{6,5,4,3,2,1,0:T(8,128)(2,1)S(1)}, bf16[1,1,2,6,6,256,256]{6,5,4,3,2,1,0:T(8,128)(2,1)}, u32[]{:S(2)}) copy-start(bf16[1,1,2,6,6,256,256]{6,5,4,3,2,1,0:T(8,128)(2,1)} %param.7) | copy-start | bytes 28311556
  15.7 1.3 %collective-permute-start.5 = (f32[16,128]{1,0:T(8,128)S(1)}, f32[16,128]{1,0:T(8,128)S(1)}, u32[]{:S(2)}, u32[]{:S(2)}) collective-permute-start(f32[16,128]{1,0:T(8,128)S(1)} %shard_map.80.refs_0_), channel_id=1, source_target_pairs={{0,1},{1,0},{2,3},{3,2},{4,5},{5,4},{6,7},{7,6},{8,9},{9,8},{10,11... | collective-permute-start | bytes 24584 | tf_op jit(solution)/shard_map/ppermute | solution.py:512
  17.1 8.5 %collective-permute-start.8 = (f32[16,128]{1,0:T(8,128)S(1)}, f32[16,128]{1,0:T(8,128)S(1)}, u32[]{:S(2)}, u32[]{:S(2)}) collective-permute-start(f32[16,128]{1,0:T(8,128)S(1)} %shard_map.81.refs_0_), channel_id=1, source_target_pairs={{0,6},{2,4},{4,2},{6,0},{1,7},{3,5},{5,3},{7,1},{8,14},{10,12},{12... | collective-permute-start | bytes 24584 | tf_op jit(solution)/shard_map/ppermute | solution.py:525
  19.6 6.0 %collective-permute-start.7 = (f32[16,128]{1,0:T(8,128)S(1)}, f32[16,128]{1,0:T(8,128)S(1)}, u32[]{:S(2)}, u32[]{:S(2)}) collective-permute-start(f32[16,128]{1,0:T(8,128)S(1)} %shard_map.81.refs_0_), channel_id=1, source_target_pairs={{0,4},{2,6},{4,0},{6,2},{1,5},{3,7},{5,1},{7,3},{8,12},{10,14},{12... | collective-permute-start | bytes 24584 | tf_op jit(solution)/shard_map/ppermute | solution.py:512
  22.9 3.7 %collective-permute-start.6 = (f32[16,128]{1,0:T(8,128)S(1)}, f32[16,128]{1,0:T(8,128)S(1)}, u32[]{:S(2)}, u32[]{:S(2)}) collective-permute-start(f32[16,128]{1,0:T(8,128)S(1)} %shard_map.81.refs_0_), channel_id=1, source_target_pairs={{0,2},{2,0},{4,6},{6,4},{1,3},{3,1},{5,7},{7,5},{8,10},{10,8},{12,... | collective-permute-start | bytes 24584 | tf_op jit(solution)/shard_map/ppermute | solution.py:512
  23.1 13.3 %copy-start.2 = (s32[1,1,2,6,6]{4,2,3,1,0:T(2,128)S(1)}, s32[1,1,2,6,6]{4,2,3,1,0:T(2,128)}, u32[]{:S(2)}) copy-start(s32[1,1,2,6,6]{4,2,3,1,0:T(2,128)} %param.8) | copy-start | bytes 868
  26.8 7.8 %collective-permute-start.11 = (f32[16,512]{1,0:T(8,128)S(1)}, f32[16,512]{1,0:T(8,128)S(1)}, u32[]{:S(2)}, u32[]{:S(2)}) collective-permute-start(f32[16,512]{1,0:T(8,128)S(1)} %shard_map.84.refs_0_), channel_id=1, source_target_pairs={{0,24},{8,16},{16,8},{24,0},{1,25},{9,17},{17,9},{25,1},{2,26},{10... | collective-permute-start | bytes 98312 | tf_op jit(solution)/shard_map/ppermute | solution.py:525
  28.3 6.3 %collective-permute-start.10 = (f32[16,512]{1,0:T(8,128)S(1)}, f32[16,512]{1,0:T(8,128)S(1)}, u32[]{:S(2)}, u32[]{:S(2)}) collective-permute-start(f32[16,512]{1,0:T(8,128)S(1)} %shard_map.84.refs_0_), channel_id=1, source_target_pairs={{0,16},{8,24},{16,0},{24,8},{1,17},{9,25},{17,1},{25,9},{2,18},{10... | collective-permute-start | bytes 98312 | tf_op jit(solution)/shard_map/ppermute | solution.py:512
  32.5 3.9 %collective-permute-start.9 = (f32[16,512]{1,0:T(8,128)S(1)}, f32[16,512]{1,0:T(8,128)S(1)}, u32[]{:S(2)}, u32[]{:S(2)}) collective-permute-start(f32[16,512]{1,0:T(8,128)S(1)} %shard_map.84.refs_0_), channel_id=1, source_target_pairs={{0,8},{8,0},{16,24},{24,16},{1,9},{9,1},{17,25},{25,17},{2,10},{10... | collective-permute-start | bytes 98312 | tf_op jit(solution)/shard_map/ppermute | solution.py:512
  43.2 1.2 collective-permute-start.12
  44.4 7.1 %collective-permute-start.13 = (f32[16,640]{1,0:T(8,128)S(1)}, f32[16,640]{1,0:T(8,128)S(1)}, u32[]{:S(2)}, u32[]{:S(2)}) collective-permute-start(f32[16,640]{1,0:T(8,128)S(1)} %get-tuple-element.118), channel_id=1, source_target_pairs={{0,2},{2,0},{4,6},{6,4},{1,3},{3,1},{5,7},{7,5},{8,10},{10,8},{12,... | collective-permute-start | bytes 122888 | tf_op jit(solution)/shard_map/ppermute | solution.py:512
  45.5 6.0 %collective-permute-start.15 = (f32[16,640]{1,0:T(8,128)S(1)}, f32[16,640]{1,0:T(8,128)S(1)}, u32[]{:S(2)}, u32[]{:S(2)}) collective-permute-start(f32[16,640]{1,0:T(8,128)S(1)} %get-tuple-element.119), channel_id=1, source_target_pairs={{0,6},{2,4},{4,2},{6,0},{1,7},{3,5},{5,3},{7,1},{8,14},{10,12},{12... | collective-permute-start | bytes 122888 | tf_op jit(solution)/shard_map/ppermute | solution.py:525
  46.9 4.6 %collective-permute-start.14 = (f32[16,128]{1,0:T(8,128)S(1)}, f32[16,128]{1,0:T(8,128)S(1)}, u32[]{:S(2)}, u32[]{:S(2)}) collective-permute-start(f32[16,128]{1,0:T(8,128)S(1)} %get-tuple-element.117.refs_0_), channel_id=1, source_target_pairs={{0,4},{2,6},{4,0},{6,2},{1,5},{3,7},{5,1},{7,3},{8,12},{10,14},{12... | collective-permute-start | bytes 24584 | tf_op jit(solution)/shard_map/ppermute | solution.py:512
  51.7 5.8 %collective-permute-start.16 = (f32[16,1024]{1,0:T(8,128)S(1)}, f32[16,1024]{1,0:T(8,128)S(1)}, u32[]{:S(2)}, u32[]{:S(2)}) collective-permute-start(f32[16,1024]{1,0:T(8,128)S(1)} %get-tuple-element.122), channel_id=1, source_target_pairs={{0,8},{8,0},{16,24},{24,16},{1,9},{9,1},{17,25},{25,17},{2,10},{10... | collective-permute-start | bytes 196616 | tf_op jit(solution)/shard_map/ppermute | solution.py:512
  51.9 5.5 %collective-permute-start.17 = (f32[16,1024]{1,0:T(8,128)S(1)}, f32[16,1024]{1,0:T(8,128)S(1)}, u32[]{:S(2)}, u32[]{:S(2)}) collective-permute-start(f32[16,1024]{1,0:T(8,128)S(1)} %get-tuple-element.123), channel_id=1, source_target_pairs={{0,24},{8,16},{16,8},{24,0},{1,25},{9,17},{17,9},{25,1},{2,26},{10... | collective-permute-start | bytes 196616 | tf_op jit(solution)/shard_map/ppermute | solution.py:525
  53.2 4.3 %collective-permute-start.18 = (f32[16,512]{1,0:T(8,128)S(1)}, f32[16,512]{1,0:T(8,128)S(1)}, u32[]{:S(2)}, u32[]{:S(2)}) collective-permute-start(f32[16,512]{1,0:T(8,128)S(1)} %get-tuple-element.124.refs_14_), channel_id=1, source_target_pairs={{0,16},{8,24},{16,0},{24,8},{1,17},{9,25},{17,1},{25,9},{2,18},{10... | collective-permute-start | bytes 98312 | tf_op jit(solution)/shard_map/ppermute | solution.py:512
  64.5 1.2 collective-permute-start.19
  65.7 7.1 %collective-permute-start.20 = (f32[16,640]{1,0:T(8,128)S(1)}, f32[16,640]{1,0:T(8,128)S(1)}, u32[]{:S(2)}, u32[]{:S(2)}) collective-permute-start(f32[16,640]{1,0:T(8,128)S(1)} %get-tuple-element.133), channel_id=1, source_target_pairs={{0,2},{2,0},{4,6},{6,4},{1,3},{3,1},{5,7},{7,5},{8,10},{10,8},{12,... | collective-permute-start | bytes 122888 | tf_op jit(solution)/shard_map/ppermute | solution.py:512
  66.3 6.6 %collective-permute-start.22 = (f32[16,640]{1,0:T(8,128)S(1)}, f32[16,640]{1,0:T(8,128)S(1)}, u32[]{:S(2)}, u32[]{:S(2)}) collective-permute-start(f32[16,640]{1,0:T(8,128)S(1)} %get-tuple-element.134), channel_id=1, source_target_pairs={{0,6},{2,4},{4,2},{6,0},{1,7},{3,5},{5,3},{7,1},{8,14},{10,12},{12... | collective-permute-start | bytes 122888 | tf_op jit(solution)/shard_map/ppermute | solution.py:525
  68.3 4.5 %collective-permute-start.21 = (f32[16,128]{1,0:T(8,128)S(1)}, f32[16,128]{1,0:T(8,128)S(1)}, u32[]{:S(2)}, u32[]{:S(2)}) collective-permute-start(f32[16,128]{1,0:T(8,128)S(1)} %get-tuple-element.132.refs_0_), channel_id=1, source_target_pairs={{0,4},{2,6},{4,0},{6,2},{1,5},{3,7},{5,1},{7,3},{8,12},{10,14},{12... | collective-permute-start | bytes 24584 | tf_op jit(solution)/shard_map/ppermute | solution.py:512
  73.1 7.1 %collective-permute-start.23 = (f32[16,1024]{1,0:T(8,128)S(1)}, f32[16,1024]{1,0:T(8,128)S(1)}, u32[]{:S(2)}, u32[]{:S(2)}) collective-permute-start(f32[16,1024]{1,0:T(8,128)S(1)} %get-tuple-element.137), channel_id=1, source_target_pairs={{0,8},{8,0},{16,24},{24,16},{1,9},{9,1},{17,25},{25,17},{2,10},{10... | collective-permute-start | bytes 196616 | tf_op jit(solution)/shard_map/ppermute | solution.py:512
  74.5 5.6 %collective-permute-start.24 = (f32[16,1024]{1,0:T(8,128)S(1)}, f32[16,1024]{1,0:T(8,128)S(1)}, u32[]{:S(2)}, u32[]{:S(2)}) collective-permute-start(f32[16,1024]{1,0:T(8,128)S(1)} %get-tuple-element.138), channel_id=1, source_target_pairs={{0,24},{8,16},{16,8},{24,0},{1,25},{9,17},{17,9},{25,1},{2,26},{10... | collective-permute-start | bytes 196616 | tf_op jit(solution)/shard_map/ppermute | solution.py:525
  76.2 3.9 %collective-permute-start.25 = (f32[16,512]{1,0:T(8,128)S(1)}, f32[16,512]{1,0:T(8,128)S(1)}, u32[]{:S(2)}, u32[]{:S(2)}) collective-permute-start(f32[16,512]{1,0:T(8,128)S(1)} %get-tuple-element.139.refs_14_), channel_id=1, source_target_pairs={{0,16},{8,24},{16,0},{24,8},{1,17},{9,25},{17,1},{25,9},{2,18},{10... | collective-permute-start | bytes 98312 | tf_op jit(solution)/shard_map/ppermute | solution.py:512
  87.1 1.2 collective-permute-start.26
  88.3 7.1 %collective-permute-start.27 = (f32[16,640]{1,0:T(8,128)S(1)}, f32[16,640]{1,0:T(8,128)S(1)}, u32[]{:S(2)}, u32[]{:S(2)}) collective-permute-start(f32[16,640]{1,0:T(8,128)S(1)} %get-tuple-element.153), channel_id=1, source_target_pairs={{0,2},{2,0},{4,6},{6,4},{1,3},{3,1},{5,7},{7,5},{8,10},{10,8},{12,... | collective-permute-start | bytes 122888 | tf_op jit(solution)/shard_map/ppermute | solution.py:512
  89.4 6.0 %collective-permute-start.29 = (f32[16,640]{1,0:T(8,128)S(1)}, f32[16,640]{1,0:T(8,128)S(1)}, u32[]{:S(2)}, u32[]{:S(2)}) collective-permute-start(f32[16,640]{1,0:T(8,128)S(1)} %get-tuple-element.154), channel_id=1, source_target_pairs={{0,6},{2,4},{4,2},{6,0},{1,7},{3,5},{5,3},{7,1},{8,14},{10,12},{12... | collective-permute-start | bytes 122888 | tf_op jit(solution)/shard_map/ppermute | solution.py:525
  90.8 4.6 %collective-permute-start.28 = (f32[16,128]{1,0:T(8,128)S(1)}, f32[16,128]{1,0:T(8,128)S(1)}, u32[]{:S(2)}, u32[]{:S(2)}) collective-permute-start(f32[16,128]{1,0:T(8,128)S(1)} %get-tuple-element.152.refs_0_), channel_id=1, source_target_pairs={{0,4},{2,6},{4,0},{6,2},{1,5},{3,7},{5,1},{7,3},{8,12},{10,14},{12... | collective-permute-start | bytes 24584 | tf_op jit(solution)/shard_map/ppermute | solution.py:512
  95.6 6.0 %collective-permute-start.30 = (f32[16,1024]{1,0:T(8,128)S(1)}, f32[16,1024]{1,0:T(8,128)S(1)}, u32[]{:S(2)}, u32[]{:S(2)}) collective-permute-start(f32[16,1024]{1,0:T(8,128)S(1)} %get-tuple-element.157), channel_id=1, source_target_pairs={{0,8},{8,0},{16,24},{24,16},{1,9},{9,1},{17,25},{25,17},{2,10},{10... | collective-permute-start | bytes 196616 | tf_op jit(solution)/shard_map/ppermute | solution.py:512
  96.1 5.5 %collective-permute-start.31 = (f32[16,1024]{1,0:T(8,128)S(1)}, f32[16,1024]{1,0:T(8,128)S(1)}, u32[]{:S(2)}, u32[]{:S(2)}) collective-permute-start(f32[16,1024]{1,0:T(8,128)S(1)} %get-tuple-element.158), channel_id=1, source_target_pairs={{0,24},{8,16},{16,8},{24,0},{1,25},{9,17},{17,9},{25,1},{2,26},{10... | collective-permute-start | bytes 196616 | tf_op jit(solution)/shard_map/ppermute | solution.py:525
  97.4 4.2 %collective-permute-start.32 = (f32[16,512]{1,0:T(8,128)S(1)}, f32[16,512]{1,0:T(8,128)S(1)}, u32[]{:S(2)}, u32[]{:S(2)}) collective-permute-start(f32[16,512]{1,0:T(8,128)S(1)} %get-tuple-element.159.refs_14_), channel_id=1, source_target_pairs={{0,16},{8,24},{16,0},{24,8},{1,17},{9,25},{17,1},{25,9},{2,18},{10... | collective-permute-start | bytes 98312 | tf_op jit(solution)/shard_map/ppermute | solution.py:512
  108.5 1.2 collective-permute-start.33
  109.8 7.1 %collective-permute-start.34 = (f32[16,640]{1,0:T(8,128)S(1)}, f32[16,640]{1,0:T(8,128)S(1)}, u32[]{:S(2)}, u32[]{:S(2)}) collective-permute-start(f32[16,640]{1,0:T(8,128)S(1)} %get-tuple-element.173), channel_id=1, source_target_pairs={{0,2},{2,0},{4,6},{6,4},{1,3},{3,1},{5,7},{7,5},{8,10},{10,8},{12,... | collective-permute-start | bytes 122888 | tf_op jit(solution)/shard_map/ppermute | solution.py:512
  110.3 6.6 %collective-permute-start.36 = (f32[16,640]{1,0:T(8,128)S(1)}, f32[16,640]{1,0:T(8,128)S(1)}, u32[]{:S(2)}, u32[]{:S(2)}) collective-permute-start(f32[16,640]{1,0:T(8,128)S(1)} %get-tuple-element.174), channel_id=1, source_target_pairs={{0,6},{2,4},{4,2},{6,0},{1,7},{3,5},{5,3},{7,1},{8,14},{10,12},{12... | collective-permute-start | bytes 122888 | tf_op jit(solution)/shard_map/ppermute | solution.py:525
  112.3 4.5 %collective-permute-start.35 = (f32[16,128]{1,0:T(8,128)S(1)}, f32[16,128]{1,0:T(8,128)S(1)}, u32[]{:S(2)}, u32[]{:S(2)}) collective-permute-start(f32[16,128]{1,0:T(8,128)S(1)} %get-tuple-element.172.refs_0_), channel_id=1, source_target_pairs={{0,4},{2,6},{4,0},{6,2},{1,5},{3,7},{5,1},{7,3},{8,12},{10,14},{12... | collective-permute-start | bytes 24584 | tf_op jit(solution)/shard_map/ppermute | solution.py:512
  117.1 7.1 %collective-permute-start.37 = (f32[16,1024]{1,0:T(8,128)S(1)}, f32[16,1024]{1,0:T(8,128)S(1)}, u32[]{:S(2)}, u32[]{:S(2)}) collective-permute-start(f32[16,1024]{1,0:T(8,128)S(1)} %get-tuple-element.177), channel_id=1, source_target_pairs={{0,8},{8,0},{16,24},{24,16},{1,9},{9,1},{17,25},{25,17},{2,10},{10... | collective-permute-start | bytes 196616 | tf_op jit(solution)/shard_map/ppermute | solution.py:512
  118.6 5.5 %collective-permute-start.38 = (f32[16,1024]{1,0:T(8,128)S(1)}, f32[16,1024]{1,0:T(8,128)S(1)}, u32[]{:S(2)}, u32[]{:S(2)}) collective-permute-start(f32[16,1024]{1,0:T(8,128)S(1)} %get-tuple-element.178), channel_id=1, source_target_pairs={{0,24},{8,16},{16,8},{24,0},{1,25},{9,17},{17,9},{25,1},{2,26},{10... | collective-permute-start | bytes 196616 | tf_op jit(solution)/shard_map/ppermute | solution.py:525
  120.2 3.9 %collective-permute-start.39 = (f32[16,512]{1,0:T(8,128)S(1)}, f32[16,512]{1,0:T(8,128)S(1)}, u32[]{:S(2)}, u32[]{:S(2)}) collective-permute-start(f32[16,512]{1,0:T(8,128)S(1)} %get-tuple-element.179.refs_6_), channel_id=1, source_target_pairs={{0,16},{8,24},{16,0},{24,8},{1,17},{9,25},{17,1},{25,9},{2,18},{10... | collective-permute-start | bytes 98312 | tf_op jit(solution)/shard_map/ppermute | solution.py:512

commit v4 on v3

--- a/solution.py
+++ b/solution.py
@@ -224,7 +224,7 @@
 
 
 def setup_kernel(sizes, rhs, modes, fmap, coarse, xa, xb, ya, yb, za, zb, *refs):
-    perm, back, lift, sums, start, solve, work, rows = refs
+    perm, back, lift, sums, start, solve, pairs, work, rows = refs
     parity, _ = position((1, 1, 1))
     nc = coarse.shape[1]
     slabs = -(-nc // 256)
@@ -271,6 +271,7 @@
             work[at : at + 8, :] = jnp.zeros((8, 256), f32)
             work[n : n + 8, :] = jnp.zeros((8, 256), f32)
             pair = split2(jnp.concatenate([own, other], 0))
+            pairs[s * 6 + f] = pair
             level = 2 * gz + s
             if d == 2:
                 target = (level + (1 if f == 2 else -1)) * 6
@@ -350,7 +351,68 @@
     return jnp.concatenate([left, left], 1)
 
 
-def apply_factors(residual, pattern, factors, turned, perm, back, sums, masks, parity, previous, forward, image, sends):
+def forward_faces(faces, js, pattern, turned, perm):
+    sums = {}
+    for s in range(2):
+        sides = {}
+        for j in js:
+            rows = faces[s, j]
+            sides[j] = rows if j < 3 else (-mm(rows, perm[s * 3 + j - 3], NN)).astype(bf16)
+        for i in range(6):
+            acc = jnp.zeros((32, 256), f32)
+            for j in js:
+                acc += mm(sides[j] * pattern[i, s, j].astype(f32).astype(bf16), turned[s, i, j], NN)
+            sums[s, i] = acc
+    return sums
+
+
+def lifted_kernel(sizes, pattern, turned, perm, pairs, out, work):
+    _, masks = position(sizes)
+    for s in range(2):
+        for i in range(6):
+            work[s * 6 + i] = jnp.zeros((LANES, 256), f32)
+    for j in range(6):
+        faces = {}
+        for s in range(2):
+            rows = pairs[s * 6 + j]
+            faces[s, j] = rows if masks[s][j] is None else (rows.astype(f32) * masks[s][j]).astype(bf16)
+        sums = forward_faces(faces, (j,), pattern, turned, perm)
+        for s in range(2):
+            at, n = own_slot(s) * SLOT, nbr_slot(s, j) * SLOT
+            for i in range(6):
+                got = fold2(sums[s, i])
+                work[s * 6 + i, at : at + 8, :] += got[:8]
+                work[s * 6 + i, n : n + 8, :] += got[8:]
+    for k in range(12):
+        out[k] = split2(work[k])
+
+
+def sum_of_sides(s, f, image, pair, parity, mask):
+    d = f % 3
+    if pair is None:
+        other = image[1 - s, 5 if f == 2 else 2]
+    else:
+        at = 256 * s if d < 2 else 0
+        va, vb = (face[:, at : at + 256] for face in pair)
+        other = pick(parity[d], vb, va) if f < 3 else pick(parity[d], va, vb)
+    return masked(image[s, f] + other, mask)
+
+
+def early_kernel(sizes, pattern, turned, perm, image, ya, yb, za, zb, out):
+    parity, masks = position(sizes)
+    faces = {}
+    for s in range(2):
+        for f in (1, 2, 4, 5):
+            inner = f % 3 == 2 and (s == 0) == (f == 2)
+            pair = None if inner else (ya, yb) if f % 3 == 1 else (za, zb)
+            faces[s, f] = split2(sum_of_sides(s, f, image, pair, parity, masks[s][f]))
+    sums = forward_faces(faces, (1, 2, 4, 5), pattern, turned, perm)
+    for s in range(2):
+        for i in range(6):
+            out[s, i] = fold2(sums[s, i])
+
+
+def apply_factors(residual, pattern, factors, turned, perm, back, sums, masks, parity, previous, forward, image, sends, given=None):
     xa, xb, ya, yb, za, zb, part = sends
     lanes = part.shape[1]
     partial = jnp.zeros((48, 2 * lanes), f32)
@@ -365,15 +427,18 @@
             if j < 3:
                 own_sum += value * value
                 sides.append(split2(value))
-            else:
+            elif given is None:
                 sides.append((-mm(split2(value), perm[s * 3 + j - 3], NN)).astype(bf16))
         present = [[pattern[i, s, j].astype(f32).astype(bf16) for j in range(6)] for i in range(6)]
         halves = []
         for i in range(6):
-            acc = jnp.zeros((32, 256), f32)
-            for j in range(6):
-                acc += mm(sides[j] * present[i][j], turned[s, i, j], NN)
-            got = fold2(acc)
+            if given is None:
+                acc = jnp.zeros((32, 256), f32)
+                for j in range(6):
+                    acc += mm(sides[j] * present[i][j], turned[s, i, j], NN)
+                got = fold2(acc)
+            else:
+                got = given[s, i]
             forward[s, i] = got
             square += got * got
             if previous is not None:
@@ -436,22 +501,20 @@
     if first:
         beta = None
     else:
-        direction, moved, along, multipliers, scalars = old
+        direction, moved, along, multipliers, scalars = old[:5]
         beta = rho / scalars[0:1, 0:1]
         curvature = curvature + 2.0 * beta * scalar(2) + beta * beta * scalars[1:2, 0:1]
     step = rho / curvature
-    out = {}
+    out, jumps = {}, {}
     for s in range(2):
         for f in range(count):
             d = f % 3
-            if d == 2 and (s == 0) == (f == 2):
-                other = image[1 - s, 5 if f == 2 else 2]
-            else:
-                at = 256 * s if d < 2 else 0
-                va, vb = (face[:, at : at + 256] for face in faces[2 * d : 2 * d + 2])
-                other = pick(parity[d], vb, va) if f < 3 else pick(parity[d], va, vb)
-            change = image[s, f] + other - fold3(mm(left, lift[s * 6 + f], NN))
-            change = masked(change, masks[s][f])
+            inner = d == 2 and (s == 0) == (f == 2)
+            pair = None if inner else faces[2 * d : 2 * d + 2]
+            change = sum_of_sides(s, f, image, pair, parity, masks[s][f])
+            if d == 0:
+                jumps[s, f] = split2(change)
+            change -= masked(fold3(mm(left, lift[s * 6 + f], NN)), masks[s][f])
             value = residual[s, f]
             towards = value
             if not first:
@@ -461,22 +524,32 @@
             if f < 3:
                 gain = step * towards
                 out[s, f] += (gain if first else multipliers[s, f] + gain,)
-    return parity, masks, beta, rho, curvature, out
+    return parity, masks, beta, rho, curvature, out, left, step, jumps
 
 
 def middle_kernel(sizes, nc, first, count, *refs):
-    pattern, factors, turned, perm, back, lift, sums, solve = refs[:8]
-    faces, parts = refs[8:14], refs[14 : 14 + count]
-    residual, forward, image = refs[14 + count : 17 + count]
-    rest = refs[17 + count :]
+    pattern, factors, turned, perm, back, lift, sums, solve, lifted, early = refs[:10]
+    faces, parts = refs[10:16], refs[16 : 16 + count]
+    residual, forward, image = refs[16 + count : 19 + count]
+    rest = refs[19 + count :]
     if first:
         old = None
     else:
-        old, rest = rest[:5], rest[5:]
+        old, rest = rest[:6], rest[6:]
     new_residual, new_forward, new_image, new_direction, new_moved, new_along, new_multipliers, new_scalars = rest[:8]
-    parity, masks, beta, rho, curvature, out = update(
+    new_pushed = rest[8]
+    parity, masks, beta, rho, curvature, out, left, step, jumps = update(
         sizes, nc, first, faces, parts, (residual, forward, image, lift, solve, old), 6
     )
+    sides = forward_faces(jumps, (0, 3), pattern, turned, perm)
+    given = {}
+    for s in range(2):
+        for i in range(6):
+            pushed = early[s, i] + fold2(sides[s, i]) - fold3(mm(left, lifted[s * 6 + i], NN))
+            if not first:
+                pushed += beta * old[5][s, i]
+            new_pushed[s, i] = pushed
+            given[s, i] = forward[s, i] - step * pushed
     row = lax.broadcasted_iota(jnp.int32, (8, LANES), 0)
     new_scalars[...] = jnp.where(row == 0, rho, curvature)
     now = [[None] * 6 for _ in range(2)]
@@ -493,7 +566,7 @@
             line = forward[s, f] if first else forward[s, f] + beta * old[2][s, f]
             along[s][f] = line
             new_along[s, f] = line
-    apply_factors(now, pattern, factors, turned, perm, back, sums, masks, parity, along, new_forward, new_image, rest[8:])
+    apply_factors(now, pattern, factors, turned, perm, back, sums, masks, parity, along, new_forward, new_image, rest[9:], given)
 
 
 def last_kernel(sizes, nc, count, lift, solve, *refs):
@@ -598,7 +671,7 @@
         cost=pl.CostEstimate(flops=0, bytes_accessed=9 << 20, transcendentals=0),
     )
     (part,) = call(functools.partial(begin_kernel, sizes), [shape(cases, lanes)], [rhs, modes, fmap, *packs, touched])
-    perm, back, lift, sums, start, solve = call(
+    perm, back, lift, sums, start, solve, pairs = call(
         functools.partial(setup_kernel, sizes),
         [
             shape(6, dofs, dofs, dtype=bf16),
@@ -607,13 +680,14 @@
             shape(12, dofs, 2 * lanes, dtype=bf16),
             faces,
             shape(2 * LANES, 256 * slabs, dtype=bf16),
+            shape(12, 32, dofs, dtype=bf16),
         ],
         [rhs, modes, fmap, coarse_rows, *packs],
         scratch=(pltpu.VMEM((LANES, dofs), f32), pltpu.VMEM((LANES, 256 * slabs), f32)),
         cost=pl.CostEstimate(flops=0, bytes_accessed=9 << 20, transcendentals=0),
     )
 
-    def reduce(part, za, zb, along_y, along_x, also=None):
+    def reduce(part, za, zb, along_y, along_x, also=None, image=None):
         za, zb, others = exchange(za, zb, "gz", part)
         outs = [shape(cases, face.shape[1] + lanes) for face in along_y] + [shape(cases, lanes)]
         ins = [part, *others, *along_y]
@@ -624,10 +698,19 @@
             part, also = lax.optimization_barrier((part, also))
         ins = [part, *others, *place, *along_x]
         *along_x, part = call(functools.partial(place_kernel, sizes, nc, 1 + len(others)), outs, ins)
+        early = None
+        if image is not None:
+            (early,) = call(
+                functools.partial(early_kernel, sizes),
+                [faces],
+                [pattern, turned, perm, image, ya, yb, za, zb],
+                specs={0: smem},
+                cost=pl.CostEstimate(flops=0, bytes_accessed=7 << 20, transcendentals=0),
+            )
         xa, xb, others = exchange(*(along_x or (part, part)), "gx", part)
-        return [xa, xb, ya, yb, za, zb], [part, *others], also
-
-    _, parts, turned = reduce(part, part, part, (), (), turned)
+        return [xa, xb, ya, yb, za, zb], [part, *others], also, early
+
+    _, parts, turned, _ = reduce(part, part, part, (), (), turned)
     wide = shape(cases, 2 * dofs)
     sends = [wide] * 4 + [shape(cases, dofs + lanes)] * 2 + [shape(cases, lanes)]
     residual, forward, image, *out = call(
@@ -639,20 +722,31 @@
     old = []
     for iteration in range(ITERS - 1):
         xa, xb, ya, yb, za, zb, part = out
-        got, parts, _ = reduce(part, za, zb, (ya, yb), (xa, xb))
+        if iteration == 0:
+            (lifted,) = call(
+                functools.partial(lifted_kernel, sizes),
+                [shape(12, 2 * LANES, dofs, dtype=bf16)],
+                [pattern, turned, perm, pairs],
+                specs={0: smem},
+                scratch=(pltpu.VMEM((12, LANES, dofs), f32),),
+                cost=pl.CostEstimate(flops=0, bytes_accessed=9 << 20, transcendentals=0),
+            )
+            got, parts, lifted, early = reduce(part, za, zb, (ya, yb), (xa, xb), lifted, image)
+        else:
+            got, parts, _, early = reduce(part, za, zb, (ya, yb), (xa, xb), None, image)
         residual, forward, image, *out = call(
             functools.partial(middle_kernel, sizes, nc, iteration == 0, len(parts)),
-            [faces] * 6 + [shape(2, 3, cases, dofs), shape(8, LANES)] + sends,
-            [pattern, factors, turned, perm, back, lift, sums, solve, *got, *parts, residual, forward, image, *old],
+            [faces] * 6 + [shape(2, 3, cases, dofs), shape(8, LANES), faces] + sends,
+            [pattern, factors, turned, perm, back, lift, sums, solve, lifted, early, *got, *parts, residual, forward, image, *old],
             specs={0: smem},
         )
-        old, out = out[:5], out[5:]
+        old, out = out[:6], out[6:]
     xa, xb, ya, yb, za, zb, part = out
-    got, parts, _ = reduce(part, za, zb, (ya, yb), (xa, xb))
+    got, parts, _, _ = reduce(part, za, zb, (ya, yb), (xa, xb))
     multipliers, final = call(
         functools.partial(last_kernel, sizes, nc, len(parts)),
         [shape(2, 3, cases, dofs)] * 2,
-        [lift, solve, *got, *parts, residual, forward, image, *old],
+        [lift, solve, *got, *parts, residual, forward, image, *old[:5]],
     )
     return multipliers.reshape(dual_rhs.shape), final.reshape(dual_rhs.shape)
 

time: 126 us -> 124 us (0.984)
  waiting for transfers between devices: 34.5 us -> 26.2 us
  Pallas kernels: 36.7 us -> 43.1 us
    ppermute x28, waiting for transfers between devices: 34.5 us -> 26.2 us  [swap(): lax.ppermute(values, axis, [(i, i ^ distance) for i in range(lax.axis_siz...]
    pallas_call x21 -> x25, Pallas kernels: 36.7 us -> 43.1 us  [call(): pl.pallas_call(kernel, out_shape=outs, in_specs=[specs.get(i, vmem) for i...]
    unnamed x14 -> x20, local copies, waits for them, and re-layouts: 6.88 us -> 6.89 us
  transfers between devices with their start and end apart: 40 -> 40, of which waited for: 15 -> 15; matrix products, arithmetic and copies ran while one was open for 0% -> 0% of each run, Pallas kernels for 4% -> 11%
where the time goes in v4:
time: 124 us; the launch traced here: 123 us
  starting transfers between devices  46.4 us (37%)
  Pallas kernels  43.1 us (35%)
  waiting for transfers between devices  26.2 us (21%)
  local copies, waits for them, and re-layouts  6.89 us (6%)
    pallas_call x25, Pallas kernels, call(): pl.pallas_call(kernel, out_shape=outs, in_specs=[specs.get(i, vmem) for i...  43.1 us
    ppermute x28, starting transfers between devices, swap(): lax.ppermute(values, axis, [(i, i ^ distance) for i in range(lax.axis_siz...  29.4 us
    ppermute x28, waiting for transfers between devices, swap(): lax.ppermute(values, axis, [(i, i ^ distance) for i in range(lax.axis_siz...  26.2 us
    ppermute x12, starting transfers between devices, exchange(): above = lax.ppermute(second, axis, pairs)  17 us
    unnamed x20, local copies, waits for them, and re-layouts  6.89 us
  transfers between devices with their start and end apart: 40, of which 15 were waited for; matrix products, arithmetic and copies ran while one was open for 0% of the time, Pallas kernels for 11%

profile of v4, /device:TPU:0, one launch (start us, length us, event | category | flops | bytes accessed | tf_op | source)
XLA Modules:
  0.0 123.5 jit_solution(16807825719326643592)
XLA Ops:
  0.6 0.9 copy-done.3
  1.5 0.9 copy-done.4
  2.4 0.7 copy-done.5
  3.1 0.7 copy-done.6
  3.8 0.9 shard_map.77
  4.8 3.0 %collective-permute-start = (f32[80,256]{1,0:T(8,128)S(1)}, f32[80,256]{1,0:T(8,128)S(1)}, u32[]{:S(2)}, u32[]{:S(2)}) collective-permute-start(f32[80,256]{1,0:T(8,128)S(1)} %get-tuple-element.105), channel_id=1, source_target_pairs={{0,8},{8,0},{16,24},{24,16},{1,9},{9,1},{17,25},{25,17},{2,10},{10... | collective-permute-start | bytes 245768 | tf_op jit(solution)/shard_map/ppermute | solution.py:585
  7.8 0.7 collective-permute-start.1
  8.4 1.6 %collective-permute-start.2 = (f32[80,256]{1,0:T(8,128)S(1)}, f32[80,256]{1,0:T(8,128)S(1)}, u32[]{:S(2)}, u32[]{:S(2)}) collective-permute-start(f32[80,256]{1,0:T(8,128)S(1)} %get-tuple-element.107), channel_id=1, source_target_pairs={{0,2},{2,0},{4,6},{6,4},{1,3},{3,1},{5,7},{7,5},{8,10},{10,8},{12,... | collective-permute-start | bytes 245768 | tf_op jit(solution)/shard_map/ppermute | solution.py:585
  10.1 0.7 collective-permute-start.3
  10.8 3.7 %copy-done = bf16[1,1,2,6,6,256,256]{6,5,4,3,2,1,0:T(8,128)(2,1)S(1)} copy-done((bf16[1,1,2,6,6,256,256]{6,5,4,3,2,1,0:T(8,128)(2,1)S(1)}, bf16[1,1,2,6,6,256,256]{6,5,4,3,2,1,0:T(8,128)(2,1)}, u32[]{:S(2)}) %copy-start) | copy-done | bytes 9437208
  14.5 1.2 shard_map.80.refs_0_
  15.7 0.5 collective-permute-start.5
  16.2 0.8 collective-permute-done.5.refs_1_
  17.1 2.5 %collective-permute-start.8 = (f32[16,128]{1,0:T(8,128)S(1)}, f32[16,128]{1,0:T(8,128)S(1)}, u32[]{:S(2)}, u32[]{:S(2)}) collective-permute-start(f32[16,128]{1,0:T(8,128)S(1)} %shard_map.81.refs_0_), channel_id=1, source_target_pairs={{0,6},{2,4},{4,2},{6,0},{1,7},{3,5},{5,3},{7,1},{8,14},{10,12},{12... | collective-permute-start | bytes 24584 | tf_op jit(solution)/shard_map/ppermute | solution.py:598
  19.6 3.4 %collective-permute-start.7 = (f32[16,128]{1,0:T(8,128)S(1)}, f32[16,128]{1,0:T(8,128)S(1)}, u32[]{:S(2)}, u32[]{:S(2)}) collective-permute-start(f32[16,128]{1,0:T(8,128)S(1)} %shard_map.81.refs_0_), channel_id=1, source_target_pairs={{0,4},{2,6},{4,0},{6,2},{1,5},{3,7},{5,1},{7,3},{8,12},{10,14},{12... | collective-permute-start | bytes 24584 | tf_op jit(solution)/shard_map/ppermute | solution.py:585
  23.1 2.5 %shard_map.82.turned.refs_2_ = bf16[2,6,6,256,256]{4,3,2,1,0:T(8,128)(2,1)S(1)} custom-call(bf16[2,6,6,256,256]{4,3,2,1,0:T(8,128)(2,1)S(1)} %bitcast.14), custom_call_target="tpu_custom_call" | custom-call | bytes 9437184 | tf_op jit(solution)/shard_map/pallas_call | solution.py:627
  25.6 1.0 collective-permute-done.6.refs_1_
  26.8 1.5 %collective-permute-start.11 = (f32[16,512]{1,0:T(8,128)S(1)}, f32[16,512]{1,0:T(8,128)S(1)}, u32[]{:S(2)}, u32[]{:S(2)}) collective-permute-start(f32[16,512]{1,0:T(8,128)S(1)} %shard_map.84.refs_0_), channel_id=1, source_target_pairs={{0,24},{8,16},{16,8},{24,0},{1,25},{9,17},{17,9},{25,1},{2,26},{10... | collective-permute-start | bytes 98312 | tf_op jit(solution)/shard_map/ppermute | solution.py:598
  28.3 4.2 %collective-permute-start.10 = (f32[16,512]{1,0:T(8,128)S(1)}, f32[16,512]{1,0:T(8,128)S(1)}, u32[]{:S(2)}, u32[]{:S(2)}) collective-permute-start(f32[16,512]{1,0:T(8,128)S(1)} %shard_map.84.refs_0_), channel_id=1, source_target_pairs={{0,16},{8,24},{16,0},{24,8},{1,17},{9,25},{17,1},{25,9},{2,18},{10... | collective-permute-start | bytes 98312 | tf_op jit(solution)/shard_map/ppermute | solution.py:585
  32.5 2.1 %shard_map.78 = (bf16[6,256,256]{2,1,0:T(8,128)(2,1)S(1)}, bf16[6,256,256]{2,1,0:T(8,128)(2,1)S(1)}, bf16[12,256,256]{2,1,0:T(8,128)(2,1)S(1)}, bf16[12,256,256]...) custom-call(f32[2,3,16,256]{3,2,1,0:T(8,128)S(1)} %get-tuple-element, ...), custom_call_target="tpu_custom_call" | custom-call | bytes 9437184 | tf_op jit(solution)/shard_map/pallas_call | solution.py:627
  34.6 1.8 %collective-permute-done.9.refs_1_ = f32[16,512]{1,0:T(8,128)S(1)} collective-permute-done((f32[16,512]{1,0:T(8,128)S(1)}, f32[16,512]{1,0:T(8,128)S(1)}, u32[]{:S(2)}, u32[]{:S(2)}) %collective-permute-start.9) | collective-permute-done | bytes 32800 | tf_op jit(solution)/shard_map/ppermute | solution.py:585
  36.4 6.8 %shard_map.85 = (f32[2,6,16,256]{3,2,1,0:T(8,128)S(1)}, f32[2,6,16,256]{3,2,1,0:T(8,128)S(1)}, f32[2,6,16,256]{3,2,1,0:T(8,128)S(1)}, f32[16,512]{1,0:T(8,128)S(...) custom-call(s32[6,2,6]{2,1,0:T(2,128)S(1)} %bitcast.21, ...), custom_call_target="tpu_custom_call" | custom-call | tf_op jit(solution)/shard_map/pallas_call | solution.py:627
  43.2 1.2 collective-permute-done.12.refs_1_.za.zb.refs_14_.refs_15_
  44.4 1.1 collective-permute-start.13
  45.5 1.3 %collective-permute-start.14 = (f32[16,640]{1,0:T(8,128)S(1)}, f32[16,640]{1,0:T(8,128)S(1)}, u32[]{:S(2)}, u32[]{:S(2)}) collective-permute-start(f32[16,640]{1,0:T(8,128)S(1)} %get-tuple-element.127), channel_id=1, source_target_pairs={{0,6},{2,4},{4,2},{6,0},{1,7},{3,5},{5,3},{7,1},{8,14},{10,12},{12... | collective-permute-start | bytes 122888 | tf_op jit(solution)/shard_map/ppermute | solution.py:598
  46.9 1.1 collective-permute-start.15
  48.0 3.0 %shard_map.87.refs_8_ = bf16[12,256,256]{2,1,0:T(8,128)(2,1)S(1)} custom-call(s32[6,2,6]{2,1,0:T(2,128)S(1)} %bitcast.22, bf16[2,6,6,256,256]{4,3,2,1,0:T(8,128)(2,1)S(1)} %shard_map.82.turned.refs_2_, bf16[6,256,256]{2,1,0:T(8,128)(2,1)S(1)} %get-tuple-element.113.perm.refs_3_, bf16[12,32,256]{2,1,0:T(8,128)(2,1)S(1)} %get-tuple-element.123.pairs), custom_call_target="tpu_custom_call" | custom-call | bytes 9437184 | tf_op jit(solution)/shard_map/pallas_call | solution.py:627
  51.0 0.5 collective-permute-done.15.refs_2_
  51.9 1.2 %collective-permute-start.17 = (f32[16,1024]{1,0:T(8,128)S(1)}, f32[16,1024]{1,0:T(8,128)S(1)}, u32[]{:S(2)}, u32[]{:S(2)}) collective-permute-start(f32[16,1024]{1,0:T(8,128)S(1)} %get-tuple-element.132), channel_id=1, source_target_pairs={{0,24},{8,16},{16,8},{24,0},{1,25},{9,17},{17,9},{25,1},{2,26},{10... | collective-permute-start | bytes 196616 | tf_op jit(solution)/shard_map/ppermute | solution.py:598
  53.2 2.0 %collective-permute-start.18 = (f32[16,512]{1,0:T(8,128)S(1)}, f32[16,512]{1,0:T(8,128)S(1)}, u32[]{:S(2)}, u32[]{:S(2)}) collective-permute-start(f32[16,512]{1,0:T(8,128)S(1)} %get-tuple-element.133.refs_16_), channel_id=1, source_target_pairs={{0,16},{8,24},{16,0},{24,8},{1,17},{9,25},{17,1},{25,9},{2,18},{10... | collective-permute-start | bytes 98312 | tf_op jit(solution)/shard_map/ppermute | solution.py:585
  55.2 1.9 %shard_map.88.refs_9_ = f32[2,6,16,256]{3,2,1,0:T(8,128)S(1)} custom-call(s32[6,2,6]{2,1,0:T(2,128)S(1)} %bitcast.23, bf16[2,6,6,256,256]{4,3,2,1,0:T(8,128)(2,1)S(1)} %shard_map.82.turned.refs_2_, bf16[6,256,256]{2,1,0:T(8,128)(2,1)S(1)} %get-tuple-element.113.perm.refs_3_, f32[2,6,16,256]{3,2,1,0:T(8,128)S(1)} %get-tuple-element.125.image.refs_22_, ...), custom_call_target="tpu_custom_call" | custom-call | bytes 7340032 | tf_op jit(solution)/shard_map/pallas_call | solution.py:627
  57.1 0.4 collective-permute-done.18.refs_18_
  57.5 6.4 %shard_map.90 = (f32[2,6,16,256]{3,2,1,0:T(8,128)S(1)}, f32[2,6,16,256]{3,2,1,0:T(8,128)S(1)}, f32[2,6,16,256]{3,2,1,0:T(8,128)S(1)}, f32[2,6,16,256]{3,2,1,0:T(...) custom-call(s32[6,2,6]{2,1,0:T(2,128)S(1)} %bitcast.24, ...), custom_call_target="tpu_custom_call" | custom-call | tf_op jit(solution)/shard_map/pallas_call | solution.py:627
  63.9 1.2 collective-permute-done.19.refs_1_.za.zb.refs_14_.refs_15_
  65.1 1.5 %collective-permute-start.20 = (f32[16,640]{1,0:T(8,128)S(1)}, f32[16,640]{1,0:T(8,128)S(1)}, u32[]{:S(2)}, u32[]{:S(2)}) collective-permute-start(f32[16,640]{1,0:T(8,128)S(1)} %get-tuple-element.141), channel_id=1, source_target_pairs={{0,2},{2,0},{4,6},{6,4},{1,3},{3,1},{5,7},{7,5},{8,10},{10,8},{12,... | collective-permute-start | bytes 122888 | tf_op jit(solution)/shard_map/ppermute | solution.py:585
  66.6 1.4 %collective-permute-start.21 = (f32[16,640]{1,0:T(8,128)S(1)}, f32[16,640]{1,0:T(8,128)S(1)}, u32[]{:S(2)}, u32[]{:S(2)}) collective-permute-start(f32[16,640]{1,0:T(8,128)S(1)} %get-tuple-element.142), channel_id=1, source_target_pairs={{0,6},{2,4},{4,2},{6,0},{1,7},{3,5},{5,3},{7,1},{8,14},{10,12},{12... | collective-permute-start | bytes 122888 | tf_op jit(solution)/shard_map/ppermute | solution.py:598
  67.9 0.7 collective-permute-start.22
  68.7 3.8 %collective-permute-done.22.refs_2_ = f32[16,128]{1,0:T(8,128)S(1)} collective-permute-done((f32[16,128]{1,0:T(8,128)S(1)}, f32[16,128]{1,0:T(8,128)S(1)}, u32[]{:S(2)}, u32[]{:S(2)}) %collective-permute-start.22) | collective-permute-done | bytes 8224 | tf_op jit(solution)/shard_map/ppermute | solution.py:585
  72.7 1.4 %collective-permute-start.23 = (f32[16,1024]{1,0:T(8,128)S(1)}, f32[16,1024]{1,0:T(8,128)S(1)}, u32[]{:S(2)}, u32[]{:S(2)}) collective-permute-start(f32[16,1024]{1,0:T(8,128)S(1)} %get-tuple-element.146), channel_id=1, source_target_pairs={{0,8},{8,0},{16,24},{24,16},{1,9},{9,1},{17,25},{25,17},{2,10},{10... | collective-permute-start | bytes 196616 | tf_op jit(solution)/shard_map/ppermute | solution.py:585
  74.1 1.7 %collective-permute-start.24 = (f32[16,1024]{1,0:T(8,128)S(1)}, f32[16,1024]{1,0:T(8,128)S(1)}, u32[]{:S(2)}, u32[]{:S(2)}) collective-permute-start(f32[16,1024]{1,0:T(8,128)S(1)} %get-tuple-element.147), channel_id=1, source_target_pairs={{0,24},{8,16},{16,8},{24,0},{1,25},{9,17},{17,9},{25,1},{2,26},{10... | collective-permute-start | bytes 196616 | tf_op jit(solution)/shard_map/ppermute | solution.py:598
  75.8 0.4 collective-permute-start.25
  76.2 1.9 %shard_map.92.refs_9_ = f32[2,6,16,256]{3,2,1,0:T(8,128)S(1)} custom-call(s32[6,2,6]{2,1,0:T(2,128)S(1)} %bitcast.25, bf16[2,6,6,256,256]{4,3,2,1,0:T(8,128)(2,1)S(1)} %shard_map.82.turned.refs_2_, bf16[6,256,256]{2,1,0:T(8,128)(2,1)S(1)} %get-tuple-element.113.perm.refs_3_, f32[2,6,16,256]{3,2,1,0:T(8,128)S(1)} %get-tuple-element.136.image.refs_22_, ...), custom_call_target="tpu_custom_call" | custom-call | bytes 7340032 | tf_op jit(solution)/shard_map/pallas_call | solution.py:627
  78.1 1.7 %collective-permute-done.25.refs_18_ = f32[16,512]{1,0:T(8,128)S(1)} collective-permute-done((f32[16,512]{1,0:T(8,128)S(1)}, f32[16,512]{1,0:T(8,128)S(1)}, u32[]{:S(2)}, u32[]{:S(2)}) %collective-permute-start.25) | collective-permute-done | bytes 32800 | tf_op jit(solution)/shard_map/ppermute | solution.py:585
  79.7 6.2 %shard_map.94 = (f32[2,6,16,256]{3,2,1,0:T(8,128)S(1)}, f32[2,6,16,256]{3,2,1,0:T(8,128)S(1)}, f32[2,6,16,256]{3,2,1,0:T(8,128)S(1)}, f32[2,6,16,256]{3,2,1,0:T(...) custom-call(s32[6,2,6]{2,1,0:T(2,128)S(1)} %bitcast.26, ...), custom_call_target="tpu_custom_call" | custom-call | tf_op jit(solution)/shard_map/pallas_call | solution.py:627
  86.0 1.2 collective-permute-done.26.refs_1_.za.zb.refs_14_.refs_15_
  87.2 0.8 collective-permute-start.27
  88.0 1.8 %collective-permute-start.28 = (f32[16,640]{1,0:T(8,128)S(1)}, f32[16,640]{1,0:T(8,128)S(1)}, u32[]{:S(2)}, u32[]{:S(2)}) collective-permute-start(f32[16,640]{1,0:T(8,128)S(1)} %get-tuple-element.163), channel_id=1, source_target_pairs={{0,6},{2,4},{4,2},{6,0},{1,7},{3,5},{5,3},{7,1},{8,14},{10,12},{12... | collective-permute-start | bytes 122888 | tf_op jit(solution)/shard_map/ppermute | solution.py:598
  89.8 0.9 collective-permute-start.29
  90.7 3.6 %collective-permute-done.29.refs_2_ = f32[16,128]{1,0:T(8,128)S(1)} collective-permute-done((f32[16,128]{1,0:T(8,128)S(1)}, f32[16,128]{1,0:T(8,128)S(1)}, u32[]{:S(2)}, u32[]{:S(2)}) %collective-permute-start.29) | collective-permute-done | bytes 8224 | tf_op jit(solution)/shard_map/ppermute | solution.py:585
  94.5 0.5 collective-permute-start.30
  95.0 1.3 %collective-permute-start.31 = (f32[16,1024]{1,0:T(8,128)S(1)}, f32[16,1024]{1,0:T(8,128)S(1)}, u32[]{:S(2)}, u32[]{:S(2)}) collective-permute-start(f32[16,1024]{1,0:T(8,128)S(1)} %get-tuple-element.168), channel_id=1, source_target_pairs={{0,24},{8,16},{16,8},{24,0},{1,25},{9,17},{17,9},{25,1},{2,26},{10... | collective-permute-start | bytes 196616 | tf_op jit(solution)/shard_map/ppermute | solution.py:598
  96.4 1.7 %collective-permute-start.32 = (f32[16,512]{1,0:T(8,128)S(1)}, f32[16,512]{1,0:T(8,128)S(1)}, u32[]{:S(2)}, u32[]{:S(2)}) collective-permute-start(f32[16,512]{1,0:T(8,128)S(1)} %get-tuple-element.169.refs_16_), channel_id=1, source_target_pairs={{0,16},{8,24},{16,0},{24,8},{1,17},{9,25},{17,1},{25,9},{2,18},{10... | collective-permute-start | bytes 98312 | tf_op jit(solution)/shard_map/ppermute | solution.py:585
  98.1 1.9 %shard_map.96.refs_9_ = f32[2,6,16,256]{3,2,1,0:T(8,128)S(1)} custom-call(s32[6,2,6]{2,1,0:T(2,128)S(1)} %bitcast.27, bf16[2,6,6,256,256]{4,3,2,1,0:T(8,128)(2,1)S(1)} %shard_map.82.turned.refs_2_, bf16[6,256,256]{2,1,0:T(8,128)(2,1)S(1)} %get-tuple-element.113.perm.refs_3_, f32[2,6,16,256]{3,2,1,0:T(8,128)S(1)} %get-tuple-element.157.image.refs_22_, ...), custom_call_target="tpu_custom_call" | custom-call | bytes 7340032 | tf_op jit(solution)/shard_map/pallas_call | solution.py:627
  99.9 0.7 collective-permute-done.32.refs_18_
  100.6 6.2 %shard_map.98 = (f32[2,6,16,256]{3,2,1,0:T(8,128)S(1)}, f32[2,6,16,256]{3,2,1,0:T(8,128)S(1)}, f32[2,6,16,256]{3,2,1,0:T(8,128)S(1)}, f32[2,6,16,256]{3,2,1,0:T(...) custom-call(s32[6,2,6]{2,1,0:T(2,128)S(1)} %bitcast.28, ...), custom_call_target="tpu_custom_call" | custom-call | tf_op jit(solution)/shard_map/pallas_call | solution.py:627
  106.8 1.2 collective-permute-done.33.refs_1_.refs_4_.refs_5_
  108.0 1.1 collective-permute-start.34
  109.1 1.4 %collective-permute-start.36 = (f32[16,640]{1,0:T(8,128)S(1)}, f32[16,640]{1,0:T(8,128)S(1)}, u32[]{:S(2)}, u32[]{:S(2)}) collective-permute-start(f32[16,640]{1,0:T(8,128)S(1)} %get-tuple-element.184), channel_id=1, source_target_pairs={{0,6},{2,4},{4,2},{6,0},{1,7},{3,5},{5,3},{7,1},{8,14},{10,12},{12... | collective-permute-start | bytes 122888 | tf_op jit(solution)/shard_map/ppermute | solution.py:598
  110.5 1.1 collective-permute-start.35
  111.5 3.5 %collective-permute-done.35.refs_2_ = f32[16,128]{1,0:T(8,128)S(1)} collective-permute-done((f32[16,128]{1,0:T(8,128)S(1)}, f32[16,128]{1,0:T(8,128)S(1)}, u32[]{:S(2)}, u32[]{:S(2)}) %collective-permute-start.35) | collective-permute-done | bytes 8224 | tf_op jit(solution)/shard_map/ppermute | solution.py:585
  115.2 1.5 %collective-permute-start.37 = (f32[16,1024]{1,0:T(8,128)S(1)}, f32[16,1024]{1,0:T(8,128)S(1)}, u32[]{:S(2)}, u32[]{:S(2)}) collective-permute-start(f32[16,1024]{1,0:T(8,128)S(1)} %get-tuple-element.187), channel_id=1, source_target_pairs={{0,8},{8,0},{16,24},{24,16},{1,9},{9,1},{17,25},{25,17},{2,10},{10... | collective-permute-start | bytes 196616 | tf_op jit(solution)/shard_map/ppermute | solution.py:585
  116.8 1.6 %collective-permute-start.38 = (f32[16,1024]{1,0:T(8,128)S(1)}, f32[16,1024]{1,0:T(8,128)S(1)}, u32[]{:S(2)}, u32[]{:S(2)}) collective-permute-start(f32[16,1024]{1,0:T(8,128)S(1)} %get-tuple-element.188), channel_id=1, source_target_pairs={{0,24},{8,16},{16,8},{24,0},{1,25},{9,17},{17,9},{25,1},{2,26},{10... | collective-permute-start | bytes 196616 | tf_op jit(solution)/shard_map/ppermute | solution.py:598
  118.7 3.5 %collective-permute-done.39.refs_8_ = f32[16,512]{1,0:T(8,128)S(1)} collective-permute-done((f32[16,512]{1,0:T(8,128)S(1)}, f32[16,512]{1,0:T(8,128)S(1)}, u32[]{:S(2)}, u32[]{:S(2)}) %collective-permute-start.39) | collective-permute-done | bytes 32800 | tf_op jit(solution)/shard_map/ppermute | solution.py:585
  122.3 1.2 shard_map.101
  (62 shorter events, 1.9 us)
Async XLA Ops:
  0.6 0.9 copy-start.3
  1.5 0.9 copy-start.4
  2.4 0.7 copy-start.5
  3.1 0.7 copy-start.6
  4.8 9.7 %collective-permute-start = (f32[80,256]{1,0:T(8,128)S(1)}, f32[80,256]{1,0:T(8,128)S(1)}, u32[]{:S(2)}, u32[]{:S(2)}) collective-permute-start(f32[80,256]{1,0:T(8,128)S(1)} %get-tuple-element.105), channel_id=1, source_target_pairs={{0,8},{8,0},{16,24},{24,16},{1,9},{9,1},{17,25},{25,17},{2,10},{10... | collective-permute-start | bytes 245768 | tf_op jit(solution)/shard_map/ppermute | solution.py:585
  7.8 6.7 %collective-permute-start.1 = (f32[80,256]{1,0:T(8,128)S(1)}, f32[80,256]{1,0:T(8,128)S(1)}, u32[]{:S(2)}, u32[]{:S(2)}) collective-permute-start(f32[80,256]{1,0:T(8,128)S(1)} %get-tuple-element.106), channel_id=1, source_target_pairs={{8,16},{16,8},{9,17},{17,9},{10,18},{18,10},{11,19},{19,11},{12,20... | collective-permute-start | bytes 245768 | tf_op jit(solution)/shard_map/ppermute | solution.py:598
  8.4 6.1 %collective-permute-start.2 = (f32[80,256]{1,0:T(8,128)S(1)}, f32[80,256]{1,0:T(8,128)S(1)}, u32[]{:S(2)}, u32[]{:S(2)}) collective-permute-start(f32[80,256]{1,0:T(8,128)S(1)} %get-tuple-element.107), channel_id=1, source_target_pairs={{0,2},{2,0},{4,6},{6,4},{1,3},{3,1},{5,7},{7,5},{8,10},{10,8},{12,... | collective-permute-start | bytes 245768 | tf_op jit(solution)/shard_map/ppermute | solution.py:585
  10.1 4.5 %collective-permute-start.3 = (f32[80,256]{1,0:T(8,128)S(1)}, f32[80,256]{1,0:T(8,128)S(1)}, u32[]{:S(2)}, u32[]{:S(2)}) collective-permute-start(f32[80,256]{1,0:T(8,128)S(1)} %get-tuple-element.108), channel_id=1, source_target_pairs={{2,4},{4,2},{3,5},{5,3},{10,12},{12,10},{11,13},{13,11},{18,20},{2... | collective-permute-start | bytes 245768 | tf_op jit(solution)/shard_map/ppermute | solution.py:598
  10.7 3.8 %collective-permute-start.4 = (f32[56,256]{1,0:T(8,128)S(1)}, f32[56,256]{1,0:T(8,128)S(1)}, u32[]{:S(2)}, u32[]{:S(2)}) collective-permute-start(f32[56,256]{1,0:T(8,128)S(1)} %get-tuple-element.109), channel_id=1, source_target_pairs={{0,1},{1,0},{2,3},{3,2},{4,5},{5,4},{6,7},{7,6},{8,9},{9,8},{10,11... | collective-permute-start | bytes 172040 | tf_op jit(solution)/shard_map/ppermute | solution.py:585
  10.8 3.7 %copy-start = (bf16[1,1,2,6,6,256,256]{6,5,4,3,2,1,0:T(8,128)(2,1)S(1)}, bf16[1,1,2,6,6,256,256]{6,5,4,3,2,1,0:T(8,128)(2,1)}, u32[]{:S(2)}) copy-start(bf16[1,1,2,6,6,256,256]{6,5,4,3,2,1,0:T(8,128)(2,1)} %param.7) | copy-start | bytes 28311556
  14.5 8.6 %copy-start.1 = (bf16[1,1,2,6,6,256,256]{6,5,4,3,2,1,0:T(8,128)(2,1)S(1)}, bf16[1,1,2,6,6,256,256]{6,5,4,3,2,1,0:T(8,128)(2,1)}, u32[]{:S(2)}) copy-start(bf16[1,1,2,6,6,256,256]{6,5,4,3,2,1,0:T(8,128)(2,1)} %param.7) | copy-start | bytes 28311556
  15.7 1.3 %collective-permute-start.5 = (f32[16,128]{1,0:T(8,128)S(1)}, f32[16,128]{1,0:T(8,128)S(1)}, u32[]{:S(2)}, u32[]{:S(2)}) collective-permute-start(f32[16,128]{1,0:T(8,128)S(1)} %shard_map.80.refs_0_), channel_id=1, source_target_pairs={{0,1},{1,0},{2,3},{3,2},{4,5},{5,4},{6,7},{7,6},{8,9},{9,8},{10,11... | collective-permute-start | bytes 24584 | tf_op jit(solution)/shard_map/ppermute | solution.py:585
  17.1 8.5 %collective-permute-start.8 = (f32[16,128]{1,0:T(8,128)S(1)}, f32[16,128]{1,0:T(8,128)S(1)}, u32[]{:S(2)}, u32[]{:S(2)}) collective-permute-start(f32[16,128]{1,0:T(8,128)S(1)} %shard_map.81.refs_0_), channel_id=1, source_target_pairs={{0,6},{2,4},{4,2},{6,0},{1,7},{3,5},{5,3},{7,1},{8,14},{10,12},{12... | collective-permute-start | bytes 24584 | tf_op jit(solution)/shard_map/ppermute | solution.py:598
  19.6 6.0 %collective-permute-start.7 = (f32[16,128]{1,0:T(8,128)S(1)}, f32[16,128]{1,0:T(8,128)S(1)}, u32[]{:S(2)}, u32[]{:S(2)}) collective-permute-start(f32[16,128]{1,0:T(8,128)S(1)} %shard_map.81.refs_0_), channel_id=1, source_target_pairs={{0,4},{2,6},{4,0},{6,2},{1,5},{3,7},{5,1},{7,3},{8,12},{10,14},{12... | collective-permute-start | bytes 24584 | tf_op jit(solution)/shard_map/ppermute | solution.py:585
  22.9 3.7 %collective-permute-start.6 = (f32[16,128]{1,0:T(8,128)S(1)}, f32[16,128]{1,0:T(8,128)S(1)}, u32[]{:S(2)}, u32[]{:S(2)}) collective-permute-start(f32[16,128]{1,0:T(8,128)S(1)} %shard_map.81.refs_0_), channel_id=1, source_target_pairs={{0,2},{2,0},{4,6},{6,4},{1,3},{3,1},{5,7},{7,5},{8,10},{10,8},{12,... | collective-permute-start | bytes 24584 | tf_op jit(solution)/shard_map/ppermute | solution.py:585
  23.1 13.3 %copy-start.2 = (s32[1,1,2,6,6]{4,2,3,1,0:T(2,128)S(1)}, s32[1,1,2,6,6]{4,2,3,1,0:T(2,128)}, u32[]{:S(2)}) copy-start(s32[1,1,2,6,6]{4,2,3,1,0:T(2,128)} %param.8) | copy-start | bytes 868
  26.8 7.8 %collective-permute-start.11 = (f32[16,512]{1,0:T(8,128)S(1)}, f32[16,512]{1,0:T(8,128)S(1)}, u32[]{:S(2)}, u32[]{:S(2)}) collective-permute-start(f32[16,512]{1,0:T(8,128)S(1)} %shard_map.84.refs_0_), channel_id=1, source_target_pairs={{0,24},{8,16},{16,8},{24,0},{1,25},{9,17},{17,9},{25,1},{2,26},{10... | collective-permute-start | bytes 98312 | tf_op jit(solution)/shard_map/ppermute | solution.py:598
  28.3 6.3 %collective-permute-start.10 = (f32[16,512]{1,0:T(8,128)S(1)}, f32[16,512]{1,0:T(8,128)S(1)}, u32[]{:S(2)}, u32[]{:S(2)}) collective-permute-start(f32[16,512]{1,0:T(8,128)S(1)} %shard_map.84.refs_0_), channel_id=1, source_target_pairs={{0,16},{8,24},{16,0},{24,8},{1,17},{9,25},{17,1},{25,9},{2,18},{10... | collective-permute-start | bytes 98312 | tf_op jit(solution)/shard_map/ppermute | solution.py:585
  32.5 3.9 %collective-permute-start.9 = (f32[16,512]{1,0:T(8,128)S(1)}, f32[16,512]{1,0:T(8,128)S(1)}, u32[]{:S(2)}, u32[]{:S(2)}) collective-permute-start(f32[16,512]{1,0:T(8,128)S(1)} %shard_map.84.refs_0_), channel_id=1, source_target_pairs={{0,8},{8,0},{16,24},{24,16},{1,9},{9,1},{17,25},{25,17},{2,10},{10... | collective-permute-start | bytes 98312 | tf_op jit(solution)/shard_map/ppermute | solution.py:585
  43.2 1.2 collective-permute-start.12
  44.4 7.1 %collective-permute-start.13 = (f32[16,640]{1,0:T(8,128)S(1)}, f32[16,640]{1,0:T(8,128)S(1)}, u32[]{:S(2)}, u32[]{:S(2)}) collective-permute-start(f32[16,640]{1,0:T(8,128)S(1)} %get-tuple-element.126), channel_id=1, source_target_pairs={{0,2},{2,0},{4,6},{6,4},{1,3},{3,1},{5,7},{7,5},{8,10},{10,8},{12,... | collective-permute-start | bytes 122888 | tf_op jit(solution)/shard_map/ppermute | solution.py:585
  45.5 6.0 %collective-permute-start.14 = (f32[16,640]{1,0:T(8,128)S(1)}, f32[16,640]{1,0:T(8,128)S(1)}, u32[]{:S(2)}, u32[]{:S(2)}) collective-permute-start(f32[16,640]{1,0:T(8,128)S(1)} %get-tuple-element.127), channel_id=1, source_target_pairs={{0,6},{2,4},{4,2},{6,0},{1,7},{3,5},{5,3},{7,1},{8,14},{10,12},{12... | collective-permute-start | bytes 122888 | tf_op jit(solution)/shard_map/ppermute | solution.py:598
  46.9 4.6 %collective-permute-start.15 = (f32[16,128]{1,0:T(8,128)S(1)}, f32[16,128]{1,0:T(8,128)S(1)}, u32[]{:S(2)}, u32[]{:S(2)}) collective-permute-start(f32[16,128]{1,0:T(8,128)S(1)} %get-tuple-element.128.refs_0_), channel_id=1, source_target_pairs={{0,4},{2,6},{4,0},{6,2},{1,5},{3,7},{5,1},{7,3},{8,12},{10,14},{12... | collective-permute-start | bytes 24584 | tf_op jit(solution)/shard_map/ppermute | solution.py:585
  48.0 9.5 %slice-start = ((s8[9437184]{0:T(1024)(128)(4,1)}), s8[4194304]{0:T(1024)(128)(4,1)S(1)}, s32[]{:S(2)}) async-start(s8[9437184]{0:T(1024)(128)(4,1)} %bitcast.16), calls=%async_computation | async-start | bytes 8388608
  48.0 9.5 %slice-start.1 = ((s8[9437184]{0:T(1024)(128)(4,1)}), s8[4194304]{0:T(1024)(128)(4,1)S(1)}, s32[]{:S(2)}) async-start(s8[9437184]{0:T(1024)(128)(4,1)} %bitcast.16), calls=%async_computation.1 | async-start | bytes 8388608
  51.7 5.8 %collective-permute-start.16 = (f32[16,1024]{1,0:T(8,128)S(1)}, f32[16,1024]{1,0:T(8,128)S(1)}, u32[]{:S(2)}, u32[]{:S(2)}) collective-permute-start(f32[16,1024]{1,0:T(8,128)S(1)} %get-tuple-element.131), channel_id=1, source_target_pairs={{0,8},{8,0},{16,24},{24,16},{1,9},{9,1},{17,25},{25,17},{2,10},{10... | collective-permute-start | bytes 196616 | tf_op jit(solution)/shard_map/ppermute | solution.py:585
  51.9 5.5 %collective-permute-start.17 = (f32[16,1024]{1,0:T(8,128)S(1)}, f32[16,1024]{1,0:T(8,128)S(1)}, u32[]{:S(2)}, u32[]{:S(2)}) collective-permute-start(f32[16,1024]{1,0:T(8,128)S(1)} %get-tuple-element.132), channel_id=1, source_target_pairs={{0,24},{8,16},{16,8},{24,0},{1,25},{9,17},{17,9},{25,1},{2,26},{10... | collective-permute-start | bytes 196616 | tf_op jit(solution)/shard_map/ppermute | solution.py:598
  53.2 4.3 %collective-permute-start.18 = (f32[16,512]{1,0:T(8,128)S(1)}, f32[16,512]{1,0:T(8,128)S(1)}, u32[]{:S(2)}, u32[]{:S(2)}) collective-permute-start(f32[16,512]{1,0:T(8,128)S(1)} %get-tuple-element.133.refs_16_), channel_id=1, source_target_pairs={{0,16},{8,24},{16,0},{24,8},{1,17},{9,25},{17,1},{25,9},{2,18},{10... | collective-permute-start | bytes 98312 | tf_op jit(solution)/shard_map/ppermute | solution.py:585
  55.2 2.3 %slice-start.2 = ((s8[9437184]{0:T(1024)(128)(4,1)}), s8[1048576]{0:T(1024)(128)(4,1)S(1)}, s32[]{:S(2)}) async-start(s8[9437184]{0:T(1024)(128)(4,1)} %bitcast.16), calls=%async_computation.2 | async-start | bytes 2097152
  63.9 1.2 collective-permute-start.19
  65.1 7.4 %collective-permute-start.20 = (f32[16,640]{1,0:T(8,128)S(1)}, f32[16,640]{1,0:T(8,128)S(1)}, u32[]{:S(2)}, u32[]{:S(2)}) collective-permute-start(f32[16,640]{1,0:T(8,128)S(1)} %get-tuple-element.141), channel_id=1, source_target_pairs={{0,2},{2,0},{4,6},{6,4},{1,3},{3,1},{5,7},{7,5},{8,10},{10,8},{12,... | collective-permute-start | bytes 122888 | tf_op jit(solution)/shard_map/ppermute | solution.py:585
  66.6 5.9 %collective-permute-start.21 = (f32[16,640]{1,0:T(8,128)S(1)}, f32[16,640]{1,0:T(8,128)S(1)}, u32[]{:S(2)}, u32[]{:S(2)}) collective-permute-start(f32[16,640]{1,0:T(8,128)S(1)} %get-tuple-element.142), channel_id=1, source_target_pairs={{0,6},{2,4},{4,2},{6,0},{1,7},{3,5},{5,3},{7,1},{8,14},{10,12},{12... | collective-permute-start | bytes 122888 | tf_op jit(solution)/shard_map/ppermute | solution.py:598
  67.9 4.5 %collective-permute-start.22 = (f32[16,128]{1,0:T(8,128)S(1)}, f32[16,128]{1,0:T(8,128)S(1)}, u32[]{:S(2)}, u32[]{:S(2)}) collective-permute-start(f32[16,128]{1,0:T(8,128)S(1)} %get-tuple-element.143.refs_0_), channel_id=1, source_target_pairs={{0,4},{2,6},{4,0},{6,2},{1,5},{3,7},{5,1},{7,3},{8,12},{10,14},{12... | collective-permute-start | bytes 24584 | tf_op jit(solution)/shard_map/ppermute | solution.py:585
  72.7 7.0 %collective-permute-start.23 = (f32[16,1024]{1,0:T(8,128)S(1)}, f32[16,1024]{1,0:T(8,128)S(1)}, u32[]{:S(2)}, u32[]{:S(2)}) collective-permute-start(f32[16,1024]{1,0:T(8,128)S(1)} %get-tuple-element.146), channel_id=1, source_target_pairs={{0,8},{8,0},{16,24},{24,16},{1,9},{9,1},{17,25},{25,17},{2,10},{10... | collective-permute-start | bytes 196616 | tf_op jit(solution)/shard_map/ppermute | solution.py:585
  74.1 5.6 %collective-permute-start.24 = (f32[16,1024]{1,0:T(8,128)S(1)}, f32[16,1024]{1,0:T(8,128)S(1)}, u32[]{:S(2)}, u32[]{:S(2)}) collective-permute-start(f32[16,1024]{1,0:T(8,128)S(1)} %get-tuple-element.147), channel_id=1, source_target_pairs={{0,24},{8,16},{16,8},{24,0},{1,25},{9,17},{17,9},{25,1},{2,26},{10... | collective-permute-start | bytes 196616 | tf_op jit(solution)/shard_map/ppermute | solution.py:598
  75.8 3.9 %collective-permute-start.25 = (f32[16,512]{1,0:T(8,128)S(1)}, f32[16,512]{1,0:T(8,128)S(1)}, u32[]{:S(2)}, u32[]{:S(2)}) collective-permute-start(f32[16,512]{1,0:T(8,128)S(1)} %get-tuple-element.148.refs_16_), channel_id=1, source_target_pairs={{0,16},{8,24},{16,0},{24,8},{1,17},{9,25},{17,1},{25,9},{2,18},{10... | collective-permute-start | bytes 98312 | tf_op jit(solution)/shard_map/ppermute | solution.py:585
  86.0 1.2 collective-permute-start.26
  87.2 7.2 %collective-permute-start.27 = (f32[16,640]{1,0:T(8,128)S(1)}, f32[16,640]{1,0:T(8,128)S(1)}, u32[]{:S(2)}, u32[]{:S(2)}) collective-permute-start(f32[16,640]{1,0:T(8,128)S(1)} %get-tuple-element.162), channel_id=1, source_target_pairs={{0,2},{2,0},{4,6},{6,4},{1,3},{3,1},{5,7},{7,5},{8,10},{10,8},{12,... | collective-permute-start | bytes 122888 | tf_op jit(solution)/shard_map/ppermute | solution.py:585
  88.0 6.4 %collective-permute-start.28 = (f32[16,640]{1,0:T(8,128)S(1)}, f32[16,640]{1,0:T(8,128)S(1)}, u32[]{:S(2)}, u32[]{:S(2)}) collective-permute-start(f32[16,640]{1,0:T(8,128)S(1)} %get-tuple-element.163), channel_id=1, source_target_pairs={{0,6},{2,4},{4,2},{6,0},{1,7},{3,5},{5,3},{7,1},{8,14},{10,12},{12... | collective-permute-start | bytes 122888 | tf_op jit(solution)/shard_map/ppermute | solution.py:598
  89.8 4.5 %collective-permute-start.29 = (f32[16,128]{1,0:T(8,128)S(1)}, f32[16,128]{1,0:T(8,128)S(1)}, u32[]{:S(2)}, u32[]{:S(2)}) collective-permute-start(f32[16,128]{1,0:T(8,128)S(1)} %get-tuple-element.164.refs_0_), channel_id=1, source_target_pairs={{0,4},{2,6},{4,0},{6,2},{1,5},{3,7},{5,1},{7,3},{8,12},{10,14},{12... | collective-permute-start | bytes 24584 | tf_op jit(solution)/shard_map/ppermute | solution.py:585
  94.5 6.0 %collective-permute-start.30 = (f32[16,1024]{1,0:T(8,128)S(1)}, f32[16,1024]{1,0:T(8,128)S(1)}, u32[]{:S(2)}, u32[]{:S(2)}) collective-permute-start(f32[16,1024]{1,0:T(8,128)S(1)} %get-tuple-element.167), channel_id=1, source_target_pairs={{0,8},{8,0},{16,24},{24,16},{1,9},{9,1},{17,25},{25,17},{2,10},{10... | collective-permute-start | bytes 196616 | tf_op jit(solution)/shard_map/ppermute | solution.py:585
  95.0 5.5 %collective-permute-start.31 = (f32[16,1024]{1,0:T(8,128)S(1)}, f32[16,1024]{1,0:T(8,128)S(1)}, u32[]{:S(2)}, u32[]{:S(2)}) collective-permute-start(f32[16,1024]{1,0:T(8,128)S(1)} %get-tuple-element.168), channel_id=1, source_target_pairs={{0,24},{8,16},{16,8},{24,0},{1,25},{9,17},{17,9},{25,1},{2,26},{10... | collective-permute-start | bytes 196616 | tf_op jit(solution)/shard_map/ppermute | solution.py:598
  96.4 4.2 %collective-permute-start.32 = (f32[16,512]{1,0:T(8,128)S(1)}, f32[16,512]{1,0:T(8,128)S(1)}, u32[]{:S(2)}, u32[]{:S(2)}) collective-permute-start(f32[16,512]{1,0:T(8,128)S(1)} %get-tuple-element.169.refs_16_), channel_id=1, source_target_pairs={{0,16},{8,24},{16,0},{24,8},{1,17},{9,25},{17,1},{25,9},{2,18},{10... | collective-permute-start | bytes 98312 | tf_op jit(solution)/shard_map/ppermute | solution.py:585
  106.8 1.2 collective-permute-start.33
  108.0 7.0 %collective-permute-start.34 = (f32[16,640]{1,0:T(8,128)S(1)}, f32[16,640]{1,0:T(8,128)S(1)}, u32[]{:S(2)}, u32[]{:S(2)}) collective-permute-start(f32[16,640]{1,0:T(8,128)S(1)} %get-tuple-element.183), channel_id=1, source_target_pairs={{0,2},{2,0},{4,6},{6,4},{1,3},{3,1},{5,7},{7,5},{8,10},{10,8},{12,... | collective-permute-start | bytes 122888 | tf_op jit(solution)/shard_map/ppermute | solution.py:585
  109.1 5.9 %collective-permute-start.36 = (f32[16,640]{1,0:T(8,128)S(1)}, f32[16,640]{1,0:T(8,128)S(1)}, u32[]{:S(2)}, u32[]{:S(2)}) collective-permute-start(f32[16,640]{1,0:T(8,128)S(1)} %get-tuple-element.184), channel_id=1, source_target_pairs={{0,6},{2,4},{4,2},{6,0},{1,7},{3,5},{5,3},{7,1},{8,14},{10,12},{12... | collective-permute-start | bytes 122888 | tf_op jit(solution)/shard_map/ppermute | solution.py:598
  110.5 4.5 %collective-permute-start.35 = (f32[16,128]{1,0:T(8,128)S(1)}, f32[16,128]{1,0:T(8,128)S(1)}, u32[]{:S(2)}, u32[]{:S(2)}) collective-permute-start(f32[16,128]{1,0:T(8,128)S(1)} %get-tuple-element.182.refs_0_), channel_id=1, source_target_pairs={{0,4},{2,6},{4,0},{6,2},{1,5},{3,7},{5,1},{7,3},{8,12},{10,14},{12... | collective-permute-start | bytes 24584 | tf_op jit(solution)/shard_map/ppermute | solution.py:585
  115.2 7.1 %collective-permute-start.37 = (f32[16,1024]{1,0:T(8,128)S(1)}, f32[16,1024]{1,0:T(8,128)S(1)}, u32[]{:S(2)}, u32[]{:S(2)}) collective-permute-start(f32[16,1024]{1,0:T(8,128)S(1)} %get-tuple-element.187), channel_id=1, source_target_pairs={{0,8},{8,0},{16,24},{24,16},{1,9},{9,1},{17,25},{25,17},{2,10},{10... | collective-permute-start | bytes 196616 | tf_op jit(solution)/shard_map/ppermute | solution.py:585
  116.8 5.5 %collective-permute-start.38 = (f32[16,1024]{1,0:T(8,128)S(1)}, f32[16,1024]{1,0:T(8,128)S(1)}, u32[]{:S(2)}, u32[]{:S(2)}) collective-permute-start(f32[16,1024]{1,0:T(8,128)S(1)} %get-tuple-element.188), channel_id=1, source_target_pairs={{0,24},{8,16},{16,8},{24,0},{1,25},{9,17},{17,9},{25,1},{2,26},{10... | collective-permute-start | bytes 196616 | tf_op jit(solution)/shard_map/ppermute | solution.py:598
  118.4 3.9 %collective-permute-start.39 = (f32[16,512]{1,0:T(8,128)S(1)}, f32[16,512]{1,0:T(8,128)S(1)}, u32[]{:S(2)}, u32[]{:S(2)}) collective-permute-start(f32[16,512]{1,0:T(8,128)S(1)} %get-tuple-element.189.refs_6_), channel_id=1, source_target_pairs={{0,16},{8,24},{16,0},{24,8},{1,17},{9,25},{17,1},{25,9},{2,18},{10... | collective-permute-start | bytes 98312 | tf_op jit(solution)/shard_map/ppermute | solution.py:585

commit v5 on v4

--- a/solution.py
+++ b/solution.py
@@ -165,7 +165,7 @@
     return minus[d][base : base + 16, :] * inside.astype(f32)
 
 
-def begin_kernel(sizes, rhs, modes, fmap, xa, xb, ya, yb, za, zb, touched, part):
+def begin_kernel(sizes, rhs, modes, fmap, xa, xb, ya, yb, za, zb, part):
     parity, _ = position((1, 1, 1))
     levels = 2 * sizes[2]
     lanes = part.shape[1]
@@ -216,7 +216,7 @@
     out[...] = factors[0, 0, 0, 0:16, 0:LANES].astype(f32)[:8]
 
 
-def turn_kernel(factors, turned):
+def turn_kernel(factors, touched, turned):
     for s in range(factors.shape[0]):
         for i in range(factors.shape[1]):
             for j in range(factors.shape[2]):
@@ -657,12 +657,6 @@
     xa, xb, _ = exchange(xa, xb, "gx", ends=False)
     ya, yb, _ = exchange(ya, yb, "gy", ends=False)
     packs = [xa, xb, ya, yb, za, zb]
-    (turned,) = call(
-        turn_kernel,
-        [jax.ShapeDtypeStruct(factors.shape, factors.dtype)],
-        [factors],
-        cost=pl.CostEstimate(flops=0, bytes_accessed=9 << 20, transcendentals=0),
-    )
     faces = shape(2, 6, cases, dofs)
     (touched,) = call(
         touch_kernel,
@@ -670,7 +664,7 @@
         [factors],
         cost=pl.CostEstimate(flops=0, bytes_accessed=9 << 20, transcendentals=0),
     )
-    (part,) = call(functools.partial(begin_kernel, sizes), [shape(cases, lanes)], [rhs, modes, fmap, *packs, touched])
+    (part,) = call(functools.partial(begin_kernel, sizes), [shape(cases, lanes)], [rhs, modes, fmap, *packs])
     perm, back, lift, sums, start, solve, pairs = call(
         functools.partial(setup_kernel, sizes),
         [
@@ -710,7 +704,13 @@
         xa, xb, others = exchange(*(along_x or (part, part)), "gx", part)
         return [xa, xb, ya, yb, za, zb], [part, *others], also, early
 
-    _, parts, turned, _ = reduce(part, part, part, (), (), turned)
+    _, parts, touched, _ = reduce(part, part, part, (), (), touched)
+    (turned,) = call(
+        turn_kernel,
+        [jax.ShapeDtypeStruct(factors.shape, factors.dtype)],
+        [factors, touched],
+        cost=pl.CostEstimate(flops=0, bytes_accessed=9 << 20, transcendentals=0),
+    )
     wide = shape(cases, 2 * dofs)
     sends = [wide] * 4 + [shape(cases, dofs + lanes)] * 2 + [shape(cases, lanes)]
     residual, forward, image, *out = call(

time: 124 us -> 126 us (1.016)
    ppermute x12, starting transfers between devices: 17 us -> 21.6 us  [exchange(): above = lax.ppermute(second, axis, pairs)]
    ppermute x28, starting transfers between devices: 29.4 us -> 26 us  [swap(): lax.ppermute(values, axis, [(i, i ^ distance) for i in range(lax.axis_siz...]
  transfers between devices with their start and end apart: 40 -> 40, of which waited for: 15 -> 16; matrix products, arithmetic and copies ran while one was open for 0% -> 0% of each run, Pallas kernels for 11% -> 10%
where the time goes in v5:
time: 126 us
  starting transfers between devices  47.6 us (38%)
  Pallas kernels  43.1 us (34%)
  waiting for transfers between devices  27.3 us (22%)
  local copies, waits for them, and re-layouts  6.89 us (5%)
    pallas_call x25, Pallas kernels, call(): pl.pallas_call(kernel, out_shape=outs, in_specs=[specs.get(i, vmem) for i...  43.1 us
    ppermute x28, waiting for transfers between devices, swap(): lax.ppermute(values, axis, [(i, i ^ distance) for i in range(lax.axis_siz...  26.5 us
    ppermute x28, starting transfers between devices, swap(): lax.ppermute(values, axis, [(i, i ^ distance) for i in range(lax.axis_siz...  26 us
    ppermute x12, starting transfers between devices, exchange(): above = lax.ppermute(second, axis, pairs)  21.6 us
    unnamed x20, local copies, waits for them, and re-layouts  6.89 us
  transfers between devices with their start and end apart: 40, of which 16 were waited for; matrix products, arithmetic and copies ran while one was open for 0% of the time, Pallas kernels for 10%

profile of v5, /device:TPU:0, one launch (start us, length us, event | category | flops | bytes accessed | tf_op | source)
XLA Modules:
  0.0 125.7 jit_solution(12799914788373185951)
XLA Ops:
  0.6 0.9 copy-done.3
  1.5 0.9 copy-done.4
  2.4 0.7 copy-done.5
  3.1 0.7 copy-done.6
  3.8 0.9 shard_map.77
  4.8 3.0 %collective-permute-start = (f32[80,256]{1,0:T(8,128)S(1)}, f32[80,256]{1,0:T(8,128)S(1)}, u32[]{:S(2)}, u32[]{:S(2)}) collective-permute-start(f32[80,256]{1,0:T(8,128)S(1)} %get-tuple-element.105), channel_id=1, source_target_pairs={{0,8},{8,0},{16,24},{24,16},{1,9},{9,1},{17,25},{25,17},{2,10},{10... | collective-permute-start | bytes 245768 | tf_op jit(solution)/shard_map/ppermute | solution.py:585
  7.8 0.7 collective-permute-start.1
  8.4 1.6 %collective-permute-start.2 = (f32[80,256]{1,0:T(8,128)S(1)}, f32[80,256]{1,0:T(8,128)S(1)}, u32[]{:S(2)}, u32[]{:S(2)}) collective-permute-start(f32[80,256]{1,0:T(8,128)S(1)} %get-tuple-element.107), channel_id=1, source_target_pairs={{0,2},{2,0},{4,6},{6,4},{1,3},{3,1},{5,7},{7,5},{8,10},{10,8},{12,... | collective-permute-start | bytes 245768 | tf_op jit(solution)/shard_map/ppermute | solution.py:585
  10.1 0.7 collective-permute-start.3
  10.8 1.2 collective-permute-done.4.za.zb
  12.0 0.9 collective-permute-done.2.ya
  12.9 1.2 shard_map.79.refs_0_
  14.1 1.2 collective-permute-done.5.refs_1_
  15.3 3.6 %collective-permute-start.8 = (f32[16,128]{1,0:T(8,128)S(1)}, f32[16,128]{1,0:T(8,128)S(1)}, u32[]{:S(2)}, u32[]{:S(2)}) collective-permute-start(f32[16,128]{1,0:T(8,128)S(1)} %shard_map.80.refs_0_), channel_id=1, source_target_pairs={{0,6},{2,4},{4,2},{6,0},{1,7},{3,5},{5,3},{7,1},{8,14},{10,12},{12... | collective-permute-start | bytes 24584 | tf_op jit(solution)/shard_map/ppermute | solution.py:598
  18.9 2.5 %collective-permute-start.7 = (f32[16,128]{1,0:T(8,128)S(1)}, f32[16,128]{1,0:T(8,128)S(1)}, u32[]{:S(2)}, u32[]{:S(2)}) collective-permute-start(f32[16,128]{1,0:T(8,128)S(1)} %shard_map.80.refs_0_), channel_id=1, source_target_pairs={{0,4},{2,6},{4,0},{6,2},{1,5},{3,7},{5,1},{7,3},{8,12},{10,14},{12... | collective-permute-start | bytes 24584 | tf_op jit(solution)/shard_map/ppermute | solution.py:585
  21.4 0.6 collective-permute-start.6
  22.0 3.7 %copy-done = bf16[1,1,2,6,6,256,256]{6,5,4,3,2,1,0:T(8,128)(2,1)S(1)} copy-done((bf16[1,1,2,6,6,256,256]{6,5,4,3,2,1,0:T(8,128)(2,1)S(1)}, bf16[1,1,2,6,6,256,256]{6,5,4,3,2,1,0:T(8,128)(2,1)}, u32[]{:S(2)}) %copy-start) | copy-done | bytes 9437208
  25.9 1.5 %collective-permute-start.11 = (f32[16,512]{1,0:T(8,128)S(1)}, f32[16,512]{1,0:T(8,128)S(1)}, u32[]{:S(2)}, u32[]{:S(2)}) collective-permute-start(f32[16,512]{1,0:T(8,128)S(1)} %shard_map.84.refs_0_), channel_id=1, source_target_pairs={{0,24},{8,16},{16,8},{24,0},{1,25},{9,17},{17,9},{25,1},{2,26},{10... | collective-permute-start | bytes 98312 | tf_op jit(solution)/shard_map/ppermute | solution.py:598
  27.4 4.2 %collective-permute-start.10 = (f32[16,512]{1,0:T(8,128)S(1)}, f32[16,512]{1,0:T(8,128)S(1)}, u32[]{:S(2)}, u32[]{:S(2)}) collective-permute-start(f32[16,512]{1,0:T(8,128)S(1)} %shard_map.84.refs_0_), channel_id=1, source_target_pairs={{0,16},{8,24},{16,0},{24,8},{1,17},{9,25},{17,1},{25,9},{2,18},{10... | collective-permute-start | bytes 98312 | tf_op jit(solution)/shard_map/ppermute | solution.py:585
  31.6 2.0 %shard_map.78 = (bf16[6,256,256]{2,1,0:T(8,128)(2,1)S(1)}, bf16[6,256,256]{2,1,0:T(8,128)(2,1)S(1)}, bf16[12,256,256]{2,1,0:T(8,128)(2,1)S(1)}, bf16[12,256,256]...) custom-call(f32[2,3,16,256]{3,2,1,0:T(8,128)S(1)} %get-tuple-element, ...), custom_call_target="tpu_custom_call" | custom-call | bytes 9437184 | tf_op jit(solution)/shard_map/pallas_call | solution.py:627
  33.7 2.5 %shard_map.82.turned.refs_2_ = bf16[2,6,6,256,256]{4,3,2,1,0:T(8,128)(2,1)S(1)} custom-call(bf16[2,6,6,256,256]{4,3,2,1,0:T(8,128)(2,1)S(1)} %bitcast.14, f32[8,128]{1,0:T(8,128)S(1)} %shard_map.81.touched), custom_call_target="tpu_custom_call" | custom-call | bytes 9437184 | tf_op jit(solution)/shard_map/pallas_call | solution.py:627
  36.2 6.8 %shard_map.85 = (f32[2,6,16,256]{3,2,1,0:T(8,128)S(1)}, f32[2,6,16,256]{3,2,1,0:T(8,128)S(1)}, f32[2,6,16,256]{3,2,1,0:T(8,128)S(1)}, f32[16,512]{1,0:T(8,128)S(...) custom-call(s32[6,2,6]{2,1,0:T(2,128)S(1)} %bitcast.21, ...), custom_call_target="tpu_custom_call" | custom-call | tf_op jit(solution)/shard_map/pallas_call | solution.py:627
  43.1 1.2 collective-permute-done.12.refs_1_.za.zb.refs_14_.refs_15_
  44.3 1.5 %collective-permute-start.13 = (f32[16,640]{1,0:T(8,128)S(1)}, f32[16,640]{1,0:T(8,128)S(1)}, u32[]{:S(2)}, u32[]{:S(2)}) collective-permute-start(f32[16,640]{1,0:T(8,128)S(1)} %get-tuple-element.126), channel_id=1, source_target_pairs={{0,2},{2,0},{4,6},{6,4},{1,3},{3,1},{5,7},{7,5},{8,10},{10,8},{12,... | collective-permute-start | bytes 122888 | tf_op jit(solution)/shard_map/ppermute | solution.py:585
  45.8 2.9 %collective-permute-start.14 = (f32[16,640]{1,0:T(8,128)S(1)}, f32[16,640]{1,0:T(8,128)S(1)}, u32[]{:S(2)}, u32[]{:S(2)}) collective-permute-start(f32[16,640]{1,0:T(8,128)S(1)} %get-tuple-element.127), channel_id=1, source_target_pairs={{0,6},{2,4},{4,2},{6,0},{1,7},{3,5},{5,3},{7,1},{8,14},{10,12},{12... | collective-permute-start | bytes 122888 | tf_op jit(solution)/shard_map/ppermute | solution.py:598
  48.7 3.0 %shard_map.87.refs_8_ = bf16[12,256,256]{2,1,0:T(8,128)(2,1)S(1)} custom-call(s32[6,2,6]{2,1,0:T(2,128)S(1)} %bitcast.22, bf16[2,6,6,256,256]{4,3,2,1,0:T(8,128)(2,1)S(1)} %shard_map.82.turned.refs_2_, bf16[6,256,256]{2,1,0:T(8,128)(2,1)S(1)} %get-tuple-element.113.perm.refs_3_, bf16[12,32,256]{2,1,0:T(8,128)(2,1)S(1)} %get-tuple-element.123.pairs), custom_call_target="tpu_custom_call" | custom-call | bytes 9437184 | tf_op jit(solution)/shard_map/pallas_call | solution.py:627
  51.7 1.6 %collective-permute-done.15.refs_2_ = f32[16,128]{1,0:T(8,128)S(1)} collective-permute-done((f32[16,128]{1,0:T(8,128)S(1)}, f32[16,128]{1,0:T(8,128)S(1)}, u32[]{:S(2)}, u32[]{:S(2)}) %collective-permute-start.15) | collective-permute-done | bytes 8224 | tf_op jit(solution)/shard_map/ppermute | solution.py:585
  53.5 2.0 %collective-permute-start.16 = (f32[16,1024]{1,0:T(8,128)S(1)}, f32[16,1024]{1,0:T(8,128)S(1)}, u32[]{:S(2)}, u32[]{:S(2)}) collective-permute-start(f32[16,1024]{1,0:T(8,128)S(1)} %get-tuple-element.131), channel_id=1, source_target_pairs={{0,8},{8,0},{16,24},{24,16},{1,9},{9,1},{17,25},{25,17},{2,10},{10... | collective-permute-start | bytes 196616 | tf_op jit(solution)/shard_map/ppermute | solution.py:585
  55.5 0.5 collective-permute-start.17
  56.0 1.1 collective-permute-start.18
  57.1 1.9 %shard_map.88.refs_9_ = f32[2,6,16,256]{3,2,1,0:T(8,128)S(1)} custom-call(s32[6,2,6]{2,1,0:T(2,128)S(1)} %bitcast.23, bf16[2,6,6,256,256]{4,3,2,1,0:T(8,128)(2,1)S(1)} %shard_map.82.turned.refs_2_, bf16[6,256,256]{2,1,0:T(8,128)(2,1)S(1)} %get-tuple-element.113.perm.refs_3_, f32[2,6,16,256]{3,2,1,0:T(8,128)S(1)} %get-tuple-element.125.image.refs_22_, ...), custom_call_target="tpu_custom_call" | custom-call | bytes 7340032 | tf_op jit(solution)/shard_map/pallas_call | solution.py:627
  58.9 1.0 collective-permute-done.18.refs_18_
  59.9 0.8 collective-permute-done.17.refs_11_.refs_19_
  60.7 6.4 %shard_map.90 = (f32[2,6,16,256]{3,2,1,0:T(8,128)S(1)}, f32[2,6,16,256]{3,2,1,0:T(8,128)S(1)}, f32[2,6,16,256]{3,2,1,0:T(8,128)S(1)}, f32[2,6,16,256]{3,2,1,0:T(...) custom-call(s32[6,2,6]{2,1,0:T(2,128)S(1)} %bitcast.24, ...), custom_call_target="tpu_custom_call" | custom-call | tf_op jit(solution)/shard_map/pallas_call | solution.py:627
  67.1 1.2 collective-permute-done.19.refs_1_.za.zb.refs_14_.refs_15_
  68.4 2.8 %collective-permute-start.21 = (f32[16,640]{1,0:T(8,128)S(1)}, f32[16,640]{1,0:T(8,128)S(1)}, u32[]{:S(2)}, u32[]{:S(2)}) collective-permute-start(f32[16,640]{1,0:T(8,128)S(1)} %get-tuple-element.142), channel_id=1, source_target_pairs={{0,6},{2,4},{4,2},{6,0},{1,7},{3,5},{5,3},{7,1},{8,14},{10,12},{12... | collective-permute-start | bytes 122888 | tf_op jit(solution)/shard_map/ppermute | solution.py:598
  71.2 0.6 collective-permute-start.22
  71.9 3.9 %collective-permute-done.22.refs_2_ = f32[16,128]{1,0:T(8,128)S(1)} collective-permute-done((f32[16,128]{1,0:T(8,128)S(1)}, f32[16,128]{1,0:T(8,128)S(1)}, u32[]{:S(2)}, u32[]{:S(2)}) %collective-permute-start.22) | collective-permute-done | bytes 8224 | tf_op jit(solution)/shard_map/ppermute | solution.py:585
  76.0 0.5 collective-permute-start.23
  76.5 1.4 %collective-permute-start.24 = (f32[16,1024]{1,0:T(8,128)S(1)}, f32[16,1024]{1,0:T(8,128)S(1)}, u32[]{:S(2)}, u32[]{:S(2)}) collective-permute-start(f32[16,1024]{1,0:T(8,128)S(1)} %get-tuple-element.147), channel_id=1, source_target_pairs={{0,24},{8,16},{16,8},{24,0},{1,25},{9,17},{17,9},{25,1},{2,26},{10... | collective-permute-start | bytes 196616 | tf_op jit(solution)/shard_map/ppermute | solution.py:598
  77.8 1.7 %collective-permute-start.25 = (f32[16,512]{1,0:T(8,128)S(1)}, f32[16,512]{1,0:T(8,128)S(1)}, u32[]{:S(2)}, u32[]{:S(2)}) collective-permute-start(f32[16,512]{1,0:T(8,128)S(1)} %get-tuple-element.148.refs_16_), channel_id=1, source_target_pairs={{0,16},{8,24},{16,0},{24,8},{1,17},{9,25},{17,1},{25,9},{2,18},{10... | collective-permute-start | bytes 98312 | tf_op jit(solution)/shard_map/ppermute | solution.py:585
  79.5 1.9 %shard_map.92.refs_9_ = f32[2,6,16,256]{3,2,1,0:T(8,128)S(1)} custom-call(s32[6,2,6]{2,1,0:T(2,128)S(1)} %bitcast.25, bf16[2,6,6,256,256]{4,3,2,1,0:T(8,128)(2,1)S(1)} %shard_map.82.turned.refs_2_, bf16[6,256,256]{2,1,0:T(8,128)(2,1)S(1)} %get-tuple-element.113.perm.refs_3_, f32[2,6,16,256]{3,2,1,0:T(8,128)S(1)} %get-tuple-element.136.image.refs_22_, ...), custom_call_target="tpu_custom_call" | custom-call | bytes 7340032 | tf_op jit(solution)/shard_map/pallas_call | solution.py:627
  81.4 0.6 collective-permute-done.25.refs_18_
  82.0 6.2 %shard_map.94 = (f32[2,6,16,256]{3,2,1,0:T(8,128)S(1)}, f32[2,6,16,256]{3,2,1,0:T(8,128)S(1)}, f32[2,6,16,256]{3,2,1,0:T(8,128)S(1)}, f32[2,6,16,256]{3,2,1,0:T(...) custom-call(s32[6,2,6]{2,1,0:T(2,128)S(1)} %bitcast.26, ...), custom_call_target="tpu_custom_call" | custom-call | tf_op jit(solution)/shard_map/pallas_call | solution.py:627
  88.2 1.2 collective-permute-done.26.refs_1_.za.zb.refs_14_.refs_15_
  89.5 2.1 %collective-permute-start.28 = (f32[16,640]{1,0:T(8,128)S(1)}, f32[16,640]{1,0:T(8,128)S(1)}, u32[]{:S(2)}, u32[]{:S(2)}) collective-permute-start(f32[16,640]{1,0:T(8,128)S(1)} %get-tuple-element.163), channel_id=1, source_target_pairs={{0,6},{2,4},{4,2},{6,0},{1,7},{3,5},{5,3},{7,1},{8,14},{10,12},{12... | collective-permute-start | bytes 122888 | tf_op jit(solution)/shard_map/ppermute | solution.py:598
  91.6 1.4 %collective-permute-start.29 = (f32[16,128]{1,0:T(8,128)S(1)}, f32[16,128]{1,0:T(8,128)S(1)}, u32[]{:S(2)}, u32[]{:S(2)}) collective-permute-start(f32[16,128]{1,0:T(8,128)S(1)} %get-tuple-element.164.refs_0_), channel_id=1, source_target_pairs={{0,4},{2,6},{4,0},{6,2},{1,5},{3,7},{5,1},{7,3},{8,12},{10,14},{12... | collective-permute-start | bytes 24584 | tf_op jit(solution)/shard_map/ppermute | solution.py:585
  93.0 3.2 %collective-permute-done.29.refs_2_ = f32[16,128]{1,0:T(8,128)S(1)} collective-permute-done((f32[16,128]{1,0:T(8,128)S(1)}, f32[16,128]{1,0:T(8,128)S(1)}, u32[]{:S(2)}, u32[]{:S(2)}) %collective-permute-start.29) | collective-permute-done | bytes 8224 | tf_op jit(solution)/shard_map/ppermute | solution.py:585
  96.3 1.7 %collective-permute-start.30 = (f32[16,1024]{1,0:T(8,128)S(1)}, f32[16,1024]{1,0:T(8,128)S(1)}, u32[]{:S(2)}, u32[]{:S(2)}) collective-permute-start(f32[16,1024]{1,0:T(8,128)S(1)} %get-tuple-element.167), channel_id=1, source_target_pairs={{0,8},{8,0},{16,24},{24,16},{1,9},{9,1},{17,25},{25,17},{2,10},{10... | collective-permute-start | bytes 196616 | tf_op jit(solution)/shard_map/ppermute | solution.py:585
  98.0 1.6 %collective-permute-start.31 = (f32[16,1024]{1,0:T(8,128)S(1)}, f32[16,1024]{1,0:T(8,128)S(1)}, u32[]{:S(2)}, u32[]{:S(2)}) collective-permute-start(f32[16,1024]{1,0:T(8,128)S(1)} %get-tuple-element.168), channel_id=1, source_target_pairs={{0,24},{8,16},{16,8},{24,0},{1,25},{9,17},{17,9},{25,1},{2,26},{10... | collective-permute-start | bytes 196616 | tf_op jit(solution)/shard_map/ppermute | solution.py:598
  99.6 0.2 collective-permute-start.32
  99.8 1.9 %shard_map.96.refs_9_ = f32[2,6,16,256]{3,2,1,0:T(8,128)S(1)} custom-call(s32[6,2,6]{2,1,0:T(2,128)S(1)} %bitcast.27, bf16[2,6,6,256,256]{4,3,2,1,0:T(8,128)(2,1)S(1)} %shard_map.82.turned.refs_2_, bf16[6,256,256]{2,1,0:T(8,128)(2,1)S(1)} %get-tuple-element.113.perm.refs_3_, f32[2,6,16,256]{3,2,1,0:T(8,128)S(1)} %get-tuple-element.157.image.refs_22_, ...), custom_call_target="tpu_custom_call" | custom-call | bytes 7340032 | tf_op jit(solution)/shard_map/pallas_call | solution.py:627
  101.7 1.8 %collective-permute-done.32.refs_18_ = f32[16,512]{1,0:T(8,128)S(1)} collective-permute-done((f32[16,512]{1,0:T(8,128)S(1)}, f32[16,512]{1,0:T(8,128)S(1)}, u32[]{:S(2)}, u32[]{:S(2)}) %collective-permute-start.32) | collective-permute-done | bytes 32800 | tf_op jit(solution)/shard_map/ppermute | solution.py:585
  103.5 6.2 %shard_map.98 = (f32[2,6,16,256]{3,2,1,0:T(8,128)S(1)}, f32[2,6,16,256]{3,2,1,0:T(8,128)S(1)}, f32[2,6,16,256]{3,2,1,0:T(8,128)S(1)}, f32[2,6,16,256]{3,2,1,0:T(...) custom-call(s32[6,2,6]{2,1,0:T(2,128)S(1)} %bitcast.28, ...), custom_call_target="tpu_custom_call" | custom-call | tf_op jit(solution)/shard_map/pallas_call | solution.py:627
  109.8 1.2 collective-permute-done.33.refs_1_.refs_4_.refs_5_
  111.0 0.4 collective-permute-start.34
  111.4 2.5 %collective-permute-start.36 = (f32[16,640]{1,0:T(8,128)S(1)}, f32[16,640]{1,0:T(8,128)S(1)}, u32[]{:S(2)}, u32[]{:S(2)}) collective-permute-start(f32[16,640]{1,0:T(8,128)S(1)} %get-tuple-element.184), channel_id=1, source_target_pairs={{0,6},{2,4},{4,2},{6,0},{1,7},{3,5},{5,3},{7,1},{8,14},{10,12},{12... | collective-permute-start | bytes 122888 | tf_op jit(solution)/shard_map/ppermute | solution.py:598
  113.9 0.6 collective-permute-start.35
  114.5 3.9 %collective-permute-done.35.refs_2_ = f32[16,128]{1,0:T(8,128)S(1)} collective-permute-done((f32[16,128]{1,0:T(8,128)S(1)}, f32[16,128]{1,0:T(8,128)S(1)}, u32[]{:S(2)}, u32[]{:S(2)}) %collective-permute-start.35) | collective-permute-done | bytes 8224 | tf_op jit(solution)/shard_map/ppermute | solution.py:585
  118.6 0.4 collective-permute-start.37
  119.0 1.4 %collective-permute-start.38 = (f32[16,1024]{1,0:T(8,128)S(1)}, f32[16,1024]{1,0:T(8,128)S(1)}, u32[]{:S(2)}, u32[]{:S(2)}) collective-permute-start(f32[16,1024]{1,0:T(8,128)S(1)} %get-tuple-element.188), channel_id=1, source_target_pairs={{0,24},{8,16},{16,8},{24,0},{1,25},{9,17},{17,9},{25,1},{2,26},{10... | collective-permute-start | bytes 196616 | tf_op jit(solution)/shard_map/ppermute | solution.py:598
  120.4 1.8 %collective-permute-start.39 = (f32[16,512]{1,0:T(8,128)S(1)}, f32[16,512]{1,0:T(8,128)S(1)}, u32[]{:S(2)}, u32[]{:S(2)}) collective-permute-start(f32[16,512]{1,0:T(8,128)S(1)} %get-tuple-element.189.refs_6_), channel_id=1, source_target_pairs={{0,16},{8,24},{16,0},{24,8},{1,17},{9,25},{17,1},{25,9},{2,18},{10... | collective-permute-start | bytes 98312 | tf_op jit(solution)/shard_map/ppermute | solution.py:585
  122.1 2.4 %collective-permute-done.39.refs_8_ = f32[16,512]{1,0:T(8,128)S(1)} collective-permute-done((f32[16,512]{1,0:T(8,128)S(1)}, f32[16,512]{1,0:T(8,128)S(1)}, u32[]{:S(2)}, u32[]{:S(2)}) %collective-permute-start.39) | collective-permute-done | bytes 32800 | tf_op jit(solution)/shard_map/ppermute | solution.py:585
  124.5 1.2 shard_map.101
  (62 shorter events, 1.4 us)
Async XLA Ops:
  0.6 0.9 copy-start.3
  1.5 0.9 copy-start.4
  2.4 0.7 copy-start.5
  3.1 0.7 copy-start.6
  4.8 7.3 %collective-permute-start = (f32[80,256]{1,0:T(8,128)S(1)}, f32[80,256]{1,0:T(8,128)S(1)}, u32[]{:S(2)}, u32[]{:S(2)}) collective-permute-start(f32[80,256]{1,0:T(8,128)S(1)} %get-tuple-element.105), channel_id=1, source_target_pairs={{0,8},{8,0},{16,24},{24,16},{1,9},{9,1},{17,25},{25,17},{2,10},{10... | collective-permute-start | bytes 245768 | tf_op jit(solution)/shard_map/ppermute | solution.py:585
  7.8 4.3 %collective-permute-start.1 = (f32[80,256]{1,0:T(8,128)S(1)}, f32[80,256]{1,0:T(8,128)S(1)}, u32[]{:S(2)}, u32[]{:S(2)}) collective-permute-start(f32[80,256]{1,0:T(8,128)S(1)} %get-tuple-element.106), channel_id=1, source_target_pairs={{8,16},{16,8},{9,17},{17,9},{10,18},{18,10},{11,19},{19,11},{12,20... | collective-permute-start | bytes 245768 | tf_op jit(solution)/shard_map/ppermute | solution.py:598
  8.4 4.5 %collective-permute-start.2 = (f32[80,256]{1,0:T(8,128)S(1)}, f32[80,256]{1,0:T(8,128)S(1)}, u32[]{:S(2)}, u32[]{:S(2)}) collective-permute-start(f32[80,256]{1,0:T(8,128)S(1)} %get-tuple-element.107), channel_id=1, source_target_pairs={{0,2},{2,0},{4,6},{6,4},{1,3},{3,1},{5,7},{7,5},{8,10},{10,8},{12,... | collective-permute-start | bytes 245768 | tf_op jit(solution)/shard_map/ppermute | solution.py:585
  10.1 2.9 %collective-permute-start.3 = (f32[80,256]{1,0:T(8,128)S(1)}, f32[80,256]{1,0:T(8,128)S(1)}, u32[]{:S(2)}, u32[]{:S(2)}) collective-permute-start(f32[80,256]{1,0:T(8,128)S(1)} %get-tuple-element.108), channel_id=1, source_target_pairs={{2,4},{4,2},{3,5},{5,3},{10,12},{12,10},{11,13},{13,11},{18,20},{2... | collective-permute-start | bytes 245768 | tf_op jit(solution)/shard_map/ppermute | solution.py:598
  10.7 1.3 %collective-permute-start.4 = (f32[56,256]{1,0:T(8,128)S(1)}, f32[56,256]{1,0:T(8,128)S(1)}, u32[]{:S(2)}, u32[]{:S(2)}) collective-permute-start(f32[56,256]{1,0:T(8,128)S(1)} %get-tuple-element.109), channel_id=1, source_target_pairs={{0,1},{1,0},{2,3},{3,2},{4,5},{5,4},{6,7},{7,6},{8,9},{9,8},{10,11... | collective-permute-start | bytes 172040 | tf_op jit(solution)/shard_map/ppermute | solution.py:585
  14.1 1.2 collective-permute-start.5
  15.3 10.4 %collective-permute-start.8 = (f32[16,128]{1,0:T(8,128)S(1)}, f32[16,128]{1,0:T(8,128)S(1)}, u32[]{:S(2)}, u32[]{:S(2)}) collective-permute-start(f32[16,128]{1,0:T(8,128)S(1)} %shard_map.80.refs_0_), channel_id=1, source_target_pairs={{0,6},{2,4},{4,2},{6,0},{1,7},{3,5},{5,3},{7,1},{8,14},{10,12},{12... | collective-permute-start | bytes 24584 | tf_op jit(solution)/shard_map/ppermute | solution.py:598
  18.9 6.8 %collective-permute-start.7 = (f32[16,128]{1,0:T(8,128)S(1)}, f32[16,128]{1,0:T(8,128)S(1)}, u32[]{:S(2)}, u32[]{:S(2)}) collective-permute-start(f32[16,128]{1,0:T(8,128)S(1)} %shard_map.80.refs_0_), channel_id=1, source_target_pairs={{0,4},{2,6},{4,0},{6,2},{1,5},{3,7},{5,1},{7,3},{8,12},{10,14},{12... | collective-permute-start | bytes 24584 | tf_op jit(solution)/shard_map/ppermute | solution.py:585
  21.4 4.4 %collective-permute-start.6 = (f32[16,128]{1,0:T(8,128)S(1)}, f32[16,128]{1,0:T(8,128)S(1)}, u32[]{:S(2)}, u32[]{:S(2)}) collective-permute-start(f32[16,128]{1,0:T(8,128)S(1)} %shard_map.80.refs_0_), channel_id=1, source_target_pairs={{0,2},{2,0},{4,6},{6,4},{1,3},{3,1},{5,7},{7,5},{8,10},{10,8},{12,... | collective-permute-start | bytes 24584 | tf_op jit(solution)/shard_map/ppermute | solution.py:585
  22.0 3.7 %copy-start = (bf16[1,1,2,6,6,256,256]{6,5,4,3,2,1,0:T(8,128)(2,1)S(1)}, bf16[1,1,2,6,6,256,256]{6,5,4,3,2,1,0:T(8,128)(2,1)}, u32[]{:S(2)}) copy-start(bf16[1,1,2,6,6,256,256]{6,5,4,3,2,1,0:T(8,128)(2,1)} %param.7) | copy-start | bytes 28311556
  25.7 8.0 %copy-start.1 = (bf16[1,1,2,6,6,256,256]{6,5,4,3,2,1,0:T(8,128)(2,1)S(1)}, bf16[1,1,2,6,6,256,256]{6,5,4,3,2,1,0:T(8,128)(2,1)}, u32[]{:S(2)}) copy-start(bf16[1,1,2,6,6,256,256]{6,5,4,3,2,1,0:T(8,128)(2,1)} %param.7) | copy-start | bytes 28311556
  25.9 10.3 %collective-permute-start.11 = (f32[16,512]{1,0:T(8,128)S(1)}, f32[16,512]{1,0:T(8,128)S(1)}, u32[]{:S(2)}, u32[]{:S(2)}) collective-permute-start(f32[16,512]{1,0:T(8,128)S(1)} %shard_map.84.refs_0_), channel_id=1, source_target_pairs={{0,24},{8,16},{16,8},{24,0},{1,25},{9,17},{17,9},{25,1},{2,26},{10... | collective-permute-start | bytes 98312 | tf_op jit(solution)/shard_map/ppermute | solution.py:598
  27.4 8.8 %collective-permute-start.10 = (f32[16,512]{1,0:T(8,128)S(1)}, f32[16,512]{1,0:T(8,128)S(1)}, u32[]{:S(2)}, u32[]{:S(2)}) collective-permute-start(f32[16,512]{1,0:T(8,128)S(1)} %shard_map.84.refs_0_), channel_id=1, source_target_pairs={{0,16},{8,24},{16,0},{24,8},{1,17},{9,25},{17,1},{25,9},{2,18},{10... | collective-permute-start | bytes 98312 | tf_op jit(solution)/shard_map/ppermute | solution.py:585
  31.6 4.6 %collective-permute-start.9 = (f32[16,512]{1,0:T(8,128)S(1)}, f32[16,512]{1,0:T(8,128)S(1)}, u32[]{:S(2)}, u32[]{:S(2)}) collective-permute-start(f32[16,512]{1,0:T(8,128)S(1)} %shard_map.84.refs_0_), channel_id=1, source_target_pairs={{0,8},{8,0},{16,24},{24,16},{1,9},{9,1},{17,25},{25,17},{2,10},{10... | collective-permute-start | bytes 98312 | tf_op jit(solution)/shard_map/ppermute | solution.py:585
  33.7 2.5 %copy-start.2 = (s32[1,1,2,6,6]{4,2,3,1,0:T(2,128)S(1)}, s32[1,1,2,6,6]{4,2,3,1,0:T(2,128)}, u32[]{:S(2)}) copy-start(s32[1,1,2,6,6]{4,2,3,1,0:T(2,128)} %param.8) | copy-start | bytes 868
  43.1 1.2 collective-permute-start.12
  44.3 9.0 %collective-permute-start.13 = (f32[16,640]{1,0:T(8,128)S(1)}, f32[16,640]{1,0:T(8,128)S(1)}, u32[]{:S(2)}, u32[]{:S(2)}) collective-permute-start(f32[16,640]{1,0:T(8,128)S(1)} %get-tuple-element.126), channel_id=1, source_target_pairs={{0,2},{2,0},{4,6},{6,4},{1,3},{3,1},{5,7},{7,5},{8,10},{10,8},{12,... | collective-permute-start | bytes 122888 | tf_op jit(solution)/shard_map/ppermute | solution.py:585
  45.8 7.5 %collective-permute-start.14 = (f32[16,640]{1,0:T(8,128)S(1)}, f32[16,640]{1,0:T(8,128)S(1)}, u32[]{:S(2)}, u32[]{:S(2)}) collective-permute-start(f32[16,640]{1,0:T(8,128)S(1)} %get-tuple-element.127), channel_id=1, source_target_pairs={{0,6},{2,4},{4,2},{6,0},{1,7},{3,5},{5,3},{7,1},{8,14},{10,12},{12... | collective-permute-start | bytes 122888 | tf_op jit(solution)/shard_map/ppermute | solution.py:598
  48.7 4.5 %collective-permute-start.15 = (f32[16,128]{1,0:T(8,128)S(1)}, f32[16,128]{1,0:T(8,128)S(1)}, u32[]{:S(2)}, u32[]{:S(2)}) collective-permute-start(f32[16,128]{1,0:T(8,128)S(1)} %get-tuple-element.128.refs_0_), channel_id=1, source_target_pairs={{0,4},{2,6},{4,0},{6,2},{1,5},{3,7},{5,1},{7,3},{8,12},{10,14},{12... | collective-permute-start | bytes 24584 | tf_op jit(solution)/shard_map/ppermute | solution.py:585
  48.7 12.0 %slice-start = ((s8[9437184]{0:T(1024)(128)(4,1)}), s8[4194304]{0:T(1024)(128)(4,1)S(1)}, s32[]{:S(2)}) async-start(s8[9437184]{0:T(1024)(128)(4,1)} %bitcast.16), calls=%async_computation | async-start | bytes 8388608
  48.7 12.0 %slice-start.1 = ((s8[9437184]{0:T(1024)(128)(4,1)}), s8[4194304]{0:T(1024)(128)(4,1)S(1)}, s32[]{:S(2)}) async-start(s8[9437184]{0:T(1024)(128)(4,1)} %bitcast.16), calls=%async_computation.1 | async-start | bytes 8388608
  53.5 6.4 %collective-permute-start.16 = (f32[16,1024]{1,0:T(8,128)S(1)}, f32[16,1024]{1,0:T(8,128)S(1)}, u32[]{:S(2)}, u32[]{:S(2)}) collective-permute-start(f32[16,1024]{1,0:T(8,128)S(1)} %get-tuple-element.131), channel_id=1, source_target_pairs={{0,8},{8,0},{16,24},{24,16},{1,9},{9,1},{17,25},{25,17},{2,10},{10... | collective-permute-start | bytes 196616 | tf_op jit(solution)/shard_map/ppermute | solution.py:585
  55.5 5.2 %collective-permute-start.17 = (f32[16,1024]{1,0:T(8,128)S(1)}, f32[16,1024]{1,0:T(8,128)S(1)}, u32[]{:S(2)}, u32[]{:S(2)}) collective-permute-start(f32[16,1024]{1,0:T(8,128)S(1)} %get-tuple-element.132), channel_id=1, source_target_pairs={{0,24},{8,16},{16,8},{24,0},{1,25},{9,17},{17,9},{25,1},{2,26},{10... | collective-permute-start | bytes 196616 | tf_op jit(solution)/shard_map/ppermute | solution.py:598
  56.0 3.9 %collective-permute-start.18 = (f32[16,512]{1,0:T(8,128)S(1)}, f32[16,512]{1,0:T(8,128)S(1)}, u32[]{:S(2)}, u32[]{:S(2)}) collective-permute-start(f32[16,512]{1,0:T(8,128)S(1)} %get-tuple-element.133.refs_16_), channel_id=1, source_target_pairs={{0,16},{8,24},{16,0},{24,8},{1,17},{9,25},{17,1},{25,9},{2,18},{10... | collective-permute-start | bytes 98312 | tf_op jit(solution)/shard_map/ppermute | solution.py:585
  57.1 3.6 %slice-start.2 = ((s8[9437184]{0:T(1024)(128)(4,1)}), s8[1048576]{0:T(1024)(128)(4,1)S(1)}, s32[]{:S(2)}) async-start(s8[9437184]{0:T(1024)(128)(4,1)} %bitcast.16), calls=%async_computation.2 | async-start | bytes 2097152
  67.1 1.2 collective-permute-start.19
  68.3 7.5 %collective-permute-start.20 = (f32[16,640]{1,0:T(8,128)S(1)}, f32[16,640]{1,0:T(8,128)S(1)}, u32[]{:S(2)}, u32[]{:S(2)}) collective-permute-start(f32[16,640]{1,0:T(8,128)S(1)} %get-tuple-element.141), channel_id=1, source_target_pairs={{0,2},{2,0},{4,6},{6,4},{1,3},{3,1},{5,7},{7,5},{8,10},{10,8},{12,... | collective-permute-start | bytes 122888 | tf_op jit(solution)/shard_map/ppermute | solution.py:585
  68.4 7.4 %collective-permute-start.21 = (f32[16,640]{1,0:T(8,128)S(1)}, f32[16,640]{1,0:T(8,128)S(1)}, u32[]{:S(2)}, u32[]{:S(2)}) collective-permute-start(f32[16,640]{1,0:T(8,128)S(1)} %get-tuple-element.142), channel_id=1, source_target_pairs={{0,6},{2,4},{4,2},{6,0},{1,7},{3,5},{5,3},{7,1},{8,14},{10,12},{12... | collective-permute-start | bytes 122888 | tf_op jit(solution)/shard_map/ppermute | solution.py:598
  71.2 4.5 %collective-permute-start.22 = (f32[16,128]{1,0:T(8,128)S(1)}, f32[16,128]{1,0:T(8,128)S(1)}, u32[]{:S(2)}, u32[]{:S(2)}) collective-permute-start(f32[16,128]{1,0:T(8,128)S(1)} %get-tuple-element.143.refs_0_), channel_id=1, source_target_pairs={{0,4},{2,6},{4,0},{6,2},{1,5},{3,7},{5,1},{7,3},{8,12},{10,14},{12... | collective-permute-start | bytes 24584 | tf_op jit(solution)/shard_map/ppermute | solution.py:585
  76.0 6.0 %collective-permute-start.23 = (f32[16,1024]{1,0:T(8,128)S(1)}, f32[16,1024]{1,0:T(8,128)S(1)}, u32[]{:S(2)}, u32[]{:S(2)}) collective-permute-start(f32[16,1024]{1,0:T(8,128)S(1)} %get-tuple-element.146), channel_id=1, source_target_pairs={{0,8},{8,0},{16,24},{24,16},{1,9},{9,1},{17,25},{25,17},{2,10},{10... | collective-permute-start | bytes 196616 | tf_op jit(solution)/shard_map/ppermute | solution.py:585
  76.5 5.5 %collective-permute-start.24 = (f32[16,1024]{1,0:T(8,128)S(1)}, f32[16,1024]{1,0:T(8,128)S(1)}, u32[]{:S(2)}, u32[]{:S(2)}) collective-permute-start(f32[16,1024]{1,0:T(8,128)S(1)} %get-tuple-element.147), channel_id=1, source_target_pairs={{0,24},{8,16},{16,8},{24,0},{1,25},{9,17},{17,9},{25,1},{2,26},{10... | collective-permute-start | bytes 196616 | tf_op jit(solution)/shard_map/ppermute | solution.py:598
  77.8 4.1 %collective-permute-start.25 = (f32[16,512]{1,0:T(8,128)S(1)}, f32[16,512]{1,0:T(8,128)S(1)}, u32[]{:S(2)}, u32[]{:S(2)}) collective-permute-start(f32[16,512]{1,0:T(8,128)S(1)} %get-tuple-element.148.refs_16_), channel_id=1, source_target_pairs={{0,16},{8,24},{16,0},{24,8},{1,17},{9,25},{17,1},{25,9},{2,18},{10... | collective-permute-start | bytes 98312 | tf_op jit(solution)/shard_map/ppermute | solution.py:585
  88.2 1.2 collective-permute-start.26
  89.4 6.7 %collective-permute-start.27 = (f32[16,640]{1,0:T(8,128)S(1)}, f32[16,640]{1,0:T(8,128)S(1)}, u32[]{:S(2)}, u32[]{:S(2)}) collective-permute-start(f32[16,640]{1,0:T(8,128)S(1)} %get-tuple-element.162), channel_id=1, source_target_pairs={{0,2},{2,0},{4,6},{6,4},{1,3},{3,1},{5,7},{7,5},{8,10},{10,8},{12,... | collective-permute-start | bytes 122888 | tf_op jit(solution)/shard_map/ppermute | solution.py:585
  89.5 6.6 %collective-permute-start.28 = (f32[16,640]{1,0:T(8,128)S(1)}, f32[16,640]{1,0:T(8,128)S(1)}, u32[]{:S(2)}, u32[]{:S(2)}) collective-permute-start(f32[16,640]{1,0:T(8,128)S(1)} %get-tuple-element.163), channel_id=1, source_target_pairs={{0,6},{2,4},{4,2},{6,0},{1,7},{3,5},{5,3},{7,1},{8,14},{10,12},{12... | collective-permute-start | bytes 122888 | tf_op jit(solution)/shard_map/ppermute | solution.py:598
  91.6 4.5 %collective-permute-start.29 = (f32[16,128]{1,0:T(8,128)S(1)}, f32[16,128]{1,0:T(8,128)S(1)}, u32[]{:S(2)}, u32[]{:S(2)}) collective-permute-start(f32[16,128]{1,0:T(8,128)S(1)} %get-tuple-element.164.refs_0_), channel_id=1, source_target_pairs={{0,4},{2,6},{4,0},{6,2},{1,5},{3,7},{5,1},{7,3},{8,12},{10,14},{12... | collective-permute-start | bytes 24584 | tf_op jit(solution)/shard_map/ppermute | solution.py:585
  96.3 7.2 %collective-permute-start.30 = (f32[16,1024]{1,0:T(8,128)S(1)}, f32[16,1024]{1,0:T(8,128)S(1)}, u32[]{:S(2)}, u32[]{:S(2)}) collective-permute-start(f32[16,1024]{1,0:T(8,128)S(1)} %get-tuple-element.167), channel_id=1, source_target_pairs={{0,8},{8,0},{16,24},{24,16},{1,9},{9,1},{17,25},{25,17},{2,10},{10... | collective-permute-start | bytes 196616 | tf_op jit(solution)/shard_map/ppermute | solution.py:585
  98.0 5.5 %collective-permute-start.31 = (f32[16,1024]{1,0:T(8,128)S(1)}, f32[16,1024]{1,0:T(8,128)S(1)}, u32[]{:S(2)}, u32[]{:S(2)}) collective-permute-start(f32[16,1024]{1,0:T(8,128)S(1)} %get-tuple-element.168), channel_id=1, source_target_pairs={{0,24},{8,16},{16,8},{24,0},{1,25},{9,17},{17,9},{25,1},{2,26},{10... | collective-permute-start | bytes 196616 | tf_op jit(solution)/shard_map/ppermute | solution.py:598
  99.6 3.9 %collective-permute-start.32 = (f32[16,512]{1,0:T(8,128)S(1)}, f32[16,512]{1,0:T(8,128)S(1)}, u32[]{:S(2)}, u32[]{:S(2)}) collective-permute-start(f32[16,512]{1,0:T(8,128)S(1)} %get-tuple-element.169.refs_16_), channel_id=1, source_target_pairs={{0,16},{8,24},{16,0},{24,8},{1,17},{9,25},{17,1},{25,9},{2,18},{10... | collective-permute-start | bytes 98312 | tf_op jit(solution)/shard_map/ppermute | solution.py:585
  109.8 1.2 collective-permute-start.33
  111.0 7.5 %collective-permute-start.34 = (f32[16,640]{1,0:T(8,128)S(1)}, f32[16,640]{1,0:T(8,128)S(1)}, u32[]{:S(2)}, u32[]{:S(2)}) collective-permute-start(f32[16,640]{1,0:T(8,128)S(1)} %get-tuple-element.183), channel_id=1, source_target_pairs={{0,2},{2,0},{4,6},{6,4},{1,3},{3,1},{5,7},{7,5},{8,10},{10,8},{12,... | collective-permute-start | bytes 122888 | tf_op jit(solution)/shard_map/ppermute | solution.py:585
  111.4 7.0 %collective-permute-start.36 = (f32[16,640]{1,0:T(8,128)S(1)}, f32[16,640]{1,0:T(8,128)S(1)}, u32[]{:S(2)}, u32[]{:S(2)}) collective-permute-start(f32[16,640]{1,0:T(8,128)S(1)} %get-tuple-element.184), channel_id=1, source_target_pairs={{0,6},{2,4},{4,2},{6,0},{1,7},{3,5},{5,3},{7,1},{8,14},{10,12},{12... | collective-permute-start | bytes 122888 | tf_op jit(solution)/shard_map/ppermute | solution.py:598
  113.9 4.5 %collective-permute-start.35 = (f32[16,128]{1,0:T(8,128)S(1)}, f32[16,128]{1,0:T(8,128)S(1)}, u32[]{:S(2)}, u32[]{:S(2)}) collective-permute-start(f32[16,128]{1,0:T(8,128)S(1)} %get-tuple-element.182.refs_0_), channel_id=1, source_target_pairs={{0,4},{2,6},{4,0},{6,2},{1,5},{3,7},{5,1},{7,3},{8,12},{10,14},{12... | collective-permute-start | bytes 24584 | tf_op jit(solution)/shard_map/ppermute | solution.py:585
  118.6 5.9 %collective-permute-start.37 = (f32[16,1024]{1,0:T(8,128)S(1)}, f32[16,1024]{1,0:T(8,128)S(1)}, u32[]{:S(2)}, u32[]{:S(2)}) collective-permute-start(f32[16,1024]{1,0:T(8,128)S(1)} %get-tuple-element.187), channel_id=1, source_target_pairs={{0,8},{8,0},{16,24},{24,16},{1,9},{9,1},{17,25},{25,17},{2,10},{10... | collective-permute-start | bytes 196616 | tf_op jit(solution)/shard_map/ppermute | solution.py:585
  119.0 5.5 %collective-permute-start.38 = (f32[16,1024]{1,0:T(8,128)S(1)}, f32[16,1024]{1,0:T(8,128)S(1)}, u32[]{:S(2)}, u32[]{:S(2)}) collective-permute-start(f32[16,1024]{1,0:T(8,128)S(1)} %get-tuple-element.188), channel_id=1, source_target_pairs={{0,24},{8,16},{16,8},{24,0},{1,25},{9,17},{17,9},{25,1},{2,26},{10... | collective-permute-start | bytes 196616 | tf_op jit(solution)/shard_map/ppermute | solution.py:598
  120.4 4.1 %collective-permute-start.39 = (f32[16,512]{1,0:T(8,128)S(1)}, f32[16,512]{1,0:T(8,128)S(1)}, u32[]{:S(2)}, u32[]{:S(2)}) collective-permute-start(f32[16,512]{1,0:T(8,128)S(1)} %get-tuple-element.189.refs_6_), channel_id=1, source_target_pairs={{0,16},{8,24},{16,0},{24,8},{1,17},{9,25},{17,1},{25,9},{2,18},{10... | collective-permute-start | bytes 98312 | tf_op jit(solution)/shard_map/ppermute | solution.py:585
